TPU v7x, 32 devices: a whole 2x2x4 slice. The times are simulated.
32 devices in a mesh: seq: 8 (over z, x), batch: 4 (over y, core).
Axes of the slice: x: 2, y: 2, z: 4, core: 2. Of those that a mesh axis runs over, the one named last changes fastest.
Arguments:
- tokens: bfloat16 [8, 2048, 1024], P('batch', 'seq'), may hold values from -6 to 6
- cotangent: bfloat16 [8, 2048, 1024], P('batch', 'seq'), may hold values from -6 to 6
- gate_weight: bfloat16 [1024, 1536], replicated, may hold values from -0.1875 to 0.1875
- branch_weight: bfloat16 [1024, 1536], replicated, may hold values from -0.1875 to 0.1875
- out_weight: bfloat16 [1536, 1024], replicated, may hold values from -0.4375 to 0.4375
- conv_taps: float32 [4, 1536], replicated, may hold values from -3 to 3
- conv_offset: float32 [1536], replicated, may hold values from -3 to 3
- rate_weight: bfloat16 [16, 96, 96], replicated, may hold values from -0.625 to 0.625
- inlet_weight: bfloat16 [16, 96, 96], replicated, may hold values from -0.625 to 0.625
- rate_offset: float32 [1536], replicated, may hold values from -4 to 4
- inlet_offset: float32 [1536], replicated, may hold values from -4 to 4
- decay_param: float32 [1536], replicated, may hold values from -14 to -3.8, as said below
- mixer_gain: float32 [1024], replicated, may hold values from 0.5 to 1.5
- feed_gain: float32 [1024], replicated, may hold values from 0.5 to 1.5
- feed_gate: bfloat16 [1024, 3072], replicated, may hold values from -0.1875 to 0.1875
- feed_up: bfloat16 [1024, 3072], replicated, may hold values from -0.1875 to 0.1875
- feed_down: bfloat16 [3072, 1024], replicated, may hold values from -0.15625 to 0.15625
Outputs:
- block_out: bfloat16 [8, 2048, 1024], P('batch', 'seq')
- tokens_grad: float32 [8, 2048, 1024], P('batch', 'seq')
- gate_grad: float32 [1024, 1536], P('seq')
- branch_grad: float32 [1024, 1536], P('seq')
- out_grad: float32 [1536, 1024], P('seq')
- taps_grad: float32 [4, 1536], replicated
- offset_conv: float32 [1536], replicated
- rate_grad: float32 [16, 96, 96], replicated
- inlet_grad: float32 [16, 96, 96], replicated
- offset_rate: float32 [1536], replicated
- offset_inlet: float32 [1536], replicated
- decay_grad: float32 [1536], replicated
- gain_mixer: float32 [1024], replicated
- gain_feed: float32 [1024], replicated
- gate_feed: float32 [1024, 3072], P('seq')
- up_feed: float32 [1024, 3072], P('seq')
- down_feed: float32 [3072, 1024], P('seq')
Inputs may be any that keep to these rules, and one draw needn't show every extreme that they name: `decay_param`: softplus of each entry lies between 0.05 / 2048 and 0.02.
All inputs are finite; a program needn't handle non-finite values.
Results may differ from a plain program's by a relative error of at most 0.012.
Values may be sent and summed in bfloat16 or wider, within the bound.
A program may use at most 256 MiB of HBM per device.

v0:
```python
import jax
import jax.numpy as jnp
from jax import lax
from jax.sharding import PartitionSpec as P


def from_behind(value, axis, steps):
    count = lax.axis_size(axis)
    initial, last = (max(0, -steps), min(count, count - steps))
    return lax.ppermute(value, axis, [(source, source + steps) for source in range(initial, last)])


def carried_in(part, axis, combine, identity, reverse):
    count = lax.axis_size(axis)
    place = lax.axis_index(axis)
    ahead = count - 1 - place if reverse else place
    gathered = jax.tree.map(lambda a: lax.all_gather(a, axis), part)
    state = jax.tree.map(lambda a, e: jnp.zeros_like(a) + jnp.asarray(e, a.dtype), part, identity)

    def one(lap, state):
        source = count - 1 - lap if reverse else lap
        return combine(
            state, jax.tree.map(lambda a: lax.dynamic_index_in_dim(a, source, 0, False), gathered)
        )

    return lax.fori_loop(0, ahead, one, state)


def rms_norm(values, gain):
    scale = lax.rsqrt(jnp.mean(values * values, axis=-1, keepdims=True) + 1e-06)
    return values * scale * gain


def combine(earlier, later):
    return (earlier[0] * later[0], later[0] * earlier[1] + later[1])


def matmul(left, right):
    return jnp.dot(left, right, preferred_element_type=jnp.float32)


def outer_product(left, right):
    return lax.dot_general(
        left, right, (((0,), (0,)), ((), ())), preferred_element_type=jnp.float32
    )


def back_product(grads, weight):
    return lax.dot_general(
        grads, weight, (((1,), (1,)), ((), ())), preferred_element_type=jnp.float32
    )


def convolve(extended, conv_taps, conv_offset):
    local_len = extended.shape[1] - 3
    total = conv_offset + conv_taps[0] * extended[:, 3 : 3 + local_len]
    for tap_index in range(1, 4):
        total = (
            total + conv_taps[tap_index] * extended[:, 3 - tap_index : 3 - tap_index + local_len]
        )
    return total


def gate_values(rate_prod, inlet_prod, mixed_values, rate_offset, inlet_offset, decay_param):
    rate = jax.nn.sigmoid(rate_prod + rate_offset)
    inlet = jax.nn.sigmoid(inlet_prod + inlet_offset)
    log_decay = -8.0 * rate * jax.nn.softplus(decay_param)
    decay = jnp.exp(log_decay)
    drive = jnp.sqrt(-jnp.expm1(2.0 * log_decay)) * inlet * mixed_values
    return (decay, drive)


def gated_gelu(up_gate, up_value):
    return jax.nn.gelu(up_gate) * up_value


def local(
    tokens,
    cotangent,
    gate_weight,
    branch_weight,
    out_weight,
    conv_taps,
    conv_offset,
    rate_weight,
    inlet_weight,
    rate_offset,
    inlet_offset,
    decay_param,
    mixer_gain,
    feed_gain,
    feed_gate,
    feed_up,
    feed_down,
):
    seq_count, local_len, model_width = tokens.shape
    lru_width = gate_weight.shape[1]
    block_count, block_width = (rate_weight.shape[0], rate_weight.shape[1])
    row_count = seq_count * local_len
    source = tokens.reshape(row_count, model_width).astype(jnp.float32)
    normed_full, norm_pull = jax.vjp(rms_norm, source, mixer_gain)
    normed = normed_full.astype(jnp.bfloat16)
    gate_pre = matmul(normed, gate_weight)
    branch = (
        matmul(normed, branch_weight).astype(jnp.bfloat16).reshape(seq_count, local_len, lru_width)
    )
    left_edge = from_behind(branch[:, local_len - 3 :, :], "seq", 1)
    extended = jnp.concatenate([left_edge, branch], axis=1)
    convolved, conv_pull = jax.vjp(convolve, extended.astype(jnp.float32), conv_taps, conv_offset)
    mixed = convolved.astype(jnp.bfloat16)
    mixed_blocks = mixed.reshape(row_count, block_count, block_width)
    rate_prod = jnp.einsum(
        "tbi,bio->tbo", mixed_blocks, rate_weight, preferred_element_type=jnp.float32
    )
    inlet_prod = jnp.einsum(
        "tbi,bio->tbo", mixed_blocks, inlet_weight, preferred_element_type=jnp.float32
    )
    rate_prod = rate_prod.reshape(seq_count, local_len, lru_width)
    inlet_prod = inlet_prod.reshape(seq_count, local_len, lru_width)
    (decay, drive), gate_pull = jax.vjp(
        gate_values,
        rate_prod,
        inlet_prod,
        mixed.astype(jnp.float32),
        rate_offset,
        inlet_offset,
        decay_param,
    )
    cum_decay, local_states = lax.associative_scan(combine, (decay, drive), axis=1)
    unit_rows = jnp.ones((seq_count, lru_width), jnp.float32)
    empty_rows = jnp.zeros((seq_count, lru_width), jnp.float32)
    entry = carried_in(
        (cum_decay[:, -1], local_states[:, -1]), "seq", combine, (unit_rows, empty_rows), False
    )
    states = local_states + cum_decay * entry[1][:, None, :]
    state_rows = states.reshape(row_count, lru_width)
    gate_act, gelu_pull = jax.vjp(jax.nn.gelu, gate_pre)
    joined = (gate_act * state_rows).astype(jnp.bfloat16)
    resid = source + matmul(joined, out_weight)
    normed_two_full, norm_two_pull = jax.vjp(rms_norm, resid, feed_gain)
    normed_two = normed_two_full.astype(jnp.bfloat16)
    up_gate = matmul(normed_two, feed_gate)
    up_value = matmul(normed_two, feed_up)
    hidden_full, glu_pull = jax.vjp(gated_gelu, up_gate, up_value)
    hidden = hidden_full.astype(jnp.bfloat16)
    block_out = (
        (resid + matmul(hidden, feed_down))
        .astype(jnp.bfloat16)
        .reshape(seq_count, local_len, model_width)
    )
    grad_rows = cotangent.reshape(row_count, model_width)
    down_sum = outer_product(hidden, grad_rows)
    grad_hidden = back_product(grad_rows, feed_down)
    grad_upgate, grad_upvalue = glu_pull(grad_hidden)
    upgate_low = grad_upgate.astype(jnp.bfloat16)
    upvalue_low = grad_upvalue.astype(jnp.bfloat16)
    gatefeed_sum = outer_product(normed_two, upgate_low)
    upfeed_sum = outer_product(normed_two, upvalue_low)
    grad_normed_two = back_product(upgate_low, feed_gate) + back_product(upvalue_low, feed_up)
    resid_part, feed_gain_sum = norm_two_pull(grad_normed_two)
    grad_resid = grad_rows.astype(jnp.float32) + resid_part
    resid_low = grad_resid.astype(jnp.bfloat16)
    out_sum = outer_product(joined, resid_low)
    grad_joined = back_product(resid_low, out_weight)
    again = carried_in(
        (cum_decay[:, -1], local_states[:, -1]), "seq", combine, (unit_rows, empty_rows), False
    )
    entry_back = again[1]
    states_back = local_states + cum_decay * entry_back[:, None, :]
    grad_gate_pre = gelu_pull(grad_joined * states_back.reshape(row_count, lru_width))[0].astype(
        jnp.bfloat16
    )
    grad_states = (grad_joined * gate_act).reshape(seq_count, local_len, lru_width)
    shifted = jnp.concatenate(
        [decay[:, 1:], jnp.ones((seq_count, 1, lru_width), jnp.float32)], axis=1
    )
    back_cum, local_grads = lax.associative_scan(
        combine, (shifted, grad_states), reverse=True, axis=1
    )
    first_decay = decay[:, 0]
    carried = carried_in(
        (first_decay * back_cum[:, 0], first_decay * local_grads[:, 0]),
        "seq",
        combine,
        (unit_rows, empty_rows),
        True,
    )
    state_grads = local_grads + back_cum * carried[1][:, None, :]
    previous = jnp.concatenate([entry_back[:, None, :], states_back[:, :-1]], axis=1)
    (
        grad_rate_prod,
        grad_inlet_prod,
        grad_mixed_direct,
        rate_offset_sum,
        inlet_offset_sum,
        decay_sum,
    ) = gate_pull((state_grads * previous, state_grads))
    rate_low = grad_rate_prod.astype(jnp.bfloat16).reshape(row_count, block_count, block_width)
    inlet_low = grad_inlet_prod.astype(jnp.bfloat16).reshape(row_count, block_count, block_width)
    rate_sum = jnp.einsum(
        "tbi,tbo->bio", mixed_blocks, rate_low, preferred_element_type=jnp.float32
    )
    inlet_sum = jnp.einsum(
        "tbi,tbo->bio", mixed_blocks, inlet_low, preferred_element_type=jnp.float32
    )
    mixed_back = jnp.einsum(
        "tbo,bio->tbi", rate_low, rate_weight, preferred_element_type=jnp.float32
    )
    mixed_back = mixed_back + jnp.einsum(
        "tbo,bio->tbi", inlet_low, inlet_weight, preferred_element_type=jnp.float32
    )
    grad_mixed = grad_mixed_direct + mixed_back.reshape(seq_count, local_len, lru_width)
    grad_extended, taps_sum, conv_offset_sum = conv_pull(grad_mixed)
    back_edge = from_behind(grad_extended[:, :3], "seq", -1)
    grad_branch = grad_extended[:, 3:].at[:, local_len - 3 :].add(back_edge)
    branch_low = grad_branch.reshape(row_count, lru_width).astype(jnp.bfloat16)
    branch_sum = outer_product(normed, branch_low)
    gate_sum = outer_product(normed, grad_gate_pre)
    grad_normed = back_product(grad_gate_pre, gate_weight) + back_product(branch_low, branch_weight)
    source_part, mixer_gain_sum = norm_pull(grad_normed)
    tokens_grad = (grad_resid + source_part).reshape(seq_count, local_len, model_width)
    small_sums = lax.psum(
        (
            taps_sum,
            conv_offset_sum,
            rate_sum,
            inlet_sum,
            rate_offset_sum,
            inlet_offset_sum,
            decay_sum,
            mixer_gain_sum,
            feed_gain_sum,
        ),
        ("seq", "batch"),
    )
    row_parts = (
        lax.psum_scatter(gate_sum, "seq", scatter_dimension=0, tiled=True),
        lax.psum_scatter(branch_sum, "seq", scatter_dimension=0, tiled=True),
        lax.psum_scatter(out_sum, "seq", scatter_dimension=0, tiled=True),
        lax.psum_scatter(gatefeed_sum, "seq", scatter_dimension=0, tiled=True),
        lax.psum_scatter(upfeed_sum, "seq", scatter_dimension=0, tiled=True),
        lax.psum_scatter(down_sum, "seq", scatter_dimension=0, tiled=True),
    )
    summed = lax.psum(
        (row_parts[0], row_parts[1], row_parts[2], row_parts[3], row_parts[4], row_parts[5]),
        "batch",
    )
    return (
        block_out,
        tokens_grad,
        summed[0],
        summed[1],
        summed[2],
        small_sums[0],
        small_sums[1],
        small_sums[2],
        small_sums[3],
        small_sums[4],
        small_sums[5],
        small_sums[6],
        small_sums[7],
        small_sums[8],
        summed[3],
        summed[4],
        summed[5],
    )


def solution(mesh):
    in_specs = (
        P("batch", "seq", None),
        P("batch", "seq", None),
        P(),
        P(),
        P(),
        P(),
        P(),
        P(),
        P(),
        P(),
        P(),
        P(),
        P(),
        P(),
        P(),
        P(),
        P(),
    )
    out_specs = (
        P("batch", "seq", None),
        P("batch", "seq", None),
        P("seq", None),
        P("seq", None),
        P("seq", None),
        P(),
        P(),
        P(),
        P(),
        P(),
        P(),
        P(),
        P(),
        P(),
        P("seq", None),
        P("seq", None),
        P("seq", None),
    )
    return jax.shard_map(local, mesh=mesh, in_specs=in_specs, out_specs=out_specs, check_vma=False)
```

profile of v0, /device:TPU:13, one launch (start us, length us, event | category | flops | bytes accessed | tf_op | source)
XLA Modules:
  0.0 1755.8 jit_solution(3595095496055897608)
XLA Ops:
  66.0 10.9 convert_multiply_fusion.1
  289.8 21.7 %all-gather = f32[16,1,1536]{2,1,0:T(1,128)S(1)} all-gather(f32[2,1,1536]{2,1,0:T(1,128)S(1)} %slice_add_fusion.3), channel_id=2, replica_groups=mesh['seq'=8,'batch'=4] {'seq'}, dimensions={0}, use_global_device_ids=true | all-gather | bytes 110592 | tf_op jit(solution)/shard_map/all_gather | solution.py:17
  328.1 24.5 %all-gather.1 = f32[16,1,1536]{2,1,0:T(1,128)S(1)} all-gather(f32[2,1,1536]{2,1,0:T(1,128)S(1)} %slice_add_fusion.2), channel_id=3, replica_groups=mesh['seq'=8,'batch'=4] {'seq'}, dimensions={0}, use_global_device_ids=true | all-gather | bytes 110592 | tf_op jit(solution)/shard_map/all_gather | solution.py:17
  378.6 15.0 multiply_convert_fusion
  451.5 12.9 slice.656
  464.4 8.0 slice.649
  472.4 12.8 slice.651
  561.2 8.1 slice.709
  621.7 24.8 %rev.8 = f32[2,256,1536]{2,1,0:T(8,128)} reverse(f32[2,256,1536]{2,1,0:T(8,128)} %add.616), dimensions={1} | reverse | bytes 6291456 | tf_op jit(solution)/shard_map/rev | solution.py:177
  660.2 24.9 %rev.9 = f32[2,256,1536]{2,1,0:T(8,128)} reverse(f32[2,256,1536]{2,1,0:T(8,128)} %add.624), dimensions={1} | reverse | bytes 6291456 | tf_op jit(solution)/shard_map/rev | solution.py:177
  686.2 24.6 %all-gather.3 = f32[16,1,1536]{2,1,0:T(1,128)S(1)} all-gather(f32[2,1,1536]{2,1,0:T(1,128)S(1)} %get-tuple-element.237), channel_id=5, replica_groups=mesh['seq'=8,'batch'=4] {'seq'}, dimensions={0}, use_global_device_ids=true | all-gather | bytes 110592 | tf_op jit(solution)/shard_map/all_gather | solution.py:17
  711.1 25.3 %all-gather.2 = f32[16,1,1536]{2,1,0:T(1,128)S(1)} all-gather(f32[2,1,1536]{2,1,0:T(1,128)S(1)} %get-tuple-element.238), channel_id=4, replica_groups=mesh['seq'=8,'batch'=4] {'seq'}, dimensions={0}, use_global_device_ids=true | all-gather | bytes 110592 | tf_op jit(solution)/shard_map/all_gather | solution.py:17
  741.2 12.2 fusion.66
  796.1 10.9 multiply_reduce_fusion.4
  827.7 8.3 fusion.88
  836.0 8.3 fusion.87
  845.6 8.3 fusion.89
  859.1 110.9 %reduce-scatter.9.cloned.1.call-done = f32[128,1536]{1,0:T(8,128)} async-done(((f32[1024,1536]{1,0:T(8,128)}), f32[128,1536]{1,0:T(8,128)}) %reduce-scatter.9.cloned.1.call-update) | async-done | bytes 786448 | tf_op jit(solution)/shard_map/reduce_scatter | solution.py:238
  970.0 212.1 %reduce-scatter.15.cloned.1.call-done = f32[128,3072]{1,0:T(8,128)} async-done(((f32[1024,3072]{1,0:T(8,128)}), f32[128,3072]{1,0:T(8,128)}) %reduce-scatter.15.cloned.1.call-update) | async-done | bytes 1572880 | tf_op jit(solution)/shard_map/reduce_scatter | solution.py:241
  1182.2 209.9 %reduce-scatter.13.cloned.1.call-done = f32[128,3072]{1,0:T(8,128)} async-done(((f32[1024,3072]{1,0:T(8,128)}), f32[128,3072]{1,0:T(8,128)}) %reduce-scatter.13.cloned.1.call-update) | async-done | bytes 1572880 | tf_op jit(solution)/shard_map/reduce_scatter | solution.py:240
  1392.1 209.9 %reduce-scatter.17.cloned.1.call-done = f32[384,1024]{1,0:T(8,128)} async-done(((f32[3072,1024]{1,0:T(8,128)}), f32[384,1024]{1,0:T(8,128)}) %reduce-scatter.17.cloned.1.call-update) | async-done | bytes 1572880 | tf_op jit(solution)/shard_map/reduce_scatter | solution.py:242
  1607.1 8.3 add_convert_fusion.1
  1618.9 42.1 %all-reduce.74 = (f32[4,1536]{1,0:T(4,128)}, f32[1536]{0:T(1024)}, f32[1536]{0:T(1024)}, f32[1536]{0:T(1024)}, f32[1536]{0:T(1024)}, /*index=5*/f32[1024]{0:T(1024)}, f32[1024]{0:T(1024)}) all-reduce(f32[4,1536]{1,0:T(4,128)S(1)} %pad_add_fusion.6, ...), channel_id=1, replica_groups=mesh['seq'=8,'batch'=4] {'seq','batch'}, use_global_device_ids=true, to_apply=%region_18.19 | all-reduce | flops 14336 | bytes 114688 | tf_op jit(solution)/shard_map/psum | solution.py:222
  1664.5 72.4 %all-reduce.82.cloned.1.call-done = (f32[128,1536]{1,0:T(8,128)}, f32[128,1536]{1,0:T(8,128)}, f32[192,1024]{1,0:T(8,128)}, f32[128,3072]{1,0:T(8,128)}, f32[128,3072]{1,0:T(8,128)}, /*index=5*/f32[384,1024]{1,0:T(8,128)}) async-done(((f32[128,1536]{1,0:T(8,128)}, f32[128,1536]{1,0:T(8,128)}, f32[192,1024]{1,0:T(8,128)}, f32[128,3072]{1,0:T(8,128)}, f32[128,3072]{1,0:T(8,128)}, ...) | async-done | bytes 7077904 | tf_op jit(solution)/shard_map/psum | solution.py:244
  (673 shorter events, 614.0 us)
Async XLA Ops:
  8.0 355.4 %copy-start = (bf16[1536,1024]{1,0:T(8,128)(2,1)S(1)}, bf16[1536,1024]{1,0:T(8,128)(2,1)}, u32[]{:S(2)}) copy-start(bf16[1536,1024]{1,0:T(8,128)(2,1)} %param.27) | copy-start | bytes 9437188
  8.0 851.1 %reduce-scatter.7.cloned.1.call-start = ((), (), s32[]{:S(2)}) async-start(), calls=%async_computation.6 | async-start | bytes 7077888 | tf_op jit(solution)/shard_map/reduce_scatter | solution.py:237
  16.1 5.5 collective-permute-start
  19.9 46.0 %copy-start.80 = (f32[1536]{0:T(1024)}, f32[1536]{0:T(1024)S(1)}, u32[]{:S(2)}) copy-start(f32[1536]{0:T(1024)S(1)} %get-tuple-element.182) | copy-start | bytes 18436
  19.9 46.0 %copy-start.82 = (f32[1536]{0:T(1024)}, f32[1536]{0:T(1024)S(1)}, u32[]{:S(2)}) copy-start(f32[1536]{0:T(1024)S(1)} %get-tuple-element.183) | copy-start | bytes 18436
  359.3 47.0 %copy-start.25 = (f32[2,256,1536]{2,1,0:T(8,128)}, f32[2,256,1536]{2,1,0:T(8,128)S(1)}, u32[]{:S(2)}) copy-start(f32[2,256,1536]{2,1,0:T(8,128)S(1)} %multiply_add_fusion.2) | copy-start | bytes 9437188
  419.4 439.8 %reduce-scatter.11.cloned.1.call-start = ((), (), s32[]{:S(2)}) async-start(), calls=%async_computation.8 | async-start | bytes 7077888 | tf_op jit(solution)/shard_map/reduce_scatter | solution.py:239
  595.8 374.2 %reduce-scatter.9.cloned.1.call-start = ((), (), s32[]{:S(2)}) async-start(), calls=%async_computation.7 | async-start | bytes 7077888 | tf_op jit(solution)/shard_map/reduce_scatter | solution.py:238
  660.1 81.0 %copy-start.4 = (f32[2,256,1536]{2,1,0:T(8,128)S(1)}, f32[2,256,1536]{2,1,0:T(8,128)}, u32[]{:S(2)}) copy-start(f32[2,256,1536]{2,1,0:T(8,128)} %copy.60) | copy-start | bytes 9437188
  660.1 81.0 %copy-start.81 = (f32[1536]{0:T(1024)S(1)}, f32[1536]{0:T(1024)}, u32[]{:S(2)}) copy-start(f32[1536]{0:T(1024)} %copy-done.80) | copy-start | bytes 18436
  660.1 81.0 %copy-start.83 = (f32[1536]{0:T(1024)S(1)}, f32[1536]{0:T(1024)}, u32[]{:S(2)}) copy-start(f32[1536]{0:T(1024)} %copy-done.82) | copy-start | bytes 18436
  660.1 81.0 %copy-start.86 = (f32[1536]{0:T(1024)S(1)}, f32[1536]{0:T(1024)}, u32[]{:S(2)}) copy-start(f32[1536]{0:T(1024)} %copy-done.84) | copy-start | bytes 18436
  660.1 81.0 %copy-start.90 = (f32[1536]{0:T(1024)S(1)}, f32[1536]{0:T(1024)}, u32[]{:S(2)}) copy-start(f32[1536]{0:T(1024)} %copy-done.88) | copy-start | bytes 18436
  660.1 81.0 %copy-start.93 = (f32[1536]{0:T(1024)S(1)}, f32[1536]{0:T(1024)}, u32[]{:S(2)}) copy-start(f32[1536]{0:T(1024)} %get-tuple-element.308) | copy-start | bytes 18436
  660.1 81.0 %copy-start.96 = (f32[1536]{0:T(1024)S(1)}, f32[1536]{0:T(1024)}, u32[]{:S(2)}) copy-start(f32[1536]{0:T(1024)} %param.32) | copy-start | bytes 18436
  660.1 81.0 %copy-start.102 = (f32[1536]{0:T(1024)S(1)}, f32[1536]{0:T(1024)}, u32[]{:S(2)}) copy-start(f32[1536]{0:T(1024)} %param.29) | copy-start | bytes 18436
  660.1 81.0 %copy-start.104 = (f32[1536]{0:T(1024)S(1)}, f32[1536]{0:T(1024)}, u32[]{:S(2)}) copy-start(f32[1536]{0:T(1024)} %param.33) | copy-start | bytes 18436
  808.4 10.3 collective-permute-start.1
  826.5 355.7 %reduce-scatter.15.cloned.1.call-start = ((), (), s32[]{:S(2)}) async-start(), calls=%async_computation.10 | async-start | bytes 14155776 | tf_op jit(solution)/shard_map/reduce_scatter | solution.py:241
  836.0 556.1 %reduce-scatter.13.cloned.1.call-start = ((), (), s32[]{:S(2)}) async-start(), calls=%async_computation.9 | async-start | bytes 14155776 | tf_op jit(solution)/shard_map/reduce_scatter | solution.py:240
  844.4 757.5 %reduce-scatter.17.cloned.1.call-start = ((), (), s32[]{:S(2)}) async-start(), calls=%async_computation.11 | async-start | bytes 14155776 | tf_op jit(solution)/shard_map/reduce_scatter | solution.py:242
  854.0 810.5 %all-reduce.80.cloned.1.call-start = ((), (), s32[]{:S(2)}) async-start(), calls=%async_computation.12 | async-start | bytes 3145728 | tf_op jit(solution)/shard_map/psum | solution.py:222
  858.8 878.1 %all-reduce.82.cloned.1.call-start = ((), (), s32[]{:S(2)}) async-start(), calls=%async_computation.13 | async-start | bytes 14155776 | tf_op jit(solution)/shard_map/psum | solution.py:244
  1664.5 77.7 %copy-start.73 = (f32[16,96,96]{2,1,0:T(8,128)S(1)}, f32[16,96,96]{2,1,0:T(8,128)}, u32[]{:S(2)}) copy-start(f32[16,96,96]{2,1,0:T(8,128)} %get-tuple-element.450) | copy-start | bytes 1769476
  (139 other events, 891.0 us)
Sparse Core Ops, SparseCore 0:
  419.5 133.4 reduce-scatter.6
  595.9 134.2 reduce-scatter.10
  826.6 143.4 reduce-scatter.8
  973.5 208.6 reduce-scatter.14
  1185.6 206.4 reduce-scatter.12
  1395.5 206.3 reduce-scatter.16
Sparse Core Ops, SparseCore 1:
  861.1 267.8 all-reduce.79
  1602.1 134.7 all-reduce.81
where the time goes:
time: 1770 us; the launch traced here: 1760 us
  waiting for transfers between devices  817 us (46%)
  local copies, waits for them, and re-layouts  489 us (28%)
  other arithmetic  159 us (9%)
  blocking collectives  138 us (8%)
  matrix products  123 us (7%)
  between operations  18.3 us (1%)
    reduce_scatter x1, waiting for transfers between devices, local(): lax.psum_scatter(upfeed_sum, 'seq', scatter_dimension=0, tiled=True)  212 us
    reduce_scatter x1, waiting for transfers between devices, local(): lax.psum_scatter(gatefeed_sum, 'seq', scatter_dimension=0, tiled=True)  210 us
    reduce_scatter x1, waiting for transfers between devices, local(): lax.psum_scatter(down_sum, 'seq', scatter_dimension=0, tiled=True)  210 us
    slice x57, local copies, waits for them, and re-layouts, local(): lax.associative_scan(combine, (shifted, grad_states), reverse=True, axis=1)  138 us
    reduce_scatter x1, waiting for transfers between devices, local(): lax.psum_scatter(branch_sum, 'seq', scatter_dimension=0, tiled=True)  111 us
    slice x52, local copies, waits for them, and re-layouts, local(): lax.associative_scan(combine, (decay, drive), axis=1)  105 us
    all_gather x4, blocking collectives, carried_in(): gathered = jax.tree.map(lambda a: lax.all_gather(a, axis), part)  96.1 us
    psum x1, waiting for transfers between devices, local(): lax.psum((row_parts[0], row_parts[1], row_parts[2], row_parts[3], row_par...  72.4 us
  transfers between devices with their start and end apart: 10, of which 6 were waited for; matrix products, arithmetic and copies ran while one was open for 22% of the time, Pallas kernels for 0%

commit v1 on v0

v1 whole, which is shorter than its diff:
```python
import functools
import jax
import jax.numpy as jnp
from jax import lax
from jax.experimental import pallas as pl
from jax.experimental.pallas import tpu as pltpu
from jax.sharding import PartitionSpec as P

F32, BF16 = jnp.float32, jnp.bfloat16
VLIM = 56 * 2**20
GELU_A, GELU_B = 0.7978845608028654, 0.044715


def nn(a, b):
    return lax.dot_general(a, b, (((1,), (0,)), ((), ())), preferred_element_type=F32)


def nt(a, b):
    return lax.dot_general(a, b, (((1,), (1,)), ((), ())), preferred_element_type=F32)


def tn(a, b):
    return lax.dot_general(a, b, (((0,), (0,)), ((), ())), preferred_element_type=F32)


def sigmoid(v):
    return 1.0 / (1.0 + jnp.exp(-v))


def drop(u, decay):
    v = 2.0 * u
    series = 1.0 + v * (1.0 / 7.0)
    for k in (6.0, 5.0, 4.0, 3.0, 2.0):
        series = 1.0 + (v * (1.0 / k)) * series
    return jnp.where(v > -0.35, -v * series, 1.0 - decay * decay)


def gelu_parts(v):
    square = v * v
    inner = jnp.tanh(GELU_A * v * (1.0 + GELU_B * square))
    half = 0.5 + 0.5 * inner
    act = v * half
    slope = half + 0.5 * v * (1.0 - inner * inner) * (GELU_A + 3.0 * GELU_A * GELU_B * square)
    return act, slope


def gelu(v):
    inner = jnp.tanh(GELU_A * v * (1.0 + GELU_B * (v * v)))
    return v * (0.5 + 0.5 * inner)


def spread(dense, blocks, count, width):
    for a in range(count):
        parts = []
        if a > 0:
            parts.append(jnp.zeros((width, a * width), dense.dtype))
        parts.append(blocks[a])
        if a < count - 1:
            parts.append(jnp.zeros((width, (count - 1 - a) * width), dense.dtype))
        dense[a * width : (a + 1) * width, :] = jnp.concatenate(parts, axis=1)


def params(sem=("arbitrary",), **kw):
    return pltpu.CompilerParams(dimension_semantics=sem, vmem_limit_bytes=VLIM, **kw)


def whole(shape):
    return pl.BlockSpec(shape, lambda *_: (0,) * len(shape))


def front_kernel(
    seqs, length, tok, halo, gain, gw, bw, taps, coff, wr, wi, roff, ioff, sp,
    normed, gate, branch, edge, mixed, rate, inlet, h, p, carry,
    hn, ext, dr, di, rp, ip,
):
    rows, width = seqs * length, gw.shape[1]
    sub = dr.shape[-1]

    @pl.when(pl.program_id(0) == 0)
    def _():
        def norm(i, _):
            x = tok[pl.ds(i * 32, 32), :].astype(F32)
            r = lax.rsqrt(jnp.mean(x * x, axis=-1, keepdims=True) + 1e-06)
            normed[pl.ds(i * 32, 32), :] = (x * r * gain[...]).astype(BF16)
            return 0

        lax.fori_loop(0, rows // 32, norm, 0)
        x = halo[...].astype(F32)
        r = lax.rsqrt(jnp.mean(x * x, axis=-1, keepdims=True) + 1e-06)
        hn[...] = (x * r * gain[...]).astype(BF16)

    gate[...] = nn(normed[...], gw[...])
    b16 = nn(normed[...], bw[...]).astype(BF16)
    e16 = nn(hn[...], bw[...]).astype(BF16)
    branch[...] = b16
    edge[...] = e16
    for s in range(seqs):
        ext[s, 0:8, :] = e16[8 * s : 8 * s + 8].astype(F32)
        ext[s, 8 : 8 + length, :] = b16[length * s : length * (s + 1)].astype(F32)

    tap = [taps[k : k + 1, :] for k in range(4)]
    off = coff[...]
    for s in range(seqs):

        def conv(i, _):
            x = ext[s, pl.ds(pl.multiple_of(i * 16, 16), 24), :]
            total = off + tap[0] * x[8:24]
            for k in range(1, 4):
                total = total + tap[k] * x[8 - k : 24 - k]
            mixed[pl.ds(pl.multiple_of(s * length + i * 16, 16), 16), :] = total.astype(BF16)
            return 0

        lax.fori_loop(0, length // 16, conv, 0)

    for g in range(width // sub):
        cols = slice(g * sub, (g + 1) * sub)
        spread(dr.at[g], [wr[g * 4 + a] for a in range(4)], 4, wr.shape[-1])
        spread(di.at[g], [wi[g * 4 + a] for a in range(4)], 4, wi.shape[-1])
        rp[:, cols] = nn(mixed[:, cols], dr[g])
        ip[:, cols] = nn(mixed[:, cols], di[g])

    ro, io, slope = roff[...], ioff[...], -8.0 * sp[...]

    def gates(i, _):
        at = pl.ds(pl.multiple_of(i * 16, 16), 16)
        rt = sigmoid(rp[at, :] + ro)
        it = sigmoid(ip[at, :] + io)
        log_decay = rt * slope
        decay = jnp.exp(log_decay)
        rate[at, :] = rt
        inlet[at, :] = it
        p[at, :] = decay
        h[at, :] = jnp.sqrt(drop(log_decay, decay)) * it * mixed[at, :].astype(F32)
        return 0

    lax.fori_loop(0, rows // 16, gates, 0)

    row = lax.broadcasted_iota(jnp.int32, (8, width), 0)

    def scan(i, last):
        out = []
        for s in range(seqs):
            at = pl.ds(pl.multiple_of(s * length + i * 8, 8), 8)
            a, b = p[at, :], h[at, :]
            for d in (1, 2, 4):
                keep = row >= d
                b = b + a * jnp.where(keep, pltpu.roll(b, d, 0), 0.0)
                a = a * jnp.where(keep, pltpu.roll(a, d, 0), 1.0)
            ap, bp = last[s]
            b = b + a * bp
            a = a * ap
            p[at, :] = a
            h[at, :] = b
            out.append((a[7:8], b[7:8]))
        return tuple(out)

    init = tuple((jnp.ones((1, width), F32), jnp.zeros((1, width), F32)) for _ in range(seqs))
    last = lax.fori_loop(0, length // 8, scan, init)
    for s in range(seqs):
        carry[0, s : s + 1, :] = last[s][0]
        carry[1, s : s + 1, :] = last[s][1]


def front(tok, halo, gain, gw, bw, taps, coff, wr, wi, roff, ioff, sp, seqs, length):
    rows, model = tok.shape
    lru = gw.shape[1]
    bw_, per = wr.shape[-1], 8
    width = per * bw_
    sub = 4 * bw_
    n = lru // width
    col = lambda r: pl.BlockSpec((r, width), lambda j: (0, j))
    blk = pl.BlockSpec((per, bw_, bw_), lambda j: (j, 0, 0))
    f = lambda dt: jax.ShapeDtypeStruct((rows, lru), dt)
    return pl.pallas_call(
        functools.partial(front_kernel, seqs, length),
        grid=(n,),
        in_specs=[
            whole((rows, model)), whole(halo.shape), whole((1, model)),
            pl.BlockSpec((model, width), lambda j: (0, j)), pl.BlockSpec((model, width), lambda j: (0, j)),
            col(4), col(1), blk, blk, col(1), col(1), col(1),
        ],
        out_specs=[
            whole((rows, model)), col(rows), col(rows), col(halo.shape[0]), col(rows), col(rows), col(rows), col(rows), col(rows),
            pl.BlockSpec((2, seqs, width), lambda j: (0, 0, j)),
        ],
        out_shape=[
            jax.ShapeDtypeStruct((rows, model), BF16), f(F32), f(BF16),
            jax.ShapeDtypeStruct((halo.shape[0], lru), BF16), f(BF16), f(F32), f(F32), f(F32), f(F32),
            jax.ShapeDtypeStruct((2, seqs, lru), F32),
        ],
        scratch_shapes=[
            pltpu.VMEM(halo.shape, BF16), pltpu.VMEM((seqs, 8 + length, width), F32),
            pltpu.VMEM((2, sub, sub), BF16), pltpu.VMEM((2, sub, sub), BF16),
            pltpu.VMEM((rows, width), F32), pltpu.VMEM((rows, width), F32),
        ],
        compiler_params=params(),
        name="front",
    )(tok, halo, gain, gw, bw, taps, coff, wr, wi, roff, ioff, sp)


def join_kernel(tok, gate, h, p, entry, ow, gain, joined, resid, normed):
    rows = tok.shape[0]
    ent = entry[0]

    def join(i, _):
        at = pl.ds(pl.multiple_of(i * 16, 16), 16)
        state = h[at, :] + p[at, :] * ent
        joined[at, :] = (gelu(gate[at, :]) * state).astype(BF16)
        return 0

    lax.fori_loop(0, rows // 16, join, 0)
    resid[...] = nn(joined[...], ow[...])

    def norm(i, _):
        at = pl.ds(pl.multiple_of(i * 32, 32), 32)
        y = tok[at, :].astype(F32) + resid[at, :]
        resid[at, :] = y
        r = lax.rsqrt(jnp.mean(y * y, axis=-1, keepdims=True) + 1e-06)
        normed[at, :] = (y * r * gain[...]).astype(BF16)
        return 0

    lax.fori_loop(0, rows // 32, norm, 0)


def join(tok, gate, h, p, entry, ow, gain, seqs, length):
    rows, model = tok.shape
    lru = gate.shape[1]
    tile = 128
    per = length // tile
    row = lambda w: pl.BlockSpec((tile, w), lambda i: (i, 0))
    return pl.pallas_call(
        join_kernel,
        grid=(rows // tile,),
        in_specs=[row(model), row(lru), row(lru), row(lru), pl.BlockSpec((1, 1, lru), lambda i: (i // per, 0, 0)), whole((lru, model)), whole((1, model))],
        out_specs=[row(lru), row(model), row(model)],
        out_shape=[jax.ShapeDtypeStruct((rows, lru), BF16), jax.ShapeDtypeStruct((rows, model), F32), jax.ShapeDtypeStruct((rows, model), BF16)],
        compiler_params=params(),
        name="join",
    )(tok, gate, h, p, entry.reshape(seqs, 1, lru), ow, gain)


def feed_kernel(first, who, *refs):
    if first:
        n2, cot, fg, fu, fd, hid, gg, gu, acc, ug, uv, gh = refs
    else:
        n2, cot, fg, fu, fd, start, hid, gg, gu, acc, ug, uv, gh = refs
    rows = n2.shape[0]
    ug[...] = nn(n2[...], fg[...])
    uv[...] = nn(n2[...], fu[...])
    gh[...] = nt(cot[...], fd[...])

    def body(i, _):
        at = pl.ds(pl.multiple_of(i * 16, 16), 16)
        act, slope = gelu_parts(ug[at, :])
        v, g = uv[at, :], gh[at, :]
        hid[at, :] = (act * v).astype(BF16)
        gg[at, :] = (g * v * slope).astype(BF16)
        gu[at, :] = (g * act).astype(BF16)
        return 0

    lax.fori_loop(0, rows // 16, body, 0)

    @pl.when(pl.program_id(0) == 0)
    def _():
        if first:
            acc[...] = jnp.zeros_like(acc)
        else:
            acc[...] = start[...]

    acc[...] += nt(gg[...], fg[...]) + nt(gu[...], fu[...])


def feed(half, n2, cot, fg, fu, fd, start):
    rows, model = n2.shape
    units = fg.shape[1]
    tile = 512
    n = units // 2 // tile
    first = start is None
    out = lambda: pl.BlockSpec((rows, tile), lambda i, w: (0, i))
    ins = [
        whole((rows, model)), whole((rows, model)),
        pl.BlockSpec((model, tile), lambda i, w: (0, w[0] * n + i)), pl.BlockSpec((model, tile), lambda i, w: (0, w[0] * n + i)),
        pl.BlockSpec((tile, model), lambda i, w: (w[0] * n + i, 0)),
    ]
    args = [n2, cot, fg, fu, fd]
    if not first:
        ins.append(whole((rows, model)))
        args.append(start)
    return pl.pallas_call(
        functools.partial(feed_kernel, first),
        grid_spec=pltpu.PrefetchScalarGridSpec(
            num_scalar_prefetch=1, grid=(n,), in_specs=ins, out_specs=[out(), out(), out(), whole((rows, model))],
            scratch_shapes=[pltpu.VMEM((rows, tile), F32)] * 3,
        ),
        out_shape=[jax.ShapeDtypeStruct((rows, units // 2), BF16)] * 3 + [jax.ShapeDtypeStruct((rows, model), F32)],
        compiler_params=params(),
        name="feed_a" if first else "feed_b",
    )(half, *args)


def block_out(half, resid, hid_a, hid_b, fd):
    rows, model = resid.shape
    units = fd.shape[0]
    tile = 256

    def kernel(w, r, ha, hb, fa, fb, out):
        out[...] = (r[...] + nn(ha[...], fa[...]) + nn(hb[...], fb[...])).astype(BF16)

    col = lambda: pl.BlockSpec((rows, tile), lambda i, w: (0, i))
    return pl.pallas_call(
        kernel,
        grid_spec=pltpu.PrefetchScalarGridSpec(
            num_scalar_prefetch=1, grid=(model // tile,),
            in_specs=[
                col(), whole((rows, units // 2)), whole((rows, units // 2)),
                pl.BlockSpec((units // 2, tile), lambda i, w: (1 - w[0], i)), pl.BlockSpec((units // 2, tile), lambda i, w: (w[0], i)),
            ],
            out_specs=col(),
        ),
        out_shape=jax.ShapeDtypeStruct((rows, model), BF16),
        compiler_params=params(),
        name="block_out",
    )(half, resid, hid_a, hid_b, fd, fd)


def turn_kernel(
    seqs, length, who, gn, resid, cot, fgain, ow, gate, h, p, entry, rate, sp,
    gres, glow, gain_sum, gg_theirs, gg_mine, lc, q, carry,
    gj,
):
    step = pl.program_id(0)
    rows, width = gj.shape
    model = gn.shape[1]

    @pl.when(step == 0)
    def _():
        g = fgain[...]

        def norm(i, total):
            at = pl.ds(pl.multiple_of(i * 16, 16), 16)
            y, d = resid[at, :], gn[at, :]
            r = lax.rsqrt(jnp.mean(y * y, axis=-1, keepdims=True) + 1e-06)
            dg, yr = d * g, y * r
            dot = jnp.mean(dg * yr, axis=-1, keepdims=True)
            out = cot[at, :].astype(F32) + r * (dg - yr * dot)
            gres[at, :] = out
            glow[at, :] = out.astype(BF16)
            add = d * yr
            return total + add[0:8] + add[8:16]

        total = lax.fori_loop(0, rows // 16, norm, jnp.zeros((8, model), F32))
        gain_sum[...] = jnp.sum(total, axis=0, keepdims=True)

    gj[...] = nt(glow[...], ow[...])
    slope = -8.0 * sp[...]

    def act_part(store):
        for s in range(seqs):
            ent = entry[s]

            def body(i, _):
                at = pl.ds(pl.multiple_of(s * length + i * 16, 16), 16)
                act, der = gelu_parts(gate[at, :])
                state = h[at, :] + p[at, :] * ent
                d = gj[at, :]
                store[at, :] = (d * state * der).astype(BF16)
                gj[at, :] = d * act
                return 0

            lax.fori_loop(0, length // 16, body, 0)

    @pl.when(step == 0)
    def _():
        act_part(gg_theirs)

    @pl.when(step == 1)
    def _():
        act_part(gg_mine)

    row = lax.broadcasted_iota(jnp.int32, (8, width), 0)
    tiles = length // 8

    def scan(k, last):
        i = tiles - 1 - k
        out = []
        for s in range(seqs):
            at = pl.ds(pl.multiple_of(s * length + i * 8, 8), 8)
            g = gj[at, :]
            a = jnp.exp(rate[at, :] * slope)
            b = a * g
            for d in (1, 2, 4):
                keep = row < 8 - d
                b = b + a * jnp.where(keep, pltpu.roll(b, 8 - d, 0), 0.0)
                a = a * jnp.where(keep, pltpu.roll(a, 8 - d, 0), 1.0)
            ap, bp = last[s]
            b = b + a * bp
            a = a * ap
            lc[at, :] = g + jnp.where(row < 7, pltpu.roll(b, 7, 0), bp)
            q[at, :] = jnp.where(row < 7, pltpu.roll(a, 7, 0), ap)
            out.append((a[0:1], b[0:1]))
        return tuple(out)

    init = tuple((jnp.ones((1, width), F32), jnp.zeros((1, width), F32)) for _ in range(seqs))
    last = lax.fori_loop(0, tiles, scan, init)
    for s in range(seqs):
        carry[0, s : s + 1, :] = last[s][0]
        carry[1, s : s + 1, :] = last[s][1]


def turn(half, gn, resid, cot, fgain, ow, gate, h, p, entry, rate, sp, seqs, length):
    rows, model = gn.shape
    lru = gate.shape[1]
    width = lru // 2
    grp = lambda i, w: (1 - i) * (1 - w[0]) + i * w[0]
    col = lambda r: pl.BlockSpec((r, width), lambda i, w: (0, grp(i, w)))
    three = lambda a: pl.BlockSpec((a, seqs, width), lambda i, w: (0, 0, grp(i, w)))
    half_shape = jax.ShapeDtypeStruct((rows, width), BF16)
    f = lambda dt: jax.ShapeDtypeStruct((rows, lru), dt)
    return pl.pallas_call(
        functools.partial(turn_kernel, seqs, length),
        grid_spec=pltpu.PrefetchScalarGridSpec(
            num_scalar_prefetch=1, grid=(2,),
            in_specs=[
                whole((rows, model)), whole((rows, model)), whole((rows, model)), whole((1, model)),
                pl.BlockSpec((width, model), lambda i, w: (grp(i, w), 0)),
                col(rows), col(rows), col(rows), pl.BlockSpec((seqs, 1, width), lambda i, w: (0, 0, grp(i, w))), col(rows), col(1),
            ],
            out_specs=[
                whole((rows, model)), whole((rows, model)), whole((1, model)),
                whole((rows, width)), whole((rows, width)), col(rows), col(rows), three(2),
            ],
            scratch_shapes=[pltpu.VMEM((rows, width), F32)],
        ),
        out_shape=[
            jax.ShapeDtypeStruct((rows, model), F32), jax.ShapeDtypeStruct((rows, model), BF16), jax.ShapeDtypeStruct((1, model), F32),
            half_shape, half_shape, f(F32), f(F32), jax.ShapeDtypeStruct((2, seqs, lru), F32),
        ],
        compiler_params=params(),
        name="turn",
    )(half, gn, resid, cot, fgain, ow, gate, h, p, entry.reshape(seqs, 1, lru), rate, sp)


def gates_kernel(
    seqs, length, lc, q, cin, h, p, entry, rate, inlet, mixed, branch, edge, wr, wi, taps, sp, sg,
    gb, head, tail, rate_sum, inlet_sum, taps_sum, vec_sum,
    dr, di, gr, gi, gm, ext,
):
    rows, width = gm.shape[0] * 0 + seqs * length, wr.shape[0] * wr.shape[1]
    sub = dr.shape[-1]
    bw_ = wr.shape[-1]
    soft, sgm = sp[...], sg[...]
    slope = -8.0 * soft
    zero = jnp.zeros((8, width), F32)
    row = lax.broadcasted_iota(jnp.int32, (16, width), 0)

    sums = (zero, zero, zero)
    for s in range(seqs):
        c_in, ent = cin[s], entry[s]

        def body(i, carry):
            (before, t0, t1, t2) = carry
            at = pl.ds(pl.multiple_of(s * length + i * 16, 16), 16)
            state = h[at, :] + p[at, :] * ent
            prev = jnp.where(row > 0, pltpu.roll(state, 1, 0), before)
            carried = lc[at, :] + q[at, :] * c_in
            rt, it, mx = rate[at, :], inlet[at, :], mixed[at, :].astype(F32)
            log_decay = rt * slope
            decay = jnp.exp(log_decay)
            gap = drop(log_decay, decay)
            inv = lax.rsqrt(gap)
            nf = gap * inv
            im = it * mx
            g_log = carried * decay * (prev - im * decay * inv)
            cn = carried * nf
            g_rt = g_log * slope * (rt * (1.0 - rt))
            g_it = cn * im * (1.0 - it)
            gr[at, :] = g_rt.astype(BF16)
            gi[at, :] = g_it.astype(BF16)
            gm[s, pl.ds(pl.multiple_of(i * 16, 16), 16), :] = cn * it
            lr = g_log * rt
            return (state[15:16], t0 + lr[0:8] + lr[8:16], t1 + g_rt[0:8] + g_rt[8:16], t2 + g_it[0:8] + g_it[8:16])

        _, *sums = lax.fori_loop(0, length // 16, body, (ent, *sums))
        sums = tuple(sums)
    down = lambda v: jnp.sum(v, axis=0, keepdims=True)
    vec_sum[0:1, :] = down(sums[0]) * (-8.0 * sgm)
    vec_sum[1:2, :] = down(sums[1])
    vec_sum[2:3, :] = down(sums[2])

    for g in range(width // sub):
        cols = slice(g * sub, (g + 1) * sub)
        spread(dr.at[g], [wr[g * 4 + a] for a in range(4)], 4, bw_)
        spread(di.at[g], [wi[g * 4 + a] for a in range(4)], 4, bw_)
        back = nt(gr[:, cols], dr[g]) + nt(gi[:, cols], di[g])
        rs = tn(mixed[:, cols], gr[:, cols])
        is_ = tn(mixed[:, cols], gi[:, cols])
        for a in range(4):
            cut = slice(a * bw_, (a + 1) * bw_)
            rate_sum[g * 4 + a] = rs[cut, cut]
            inlet_sum[g * 4 + a] = is_[cut, cut]
        for s in range(seqs):
            gm[s, 0:length, cols] += back[s * length : (s + 1) * length]

    for s in range(seqs):
        gm[s, length : length + 8, :] = zero
        ext[s, 0:8, :] = edge[8 * s : 8 * s + 8].astype(F32)
        ext[s, 8 : 8 + length, :] = branch[s * length : (s + 1) * length].astype(F32)
        head[8 * s : 8 * s + 8, :] = gm[s, 0:8, :]

    tap = [taps[k : k + 1, :] for k in range(4)]
    acc = (zero,) * 5
    for s in range(seqs):

        def conv(i, acc):
            lo = pl.multiple_of(i * 16, 16)
            y = gm[s, pl.ds(lo, 24), :]
            x = ext[s, pl.ds(lo, 24), :]
            total = tap[0] * y[0:16]
            for k in range(1, 4):
                total = total + tap[k] * y[k : k + 16]
            gb[pl.ds(pl.multiple_of(s * length + i * 16, 16), 16), :] = total.astype(BF16)
            now = y[0:16]
            new = []
            for k in range(4):
                prod = now * x[8 - k : 24 - k]
                new.append(acc[k] + prod[0:8] + prod[8:16])
            new.append(acc[4] + now[0:8] + now[8:16])
            return tuple(new)

        acc = lax.fori_loop(0, length // 16, conv, acc)
        y = gm[s, length - 16 : length + 8, :]
        total = tap[0] * y[0:16]
        for k in range(1, 4):
            total = total + tap[k] * y[k : k + 16]
        tail[16 * s : 16 * s + 16, :] = total
    for k in range(4):
        taps_sum[k : k + 1, :] = down(acc[k])
    vec_sum[3:4, :] = down(acc[4])


def gates_back(lc, q, cin, h, p, entry, rate, inlet, mixed, branch, edge, wr, wi, taps, sp, sg, seqs, length):
    rows, lru = lc.shape
    bw_ = wr.shape[-1]
    per = 8
    width = per * bw_
    sub = 4 * bw_
    n = lru // width
    col = lambda r: pl.BlockSpec((r, width), lambda j: (0, j))
    vec = pl.BlockSpec((seqs, 1, width), lambda j: (0, 0, j))
    blk = pl.BlockSpec((per, bw_, bw_), lambda j: (j, 0, 0))
    out = lambda r, dt=F32: jax.ShapeDtypeStruct((r, lru), dt)
    return pl.pallas_call(
        functools.partial(gates_kernel, seqs, length),
        grid=(n,),
        in_specs=[
            col(rows), col(rows), vec, col(rows), col(rows), vec, col(rows), col(rows), col(rows), col(rows), col(edge.shape[0]),
            blk, blk, col(4), col(1), col(1),
        ],
        out_specs=[col(rows), col(8 * seqs), col(16 * seqs), blk, blk, col(4), col(4)],
        out_shape=[out(rows, BF16), out(8 * seqs), out(16 * seqs), jax.ShapeDtypeStruct(wr.shape, F32), jax.ShapeDtypeStruct(wi.shape, F32), out(4), out(4)],
        scratch_shapes=[
            pltpu.VMEM((2, sub, sub), BF16), pltpu.VMEM((2, sub, sub), BF16), pltpu.VMEM((rows, width), BF16), pltpu.VMEM((rows, width), BF16),
            pltpu.VMEM((seqs, length + 8, width), F32), pltpu.VMEM((seqs, length + 8, width), F32),
        ],
        compiler_params=params(),
        name="gates_back",
    )(lc, q, cin.reshape(seqs, 1, lru), h, p, entry.reshape(seqs, 1, lru), rate, inlet, mixed, branch, edge, wr, wi, taps, sp, sg)


def seam_kernel(seqs, length, who, gb, tail, ahead, taps, theirs, mine):
    step = pl.program_id(0)

    def write(out):
        out[...] = gb[...]
        for s in range(seqs):
            y = ahead[8 * s : 8 * s + 8, :]
            t = tail[16 * s : 16 * s + 16, :]
            grown = jnp.concatenate([jnp.zeros((16, t.shape[1]), F32), y], axis=0)
            for k in range(1, 4):
                t = t + taps[k : k + 1, :] * grown[k : k + 16]
            out[(s + 1) * length - 16 : (s + 1) * length, :] = t.astype(BF16)

    @pl.when(step == 0)
    def _():
        write(theirs)

    @pl.when(step == 1)
    def _():
        write(mine)


def seam(half, gb, tail, ahead, taps, seqs, length):
    rows, lru = gb.shape
    width = lru // 2
    grp = lambda i, w: (1 - i) * (1 - w[0]) + i * w[0]
    col = lambda r: pl.BlockSpec((r, width), lambda i, w: (0, grp(i, w)))
    out = jax.ShapeDtypeStruct((rows, width), BF16)
    return pl.pallas_call(
        functools.partial(seam_kernel, seqs, length),
        grid_spec=pltpu.PrefetchScalarGridSpec(
            num_scalar_prefetch=1, grid=(2,), in_specs=[col(rows), col(16 * seqs), col(8 * seqs), col(4)],
            out_specs=[whole((rows, width)), whole((rows, width))],
        ),
        out_shape=[out, out],
        compiler_params=params(),
        name="seam",
    )(half, gb, tail, ahead, taps)


def input_grad(half, gg_theirs, gg_mine, gb_theirs, gb_mine, gw, bw, tok, gres, gain):
    rows, model = tok.shape
    width = gg_mine.shape[1]
    tile = 128

    def kernel(w, gt, gm, bt, bm, gwt, gwm, bwt, bwm, x_ref, gr, g_ref, out, gain_sum):
        d = nt(gt[...], gwt[...]) + nt(gm[...], gwm[...]) + nt(bt[...], bwt[...]) + nt(bm[...], bwm[...])
        x = x_ref[...].astype(F32)
        r = lax.rsqrt(jnp.mean(x * x, axis=-1, keepdims=True) + 1e-06)
        xr, dg = x * r, d * g_ref[...]
        out[...] = gr[...] + r * (dg - xr * jnp.mean(dg * xr, axis=-1, keepdims=True))
        part = jnp.sum(d * xr, axis=0, keepdims=True)

        @pl.when(pl.program_id(0) == 0)
        def _():
            gain_sum[...] = part

        @pl.when(pl.program_id(0) > 0)
        def _():
            gain_sum[...] += part

    row = lambda c: pl.BlockSpec((tile, c), lambda i, w: (i, 0))
    theirs = pl.BlockSpec((model, width), lambda i, w: (0, 1 - w[0]))
    mine = pl.BlockSpec((model, width), lambda i, w: (0, w[0]))
    return pl.pallas_call(
        kernel,
        grid_spec=pltpu.PrefetchScalarGridSpec(
            num_scalar_prefetch=1, grid=(rows // tile,),
            in_specs=[row(width), row(width), row(width), row(width), theirs, mine, theirs, mine, row(model), row(model), whole((1, model))],
            out_specs=[row(model), whole((1, model))],
        ),
        out_shape=[jax.ShapeDtypeStruct((rows, model), F32), jax.ShapeDtypeStruct((1, model), F32)],
        compiler_params=params(),
        name="input_grad",
    )(half, gg_theirs, gg_mine, gb_theirs, gb_mine, gw, gw, bw, bw, tok, gres, gain)


def place_of(core, s, y):
    x, high, low = s % 2, s // 4, (s // 2) % 2
    return (1 - core) * (x * 8 + high * 4 + y * 2 + low) + core * (y * 8 + x * 4 + high * 2 + low)


def put_pieces(out, acc, core, y, first, count):
    part, cols = acc.shape[0] // count, acc.shape[1]
    for j in range(count):
        at = place_of(core, first + j, y)
        for t in range(cols // 128):
            out[at, t * part : (t + 1) * part, :] = acc[j * part : (j + 1) * part, t * 128 : (t + 1) * 128].astype(BF16)


def wgrad(half, lhs, lhs_far, rhs, rhs_far, own_columns, name):
    rows, deep = lhs.shape
    wide = rhs.shape[1] if own_columns else rhs.shape[1] // 2
    tile = wide // 2

    def kernel(w, a, b, c, d, out):
        acc = tn(a[...], c[...]) + tn(b[...], d[...])
        put_pieces(out, acc, w[0], pl.program_id(0), 0, 8)

    base = (lambda w: 0) if own_columns else (lambda w: 2 * w[0])
    right = lambda: pl.BlockSpec((rows, tile), lambda y, w: (0, base(w) + y))
    shape = (16, deep // 8 * (tile // 128), 128)
    return pl.pallas_call(
        kernel,
        grid_spec=pltpu.PrefetchScalarGridSpec(
            num_scalar_prefetch=1, grid=(2,), in_specs=[whole(lhs.shape), whole(lhs.shape), right(), right()], out_specs=whole(shape),
        ),
        out_shape=jax.ShapeDtypeStruct(shape, BF16),
        compiler_params=params(),
        name=name,
    )(half, lhs, lhs_far, rhs, rhs_far)


def wgrad_down(half, theirs, mine, far_theirs, far_mine, cot, cot_far):
    rows, units = mine.shape
    tile = cot.shape[1] // 4

    def kernel(w, ht, hm, ft, fm, c, d, out):
        i, y = pl.program_id(0), pl.program_id(1)

        @pl.when(i == 0)
        def _():
            put_pieces(out, tn(ht[...], c[...]) + tn(fm[...], d[...]), w[0], y, 4 * (1 - w[0]), 4)

        @pl.when(i == 1)
        def _():
            put_pieces(out, tn(hm[...], c[...]) + tn(ft[...], d[...]), w[0], y, 4 * w[0], 4)

    right = lambda: pl.BlockSpec((rows, tile), lambda i, y, w: (0, 2 * w[0] + y))
    shape = (16, units // 4 * (tile // 128), 128)
    return pl.pallas_call(
        kernel,
        grid_spec=pltpu.PrefetchScalarGridSpec(
            num_scalar_prefetch=1, grid=(2, 2), in_specs=[whole(mine.shape)] * 4 + [right(), right()], out_specs=whole(shape),
        ),
        out_shape=jax.ShapeDtypeStruct(shape, BF16),
        compiler_params=params(("arbitrary", "arbitrary")),
        name="wgrad_down",
    )(half, theirs, mine, far_theirs, far_mine, cot, cot_far)


MESH = pl.DeviceIdType.MESH


def meet(peers):
    barrier = pltpu.get_barrier_semaphore()
    for peer in peers:
        pl.semaphore_signal(barrier, inc=1, device_id=peer, device_id_type=MESH)
    pl.semaphore_wait(barrier, len(peers))


def entry_state(part, n, reverse, collective_id):
    _, seqs, lru = part.shape

    def kernel(mine, out, got, send, recv):
        me, b = lax.axis_index("seq"), lax.axis_index("batch")
        peers = [(lax.rem(me + k, n), b) for k in range(1, n)]
        meet(peers)
        copies = []
        for k in range(1, n):
            copy = pltpu.make_async_remote_copy(
                src_ref=mine, dst_ref=got.at[me], send_sem=send.at[k], recv_sem=recv.at[k],
                device_id=peers[k - 1], device_id_type=MESH,
            )
            copy.start()
            copies.append(copy)
        got[me] = mine[...]
        for copy in copies:
            copy.wait()

        def one(k, state):
            j = n - 1 - k if reverse else k
            before = (j > me) if reverse else (j < me)
            return jnp.where(before, got[j, 0] * state + got[j, 1], state)

        out[...] = lax.fori_loop(0, n, one, jnp.zeros((seqs, lru), F32))

    return pl.pallas_call(
        kernel,
        in_specs=[pl.BlockSpec(memory_space=pltpu.VMEM)],
        out_specs=pl.BlockSpec(memory_space=pltpu.VMEM),
        out_shape=jax.ShapeDtypeStruct((seqs, lru), F32),
        scratch_shapes=[pltpu.VMEM((n, 2, seqs, lru), F32), pltpu.SemaphoreType.DMA((n,)), pltpu.SemaphoreType.DMA((n,))],
        compiler_params=pltpu.CompilerParams(collective_id=collective_id, has_side_effects=True, vmem_limit_bytes=VLIM),
        name="entry_back" if reverse else "entry",
    )(part)


def flip(index, bit):
    return index + bit - 2 * bit * (lax.rem(index // bit, 2))


def sum_all(value, seq, batch, collective_id):
    rows = value.shape[0]
    steps = [("batch", 1 << k) for k in range(batch.bit_length() - 1)] + [("seq", 1 << k) for k in range(seq.bit_length() - 1)]

    def kernel(v, out, got, send, recv):
        s, b = lax.axis_index("seq"), lax.axis_index("batch")
        peers = [(flip(s, bit), b) if axis == "seq" else (s, flip(b, bit)) for axis, bit in steps]
        meet(peers)
        copies = []
        got[0] = v[...]
        for k, peer in enumerate(peers):
            copy = pltpu.make_async_remote_copy(
                src_ref=got.at[2 * k], dst_ref=got.at[2 * k + 1], send_sem=send.at[k], recv_sem=recv.at[k], device_id=peer, device_id_type=MESH,
            )
            copy.start()
            copy.wait()
            got[2 * k + 2] = got[2 * k] + got[2 * k + 1]
        out[...] = got[2 * len(steps)]

    n = len(steps)
    return pl.pallas_call(
        kernel,
        in_specs=[pl.BlockSpec(memory_space=pltpu.VMEM)],
        out_specs=pl.BlockSpec(memory_space=pltpu.VMEM),
        out_shape=jax.ShapeDtypeStruct(value.shape, F32),
        scratch_shapes=[pltpu.VMEM((2 * n + 1, rows, 128), F32), pltpu.SemaphoreType.DMA((n,)), pltpu.SemaphoreType.DMA((n,))],
        compiler_params=pltpu.CompilerParams(collective_id=collective_id, has_side_effects=True, vmem_limit_bytes=VLIM),
        name="sum_all",
    )(value)


def scatter_sum(pieces, cut, collective_id, name):
    count, rows = len(pieces), pieces[0].shape[1]
    part = rows // cut
    chunks = count * cut

    def kernel(*refs):
        ins, out = refs[:count], refs[count]
        keep, r1, r2, r3, r4, send, recv, local, back = refs[count + 1 :]
        seq, bat = lax.axis_index("seq"), lax.axis_index("batch")
        core, y = lax.rem(bat, 2), bat // 2
        x, low, high = lax.rem(seq, 2), lax.rem(seq // 2, 2), seq // 4
        pick = lambda a, b: (1 - core) * a + core * b
        ex, elow, ehigh, ey = 1 - 2 * x, 2 - 4 * low, 4 - 8 * high, 2 - 4 * y
        bits = [pick(x, y), pick(high, x), pick(y, high), low]
        peers = [
            (seq + (1 - core) * ex, bat + core * ey),
            (seq + pick(ehigh, ex), bat),
            (seq + core * ehigh, bat + (1 - core) * ey),
            (seq + elow, bat),
            (seq, bat + ey),
            (seq, bat + 1 - 2 * core),
        ]
        meet([(seq + ex, bat), (seq + ehigh, bat), (seq + elow, bat), (seq, bat + ey), (seq, bat + 1 - 2 * core)])
        got = [r1, r2, r3, r4]

        def where(q):
            return q // cut, slice((q % cut) * part, (q % cut + 1) * part)

        def remote(k, q, src, dst):
            return pltpu.make_async_remote_copy(
                src_ref=src, dst_ref=dst, send_sem=send.at[k, q], recv_sem=recv.at[k, q], device_id=peers[k], device_id_type=MESH,
            )

        def copy_of(k, q):
            m, at = where(q)
            if k == 0:
                return remote(0, q, ins[m].at[pl.ds((1 - bits[0]) * 8, 8), at], r1.at[q])
            if k < 4:
                size = 8 >> k
                return remote(k, q, got[k - 1].at[q, pl.ds((1 - bits[k]) * size, size)], got[k].at[q])
            if k == 4:
                slot = out.at[m, core, y, at]
                return remote(4, q, slot, slot)
            slot = out.at[m, core, :, at]
            return remote(5, q, slot, slot)

        def keep_copy(q):
            m, at = where(q)
            return pltpu.make_async_copy(ins[m].at[pl.ds(bits[0] * 8, 8), at], keep.at[q], local.at[q])

        def add(dst, q, base, src, sbase, size):
            for j in range(size):

                def body(i, _):
                    a = pl.ds(pl.multiple_of(i * 64, 64), 64)
                    dst[q, base + j, a, :] = (dst[q, base + j, a, :].astype(F32) + src[q, sbase + j, a, :].astype(F32)).astype(BF16)
                    return 0

                lax.fori_loop(0, part // 64, body, 0)

        def stage(k, q):
            if k < 4:
                size = 8 >> k
                if k == 0:
                    keep_copy(q).wait()
                    src, sbase = keep, 0
                else:
                    src, sbase = got[k - 1], bits[k] * size
                copy_of(k, q).wait_recv()
                if k < 3:
                    half = size // 2
                    far, near = (1 - bits[k + 1]) * half, bits[k + 1] * half
                    add(got[k], q, far, src, sbase + far, half)
                    copy_of(k + 1, q).start()
                    add(got[k], q, near, src, sbase + near, half)
                else:
                    m, at = where(q)

                    def body(i, _):
                        a = pl.ds(pl.multiple_of(i * 64, 64), 64)
                        o = pl.ds(pl.multiple_of(at.start + i * 64, 64), 64)
                        out[m, core, y, o, :] = (r4[q, 0, a, :].astype(F32) + r3[q, sbase, a, :].astype(F32)).astype(BF16)
                        return 0

                    lax.fori_loop(0, part // 64, body, 0)
                    copy_of(4, q).start()
            elif k == 4:
                copy_of(4, q).wait()
                copy_of(5, q).start()
            else:
                copy_of(5, q).wait()

        for t in range(chunks + 8):
            for k in range(5, -1, -1):
                q = t - 2 - k
                if 0 <= q < chunks:
                    stage(k, q)
            if t < chunks:
                copy_of(0, t).start()
                keep_copy(t).start()
        for q in range(chunks):
            for k in range(4):
                copy_of(k, q).wait_send()

    hbm = pl.BlockSpec(memory_space=pl.ANY)
    buf = lambda n: pltpu.VMEM((chunks, n, part, 128), BF16)
    return pl.pallas_call(
        kernel,
        in_specs=[hbm] * count,
        out_specs=pl.BlockSpec(memory_space=pltpu.VMEM),
        out_shape=jax.ShapeDtypeStruct((count, 2, 2, rows, 128), BF16),
        scratch_shapes=[
            buf(8), buf(8), buf(4), buf(2), buf(1),
            pltpu.SemaphoreType.DMA((6, chunks)), pltpu.SemaphoreType.DMA((6, chunks)), pltpu.SemaphoreType.DMA((chunks,)), pltpu.SemaphoreType.DMA((1,)),
        ],
        compiler_params=pltpu.CompilerParams(collective_id=collective_id, has_side_effects=True, vmem_limit_bytes=VLIM),
        name=name,
    )(*pieces)


def shifted(value, axis, steps):
    count = lax.axis_size(axis)
    return lax.ppermute(value, axis, [(i, i + steps) for i in range(count) if 0 <= i + steps < count])


def swap(value):
    count = lax.axis_size("batch")
    return lax.ppermute(value, "batch", [(i, i ^ 1) for i in range(count)])


def local(
    tokens, cotangent, gate_weight, branch_weight, out_weight, conv_taps, conv_offset, rate_weight, inlet_weight,
    rate_offset, inlet_offset, decay_param, mixer_gain, feed_gain, feed_gate, feed_up, feed_down,
):
    seqs, length, model = tokens.shape
    lru, units = gate_weight.shape[1], feed_gate.shape[1]
    rows = seqs * length
    seq_n, batch_n = lax.axis_size("seq"), lax.axis_size("batch")
    core = lax.rem(lax.axis_index("batch"), 2)
    half = jnp.full((1,), core, jnp.int32)

    halo = shifted(tokens[:, length - 8 :, :], "seq", 1).reshape(8 * seqs, model)
    tok, cot = tokens.reshape(rows, model), cotangent.reshape(rows, model)
    cot_far = swap(cot)
    soft, sgm = jax.nn.softplus(decay_param)[None], jax.nn.sigmoid(decay_param)[None]
    gain1, gain2 = mixer_gain[None], feed_gain[None]

    normed, gate, branch, edge, mixed, rate, inlet, h, p, carry = front(
        tok, halo, gain1, gate_weight, branch_weight, conv_taps, conv_offset[None], rate_weight, inlet_weight,
        rate_offset[None], inlet_offset[None], soft, seqs, length,
    )
    normed_far = swap(normed)
    entry = entry_state(carry, seq_n, False, 0)
    joined, resid, normed_two = join(tok, gate, h, p, entry, out_weight, gain2, seqs, length)
    joined_far, normed_two_far = swap(joined), swap(normed_two)
    hid_t, gg_t, gu_t, acc = feed(1 - half, normed_two, cot, feed_gate, feed_up, feed_down, None)
    hid_t_far, gg_far, gu_far = swap(hid_t), swap(gg_t), swap(gu_t)
    hid_m, gg_m, gu_m, grad_two = feed(half, normed_two, cot, feed_gate, feed_up, feed_down, acc)
    hid_m_far = swap(hid_m)
    out = block_out(half, resid, hid_t, hid_m, feed_down)

    grad_resid, grad_low, feed_gain_sum, ggate_t, ggate_m, lc, q, back = turn(
        half, grad_two, resid, cot, gain2, out_weight, gate, h, p, entry, rate, soft, seqs, length
    )
    grad_low_far, ggate_far = swap(grad_low), swap(ggate_t)
    arriving = entry_state(back, seq_n, True, 1)
    gb, head, tail, rate_sum, inlet_sum, taps_sum, vec_sum = gates_back(
        lc, q, arriving, h, p, entry, rate, inlet, mixed, branch, edge, rate_weight, inlet_weight, conv_taps, soft, sgm, seqs, length
    )
    ahead = shifted(head, "seq", -1)
    gb_t, gb_m = seam(half, gb, tail, ahead, conv_taps, seqs, length)
    gb_far = swap(gb_t)
    tokens_grad, mixer_gain_sum = input_grad(half, ggate_t, ggate_m, gb_t, gb_m, gate_weight, branch_weight, tok, grad_resid, gain1)

    small = jnp.concatenate([v.reshape(-1) for v in (taps_sum, vec_sum, mixer_gain_sum, feed_gain_sum)]).reshape(-1, 128)
    small = sum_all(small, seq_n, batch_n, 2).reshape(-1)
    taps_all, vec_all = small[: 4 * lru].reshape(4, lru), small[4 * lru : 8 * lru].reshape(4, lru)
    mixer_gain_all, feed_gain_all = small[8 * lru : 8 * lru + model], small[8 * lru + model :]
    rate_all, inlet_all = lax.psum((rate_sum, inlet_sum), ("seq", "batch"))

    if (seq_n, batch_n) == (8, 4):
        feed_pieces = [
            wgrad_down(half, hid_t, hid_m, hid_t_far, hid_m_far, cot, cot_far),
            wgrad(half, normed_two, normed_two_far, gg_m, gg_far, True, "wgrad_feed_gate"),
            wgrad(half, normed_two, normed_two_far, gu_m, gu_far, True, "wgrad_feed_up"),
        ]
        mixer_pieces = [
            wgrad(half, joined, joined_far, grad_low, grad_low_far, False, "wgrad_out"),
            wgrad(half, normed, normed_far, ggate_m, ggate_far, True, "wgrad_gate"),
            wgrad(half, normed, normed_far, gb_m, gb_far, True, "wgrad_branch"),
        ]
        feed_sums = scatter_sum(feed_pieces, 2, 3, "scatter_feed")
        mixer_sums = scatter_sum(mixer_pieces, 1, 4, "scatter_mixer")

        def laid(sums, part):
            t = sums.shape[2] // part
            return sums.reshape(2, 2, t, part, 128).transpose(3, 0, 1, 2, 4).reshape(part, 4 * t * 128).astype(F32)

        down_all, gate_feed_all, up_feed_all = (
            laid(feed_sums[0], units // 8), laid(feed_sums[1], model // 8), laid(feed_sums[2], model // 8)
        )
        out_all, gate_all, branch_all = (
            laid(mixer_sums[0], lru // 8), laid(mixer_sums[1], model // 8), laid(mixer_sums[2], model // 8)
        )
    else:

        def full(theirs, mine):
            a, b = jnp.where(core == 0, mine, theirs), jnp.where(core == 0, theirs, mine)
            return jnp.concatenate([a, b], axis=1)

        def total(left, right):
            return lax.psum(lax.psum_scatter(tn(left, right), "seq", scatter_dimension=0, tiled=True), "batch")

        down_all = total(full(hid_t, hid_m), cot)
        gate_feed_all = total(normed_two, full(gg_t, gg_m))
        up_feed_all = total(normed_two, full(gu_t, gu_m))
        out_all = total(joined, grad_low)
        gate_all = total(normed, full(ggate_t, ggate_m))
        branch_all = total(normed, full(gb_t, gb_m))

    return (
        out.reshape(seqs, length, model), tokens_grad.reshape(seqs, length, model), gate_all, branch_all, out_all,
        taps_all, vec_all[3], rate_all, inlet_all, vec_all[1], vec_all[2], vec_all[0], mixer_gain_all, feed_gain_all,
        gate_feed_all, up_feed_all, down_all,
    )


def solution(mesh):
    big = P("batch", "seq", None)
    in_specs = (big, big) + (P(),) * 15
    out_specs = (big, big) + (P("seq", None),) * 3 + (P(),) * 9 + (P("seq", None),) * 3
    return jax.shard_map(local, mesh=mesh, in_specs=in_specs, out_specs=out_specs, check_vma=False)
```

time: 1770 us -> 489 us (0.28)
  waiting for transfers between devices: 817 us -> 8.46 us
  local copies, waits for them, and re-layouts: 489 us -> 32.1 us
  Pallas kernels: 0 us -> 419 us
  other arithmetic: 159 us -> 2.19 us
  blocking collectives: 138 us -> 0 us
  matrix products: 123 us -> 0 us
    reduce_scatter x6 -> x0, waiting for transfers between devices: 743 us -> none  [the longest x1 212 us: local(): lax.psum_scatter(upfeed_sum, 'seq', scatter_dimension=0, tiled=True)]
    pallas_call x0 -> x20, Pallas kernels: none -> 419 us  [the longest x2 200 us: scatter_sum(): pl.pallas_call(kernel, in_specs=[hbm] * count, out_specs=pl.BlockSpec(mem...]
    slice x113 -> x5, local copies, waits for them, and re-layouts: 245 us -> 5.85 us  [the longest x1 1.76 us: local(): feed_sums[0]]
    dot_general x24 -> x0, matrix products: 123 us -> none  [the longest x6 41.5 us: outer_product(): lax.dot_general(left, right, (((0,), (0,)), ((), ())), preferred_element_...]
    pad x56 -> x0, local copies, waits for them, and re-layouts: 96.2 us -> none  [the longest x28 64 us: local(): lax.associative_scan(combine, (decay, drive), axis=1)]
    all_gather x4 -> x0, blocking collectives: 96.1 us -> none  [carried_in(): gathered = jax.tree.map(lambda a: lax.all_gather(a, axis), part)]
    add x55 -> x0, other arithmetic: 72.4 us -> none  [the longest x20 24.7 us: combine(): return (earlier[0] * later[0], later[0] * earlier[1] + later[1])]
    psum x2 -> x1, waiting for transfers between devices: 72.4 us -> 0.01 us  [local(): rate_all, inlet_all = lax.psum((rate_sum, inlet_sum), ('seq', 'batch'))]
  transfers between devices with their start and end apart: 10 -> 14, of which waited for: 6 -> 3; matrix products, arithmetic and copies ran while one was open for 22% -> 6% of each run, Pallas kernels for 0% -> 64%
where the time goes in v1:
time: 489 us; the launch traced here: 488 us
  Pallas kernels  419 us (86%)
  local copies, waits for them, and re-layouts  32.1 us (7%)
  between operations  14.3 us (3%)
  starting transfers between devices  11.4 us (2%)
  waiting for transfers between devices  8.46 us (2%)
    pallas_call x2, Pallas kernels, scatter_sum(): pl.pallas_call(kernel, in_specs=[hbm] * count, out_specs=pl.BlockSpec(mem...  200 us
    pallas_call x2, Pallas kernels, feed(): pl.pallas_call(functools.partial(feed_kernel, first), grid_spec=pltpu.Pre...  34 us
    pallas_call x5, Pallas kernels, wgrad(): pl.pallas_call(kernel, grid_spec=pltpu.PrefetchScalarGridSpec(num_scalar_...  31.3 us
    pallas_call x1, Pallas kernels, front(): pl.pallas_call(functools.partial(front_kernel, seqs, length), grid=(n,),...  27.9 us
    pallas_call x1, Pallas kernels, turn(): pl.pallas_call(functools.partial(turn_kernel, seqs, length), grid_spec=pl...  25 us
    pallas_call x1, Pallas kernels, gates_back(): pl.pallas_call(functools.partial(gates_kernel, seqs, length), grid=(n,),...  21.3 us
    pallas_call x2, Pallas kernels, entry_state(): pl.pallas_call(kernel, in_specs=[pl.BlockSpec(memory_space=pltpu.VMEM)],...  19.3 us
    pallas_call x1, Pallas kernels, sum_all(): pl.pallas_call(kernel, in_specs=[pl.BlockSpec(memory_space=pltpu.VMEM)],...  15.1 us
  transfers between devices with their start and end apart: 14, of which 3 were waited for; matrix products, arithmetic and copies ran while one was open for 6% of the time, Pallas kernels for 64%

profile of v1, /device:TPU:13, one launch (start us, length us, event | category | flops | bytes accessed | tf_op | source)
XLA Modules:
  0.0 487.6 jit_solution(17140169420844566370)
XLA Ops:
  8.0 3.1 collective-permute-start
  16.9 27.9 %front.1 = (bf16[512,1024]{1,0:T(8,128)(2,1)}, f32[512,1536]{1,0:T(8,128)}, bf16[512,1536]{1,0:T(8,128)(2,1)}, bf16[16,1536]{1,0:T(8,128)(2,1)}, bf16[512,1536]{...) custom-call(bf16[512,1024]{1,0:T(8,128)(2,1)} %bitcast.57, ...), custom_call_target="tpu_custom_call" | custom-call | tf_op jit(solution)/shard_map/front/pallas_call | solution.py:174
  44.9 9.2 %entry.1 = f32[2,1536]{1,0:T(2,128)} custom-call(f32[2,2,1536]{2,1,0:T(2,128)} %get-tuple-element.60.mine), custom_call_target="tpu_custom_call" | custom-call | tf_op jit(solution)/shard_map/entry/pallas_call | solution.py:747
  55.4 10.8 %join.1 = (bf16[512,1536]{1,0:T(8,128)(2,1)}, f32[512,1024]{1,0:T(8,128)}, bf16[512,1024]{1,0:T(8,128)(2,1)}) custom-call(bf16[512,1024]{1,0:T(8,128)(2,1)} %bitcast.58, f32[512,1536]{1,0:T(8,128)} %get-tuple-element.57.gate, f32[512,1536]{1,0:T(8,128)} %get-tuple-element.58.h, f32[512,1536]{1,0:T(8,128)} %get-tuple-element.59.p, ...), custom_call_target="tpu_custom_call" | custom-call | tf_op jit(solution)/shard_map/join/pallas_call | solution.py:231
  66.3 16.6 %feed_a.1 = (bf16[512,1536]{1,0:T(8,128)(2,1)}, bf16[512,1536]{1,0:T(8,128)(2,1)}, bf16[512,1536]{1,0:T(8,128)(2,1)}, f32[512,1024]{1,0:T(8,128)}) custom-call(s32[1]{0:T(128)S(6)} %sub.3.who, bf16[512,1024]{1,0:T(8,128)(2,1)} %get-tuple-element.62.refs_0_.a, bf16[512,1024]{1,0:T(8,128)(2,1)} %bitcast.52, bf16[1024,3072]{1,0:T(8,128)(2,1)} %refs_2_.3, ...), custom_call_target="tpu_custom_call" | custom-call | tf_op jit(solution)/shard_map/feed_a/pallas_call | solution.py:289
  82.8 17.5 %feed_b.1 = (bf16[512,1536]{1,0:T(8,128)(2,1)}, bf16[512,1536]{1,0:T(8,128)(2,1)}, bf16[512,1536]{1,0:T(8,128)(2,1)}, f32[512,1024]{1,0:T(8,128)}) custom-call(s32[1]{0:T(128)} %bitcast.who.w, bf16[512,1024]{1,0:T(8,128)(2,1)} %get-tuple-element.62.refs_0_.a, bf16[512,1024]{1,0:T(8,128)(2,1)} %bitcast.53, bf16[1024,3072]{1,0:T(8,128)(2,1)} %refs_2_.3, ...), custom_call_target="tpu_custom_call" | custom-call | tf_op jit(solution)/shard_map/feed_b/pallas_call | solution.py:289
  100.3 25.0 %turn.1 = (f32[512,1024]{1,0:T(8,128)}, bf16[512,1024]{1,0:T(8,128)(2,1)}, f32[1,1024]{1,0:T(1,128)}, bf16[512,768]{1,0:T(8,128)(2,1)}, bf16[512,768]{1,0:T(8,12...) custom-call(s32[1]{0:T(128)} %bitcast.who.w, f32[512,1024]{1,0:T(8,128)} %get-tuple-element.66.gn, ...), custom_call_target="tpu_custom_call" | custom-call | tf_op jit(solution)/shard_map/turn/pallas_call | solution.py:419
  127.9 10.0 %entry_back.1 = f32[2,1536]{1,0:T(2,128)} custom-call(f32[2,2,1536]{2,1,0:T(2,128)} %get-tuple-element.72.mine), custom_call_target="tpu_custom_call" | custom-call | tf_op jit(solution)/shard_map/entry_back/pallas_call | solution.py:747
  139.3 21.3 %gates_back.1 = (bf16[512,1536]{1,0:T(8,128)(2,1)}, f32[16,1536]{1,0:T(8,128)}, f32[32,1536]{1,0:T(8,128)}, f32[16,96,96]{2,1,0:T(8,128)}, f32[16,96,96]{2,1,0:T...) custom-call(f32[512,1536]{1,0:T(8,128)} %get-tuple-element.70.lc, f32[512,1536]{1,0:T(8,128)} %get-tuple-element.71.q, ...), custom_call_target="tpu_custom_call" | custom-call | tf_op jit(solution)/shard_map/gates_back/pallas_call | solution.py:552
  160.6 2.9 collective-permute-start.1
  163.5 3.2 collective-permute-done.1.ahead
  167.4 2.7 seam.1
  172.0 2.6 collective-permute-done.6.d
  178.4 8.3 %block_out.1 = bf16[512,1024]{1,0:T(8,128)(2,1)} custom-call(s32[1]{0:T(128)} %bitcast.who.w, f32[512,1024]{1,0:T(8,128)} %get-tuple-element.61.r.resid, bf16[512,1536]{1,0:T(8,128)(2,1)} %get-tuple-element.63.ha.ht, bf16[512,1536]{1,0:T(8,128)(2,1)} %get-tuple-element.65.hb.hm, bf16[3072,1024]{1,0:T(8,128)(2,1)} %fb.1, bf16[3072,1024]{1,0:T(8,128)(2,1)} %fb.1), custom_call_target="tpu_custom_call" | custom-call | tf_op jit(solution)/shard_map/block_out/pallas_call | solution.py:310
  186.8 13.7 %input_grad.1 = (f32[512,1024]{1,0:T(8,128)}, f32[1,1024]{1,0:T(1,128)}) custom-call(s32[1]{0:T(128)} %bitcast.who.w, bf16[512,768]{1,0:T(8,128)(2,1)} %get-tuple-element.68.gt, bf16[512,768]{1,0:T(8,128)(2,1)} %get-tuple-element.69.gm.c, bf16[512,768]{1,0:T(8,128)(2,1)} %get-tuple-element.80.bt, bf16[512,768]{1,0:T(8,128)(2,1)} %get-tuple-element.81.bm.c, ...), custom_call_target="tpu_custom_call" | custom-call | tf_op jit(solution)/shard_map/input_grad/pallas_call | solution.py:634
  202.2 15.1 %sum_all.1 = f32[112,128]{1,0:T(8,128)} custom-call(f32[112,128]{1,0:T(8,128)} %maximum_bitcast_fusion.v), custom_call_target="tpu_custom_call" | custom-call | tf_op jit(solution)/shard_map/sum_all/pallas_call | solution.py:782
  221.4 5.6 %wgrad_branch.1.refs_2_ = bf16[16,384,128]{2,1,0:T(8,128)(2,1)} custom-call(s32[1]{0:T(128)} %bitcast.who.w, bf16[512,1024]{1,0:T(8,128)(2,1)} %get-tuple-element.86.a, bf16[512,1024]{1,0:T(8,128)(2,1)} %copy-done.5, bf16[512,768]{1,0:T(8,128)(2,1)} %get-tuple-element.81.bm.c, bf16[512,768]{1,0:T(8,128)(2,1)} %copy-done.8), custom_call_target="tpu_custom_call" | custom-call | tf_op jit(solution)/shard_map/wgrad_branch/pallas_call | solution.py:672
  227.0 5.6 %wgrad_gate.1.refs_1_ = bf16[16,384,128]{2,1,0:T(8,128)(2,1)} custom-call(s32[1]{0:T(128)} %bitcast.who.w, bf16[512,1024]{1,0:T(8,128)(2,1)} %get-tuple-element.86.a, bf16[512,1024]{1,0:T(8,128)(2,1)} %copy-done.5, bf16[512,768]{1,0:T(8,128)(2,1)} %get-tuple-element.69.gm.c, bf16[512,768]{1,0:T(8,128)(2,1)} %copy-done.7), custom_call_target="tpu_custom_call" | custom-call | tf_op jit(solution)/shard_map/wgrad_gate/pallas_call | solution.py:672
  232.6 7.4 %wgrad_feed_up.1.refs_2_ = bf16[16,768,128]{2,1,0:T(8,128)(2,1)} custom-call(s32[1]{0:T(128)} %bitcast.who.w, bf16[512,1024]{1,0:T(8,128)(2,1)} %get-tuple-element.62.refs_0_.a, bf16[512,1024]{1,0:T(8,128)(2,1)} %copy-done.3, bf16[512,1536]{1,0:T(8,128)(2,1)} %get-tuple-element.95.c, bf16[512,1536]{1,0:T(8,128)(2,1)} %collective-permute-done.12.d), custom_call_target="tpu_custom_call" | custom-call | tf_op jit(solution)/shard_map/wgrad_feed_up/pallas_call | solution.py:672
  239.9 7.4 %wgrad_feed_gate.1.refs_1_ = bf16[16,768,128]{2,1,0:T(8,128)(2,1)} custom-call(s32[1]{0:T(128)} %bitcast.who.w, bf16[512,1024]{1,0:T(8,128)(2,1)} %get-tuple-element.62.refs_0_.a, bf16[512,1024]{1,0:T(8,128)(2,1)} %copy-done.3, bf16[512,1536]{1,0:T(8,128)(2,1)} %get-tuple-element.93.c, bf16[512,1536]{1,0:T(8,128)(2,1)} %collective-permute-done.11.d), custom_call_target="tpu_custom_call" | custom-call | tf_op jit(solution)/shard_map/wgrad_feed_gate/pallas_call | solution.py:672
  247.3 9.0 %wgrad_down.1.refs_0_ = bf16[16,768,128]{2,1,0:T(8,128)(2,1)} custom-call(s32[1]{0:T(128)} %bitcast.who.w, bf16[512,1536]{1,0:T(8,128)(2,1)} %get-tuple-element.63.ha.ht, bf16[512,1536]{1,0:T(8,128)(2,1)} %get-tuple-element.65.hb.hm, bf16[512,1536]{1,0:T(8,128)(2,1)} %collective-permute-done.7.ft, bf16[512,1536]{1,0:T(8,128)(2,1)} %collective-permute-done.8.fm, ...), custom_call_target="tpu_custom_call" | custom-call | tf_op jit(solution)/shard_map/wgrad_down/pallas_call | solution.py:700
  256.4 122.3 %scatter_feed.1 = bf16[3,2,2,768,128]{4,3,2,1,0:T(8,128)(2,1)} custom-call(bf16[16,768,128]{2,1,0:T(8,128)(2,1)} %wgrad_down.1.refs_0_, bf16[16,768,128]{2,1,0:T(8,128)(2,1)} %wgrad_feed_gate.1.refs_1_, bf16[16,768,128]{2,1,0:T(8,128)(2,1)} %wgrad_feed_up.1.refs_2_), custom_call_target="tpu_custom_call" | custom-call | tf_op jit(solution)/shard_map/scatter_feed/pallas_call | solution.py:899
  388.0 5.4 %wgrad_out.1.refs_0_ = bf16[16,384,128]{2,1,0:T(8,128)(2,1)} custom-call(s32[1]{0:T(128)} %bitcast.who.w, bf16[512,1536]{1,0:T(8,128)(2,1)} %get-tuple-element.84.a, bf16[512,1536]{1,0:T(8,128)(2,1)} %collective-permute-done.2.b, bf16[512,1024]{1,0:T(8,128)(2,1)} %get-tuple-element.85.c, bf16[512,1024]{1,0:T(8,128)(2,1)} %collective-permute-done.3.d), custom_call_target="tpu_custom_call" | custom-call | tf_op jit(solution)/shard_map/wgrad_out/pallas_call | solution.py:672
  393.3 78.2 %scatter_mixer.1 = bf16[3,2,2,384,128]{4,3,2,1,0:T(8,128)(2,1)} custom-call(bf16[16,384,128]{2,1,0:T(8,128)(2,1)} %wgrad_out.1.refs_0_, bf16[16,384,128]{2,1,0:T(8,128)(2,1)} %wgrad_gate.1.refs_1_, bf16[16,384,128]{2,1,0:T(8,128)(2,1)} %wgrad_branch.1.refs_2_), custom_call_target="tpu_custom_call" | custom-call | tf_op jit(solution)/shard_map/scatter_mixer/pallas_call | solution.py:899
  (87 shorter events, 42.3 us)
Async XLA Ops:
  7.2 470.5 %all-reduce.3.cloned.1.call-start = ((), (), s32[]{:S(2)}) async-start(), calls=%async_computation | async-start | bytes 3145728 | tf_op jit(solution)/shard_map/psum | solution.py:971
  8.0 8.3 %collective-permute-start = (bf16[2,8,1024]{2,1,0:T(8,128)(2,1)S(1)}, bf16[2,8,1024]{2,1,0:T(8,128)(2,1)S(1)}, u32[]{:S(2)}, u32[]{:S(2)}) collective-permute-start(bf16[2,8,1024]{2,1,0:T(8,128)(2,1)S(1)} %slice.59), channel_id=1, source_target_pairs={{0,4},{4,8},{8,12},{12,16},{16,20},{20,24},{24,28},{1,5},{5,9},{9,... | collective-permute-start | bytes 98312 | tf_op jit(solution)/shard_map/ppermute | solution.py:915
  100.3 26.5 %copy-start.1 = (bf16[512,1024]{1,0:T(8,128)(2,1)S(1)}, bf16[512,1024]{1,0:T(8,128)(2,1)}, u32[]{:S(2)}) copy-start(bf16[512,1024]{1,0:T(8,128)(2,1)} %get-tuple-element.62.refs_0_.a) | copy-start | bytes 3145732
  125.4 46.1 %collective-permute-start.5 = (bf16[512,768]{1,0:T(8,128)(2,1)}, bf16[512,768]{1,0:T(8,128)(2,1)S(1)}, u32[]{:S(2)}, u32[]{:S(2)}) collective-permute-start(bf16[512,768]{1,0:T(8,128)(2,1)} %get-tuple-element.68.gt), channel_id=1, source_target_pairs={{0,1},{1,0},{2,3},{3,2},{4,5},{5,4},{6,7},{7,6},{8,9},{9,8},{10,11... | collective-permute-start | bytes 2359304 | tf_op jit(solution)/shard_map/ppermute | solution.py:920
  126.8 48.2 %collective-permute-start.10 = (bf16[512,1024]{1,0:T(8,128)(2,1)S(1)}, bf16[512,1024]{1,0:T(8,128)(2,1)S(1)}, u32[]{:S(2)}, u32[]{:S(2)}) collective-permute-start(bf16[512,1024]{1,0:T(8,128)(2,1)S(1)} %copy-done.1), channel_id=1, source_target_pairs={{0,1},{1,0},{2,3},{3,2},{4,5},{5,4},{6,7},{7,6},{8,9},{9,8},{10,11... | collective-permute-start | bytes 3145736 | tf_op jit(solution)/shard_map/ppermute | solution.py:920
  126.9 51.3 %collective-permute-start.12 = (bf16[512,1536]{1,0:T(8,128)(2,1)}, bf16[512,1536]{1,0:T(8,128)(2,1)}, u32[]{:S(2)}, u32[]{:S(2)}) collective-permute-start(bf16[512,1536]{1,0:T(8,128)(2,1)} %get-tuple-element.96), channel_id=1, source_target_pairs={{0,1},{1,0},{2,3},{3,2},{4,5},{5,4},{6,7},{7,6},{8,9},{9,8},{10,11... | collective-permute-start | bytes 4718600 | tf_op jit(solution)/shard_map/ppermute | solution.py:920
  139.3 32.2 %copy-start.4 = (bf16[512,1024]{1,0:T(8,128)(2,1)S(1)}, bf16[512,1024]{1,0:T(8,128)(2,1)}, u32[]{:S(2)}) copy-start(bf16[512,1024]{1,0:T(8,128)(2,1)} %get-tuple-element.86.a) | copy-start | bytes 3145732
  139.3 35.8 %copy-start.2 = (bf16[512,1536]{1,0:T(8,128)(2,1)S(1)}, bf16[512,1536]{1,0:T(8,128)(2,1)}, u32[]{:S(2)}) copy-start(bf16[512,1536]{1,0:T(8,128)(2,1)} %get-tuple-element.63.ha.ht) | copy-start | bytes 4718596
  160.6 17.2 %copy-start = (bf16[2,256,1024]{2,1,0:T(8,128)(2,1)S(1)}, bf16[2,256,1024]{2,1,0:T(8,128)(2,1)}, u32[]{:S(2)}) copy-start(bf16[2,256,1024]{2,1,0:T(8,128)(2,1)} %param.18) | copy-start | bytes 3145732
  160.6 6.1 %collective-permute-start.1 = (f32[16,1536]{1,0:T(8,128)}, f32[16,1536]{1,0:T(8,128)S(1)}, u32[]{:S(2)}, u32[]{:S(2)}) collective-permute-start(f32[16,1536]{1,0:T(8,128)} %get-tuple-element.79), channel_id=1, source_target_pairs={{4,0},{8,4},{12,8},{16,12},{20,16},{24,20},{28,24},{5,1},{9,5},{13... | collective-permute-start | bytes 294920 | tf_op jit(solution)/shard_map/ppermute | solution.py:915
  170.1 4.5 collective-permute-start.6
  171.5 29.1 %collective-permute-start.11 = (bf16[512,1536]{1,0:T(8,128)(2,1)}, bf16[512,1536]{1,0:T(8,128)(2,1)}, u32[]{:S(2)}, u32[]{:S(2)}) collective-permute-start(bf16[512,1536]{1,0:T(8,128)(2,1)} %get-tuple-element.94), channel_id=1, source_target_pairs={{0,1},{1,0},{2,3},{3,2},{4,5},{5,4},{6,7},{7,6},{8,9},{9,8},{10,11... | collective-permute-start | bytes 4718600 | tf_op jit(solution)/shard_map/ppermute | solution.py:920
  171.5 15.2 %copy-start.7 = (bf16[512,768]{1,0:T(8,128)(2,1)}, bf16[512,768]{1,0:T(8,128)(2,1)S(1)}, u32[]{:S(2)}) copy-start(bf16[512,768]{1,0:T(8,128)(2,1)S(1)} %collective-permute-done.5.d) | copy-start | bytes 2359300
  171.5 6.3 %collective-permute-start.4 = (bf16[512,1024]{1,0:T(8,128)(2,1)S(1)}, bf16[512,1024]{1,0:T(8,128)(2,1)S(1)}, u32[]{:S(2)}, u32[]{:S(2)}) collective-permute-start(bf16[512,1024]{1,0:T(8,128)(2,1)S(1)} %copy-done.4), channel_id=1, source_target_pairs={{0,1},{1,0},{2,3},{3,2},{4,5},{5,4},{6,7},{7,6},{8,9},{9,8},{10,11... | collective-permute-start | bytes 3145736 | tf_op jit(solution)/shard_map/ppermute | solution.py:920
  174.7 72.7 %collective-permute-start.8 = (bf16[512,1536]{1,0:T(8,128)(2,1)}, bf16[512,1536]{1,0:T(8,128)(2,1)}, u32[]{:S(2)}, u32[]{:S(2)}) collective-permute-start(bf16[512,1536]{1,0:T(8,128)(2,1)} %get-tuple-element.65.hb.hm), channel_id=1, source_target_pairs={{0,1},{1,0},{2,3},{3,2},{4,5},{5,4},{6,7},{7,6},{8,9},{9,8},{10,11... | collective-permute-start | bytes 4718600 | tf_op jit(solution)/shard_map/ppermute | solution.py:920
  175.0 11.6 %copy-start.3 = (bf16[512,1024]{1,0:T(8,128)(2,1)}, bf16[512,1024]{1,0:T(8,128)(2,1)S(1)}, u32[]{:S(2)}) copy-start(bf16[512,1024]{1,0:T(8,128)(2,1)S(1)} %collective-permute-done.10.b) | copy-start | bytes 3145732
  175.1 72.3 %collective-permute-start.7 = (bf16[512,1536]{1,0:T(8,128)(2,1)S(1)}, bf16[512,1536]{1,0:T(8,128)(2,1)}, u32[]{:S(2)}, u32[]{:S(2)}) collective-permute-start(bf16[512,1536]{1,0:T(8,128)(2,1)S(1)} %copy-done.2), channel_id=1, source_target_pairs={{0,1},{1,0},{2,3},{3,2},{4,5},{5,4},{6,7},{7,6},{8,9},{9,8},{10,11... | collective-permute-start | bytes 4718600 | tf_op jit(solution)/shard_map/ppermute | solution.py:920
  177.8 8.9 %copy-start.5 = (bf16[512,1024]{1,0:T(8,128)(2,1)}, bf16[512,1024]{1,0:T(8,128)(2,1)S(1)}, u32[]{:S(2)}) copy-start(bf16[512,1024]{1,0:T(8,128)(2,1)S(1)} %collective-permute-done.4.b) | copy-start | bytes 3145732
  177.8 69.5 %collective-permute-start.9 = (bf16[512,1024]{1,0:T(8,128)(2,1)S(1)}, bf16[512,1024]{1,0:T(8,128)(2,1)}, u32[]{:S(2)}, u32[]{:S(2)}) collective-permute-start(bf16[512,1024]{1,0:T(8,128)(2,1)S(1)} %bitcast.56), channel_id=1, source_target_pairs={{0,1},{1,0},{2,3},{3,2},{4,5},{5,4},{6,7},{7,6},{8,9},{9,8},{10,11... | collective-permute-start | bytes 3145736 | tf_op jit(solution)/shard_map/ppermute | solution.py:920
  178.2 8.5 %copy-start.12 = (f32[4,1536]{1,0:T(4,128)S(1)}, f32[4,1536]{1,0:T(4,128)}, u32[]{:S(2)}) copy-start(f32[4,1536]{1,0:T(4,128)} %get-tuple-element.87) | copy-start | bytes 73732
  178.2 8.6 %copy-start.11 = (f32[4,1536]{1,0:T(4,128)S(1)}, f32[4,1536]{1,0:T(4,128)}, u32[]{:S(2)}) copy-start(f32[4,1536]{1,0:T(4,128)} %get-tuple-element.88) | copy-start | bytes 73732
  178.2 209.8 %collective-permute-start.2 = (bf16[512,1536]{1,0:T(8,128)(2,1)}, bf16[512,1536]{1,0:T(8,128)(2,1)}, u32[]{:S(2)}, u32[]{:S(2)}) collective-permute-start(bf16[512,1536]{1,0:T(8,128)(2,1)} %get-tuple-element.84.a), channel_id=1, source_target_pairs={{0,1},{1,0},{2,3},{3,2},{4,5},{5,4},{6,7},{7,6},{8,9},{9,8},{10,11... | collective-permute-start | bytes 4718600 | tf_op jit(solution)/shard_map/ppermute | solution.py:920
  186.8 14.1 %copy-start.13 = (f32[1,1024]{1,0:T(1,128)S(1)}, f32[1,1024]{1,0:T(1,128)}, u32[]{:S(2)}) copy-start(f32[1,1024]{1,0:T(1,128)} %get-tuple-element.90) | copy-start | bytes 12292
  200.5 187.4 %collective-permute-start.3 = (bf16[512,1024]{1,0:T(8,128)(2,1)}, bf16[512,1024]{1,0:T(8,128)(2,1)}, u32[]{:S(2)}, u32[]{:S(2)}) collective-permute-start(bf16[512,1024]{1,0:T(8,128)(2,1)} %get-tuple-element.85.c), channel_id=1, source_target_pairs={{0,1},{1,0},{2,3},{3,2},{4,5},{5,4},{6,7},{7,6},{8,9},{9,8},{10,11... | collective-permute-start | bytes 3145736 | tf_op jit(solution)/shard_map/ppermute | solution.py:920
  (4 other events, 6.9 us)
Sparse Core Ops, SparseCore 0:
  186.9 138.4 all-reduce.2

commit v2 on v1

v2 whole, which is shorter than its diff:
```python
import functools
import jax
import jax.numpy as jnp
from jax import lax
from jax.experimental import pallas as pl
from jax.experimental.pallas import tpu as pltpu
from jax.sharding import PartitionSpec as P

F32, BF16 = jnp.float32, jnp.bfloat16
VLIM = 56 * 2**20
GELU_A, GELU_B = 0.7978845608028654, 0.044715


def nn(a, b):
    return lax.dot_general(a, b, (((1,), (0,)), ((), ())), preferred_element_type=F32)


def nt(a, b):
    return lax.dot_general(a, b, (((1,), (1,)), ((), ())), preferred_element_type=F32)


def tn(a, b):
    return lax.dot_general(a, b, (((0,), (0,)), ((), ())), preferred_element_type=F32)


def sigmoid(v):
    return 1.0 / (1.0 + jnp.exp(-v))


def drop(u, decay):
    v = 2.0 * u
    series = 1.0 + v * (1.0 / 7.0)
    for k in (6.0, 5.0, 4.0, 3.0, 2.0):
        series = 1.0 + (v * (1.0 / k)) * series
    return jnp.where(v > -0.35, -v * series, 1.0 - decay * decay)


def gelu_parts(v):
    square = v * v
    inner = jnp.tanh(GELU_A * v * (1.0 + GELU_B * square))
    half = 0.5 + 0.5 * inner
    act = v * half
    slope = half + 0.5 * v * (1.0 - inner * inner) * (GELU_A + 3.0 * GELU_A * GELU_B * square)
    return act, slope


def gelu(v):
    inner = jnp.tanh(GELU_A * v * (1.0 + GELU_B * (v * v)))
    return v * (0.5 + 0.5 * inner)


def spread(dense, blocks, count, width):
    for a in range(count):
        parts = []
        if a > 0:
            parts.append(jnp.zeros((width, a * width), dense.dtype))
        parts.append(blocks[a])
        if a < count - 1:
            parts.append(jnp.zeros((width, (count - 1 - a) * width), dense.dtype))
        dense[a * width : (a + 1) * width, :] = jnp.concatenate(parts, axis=1)


def params(sem=("arbitrary",), **kw):
    return pltpu.CompilerParams(dimension_semantics=sem, vmem_limit_bytes=VLIM, **kw)


def whole(shape):
    return pl.BlockSpec(shape, lambda *_: (0,) * len(shape))


def front_kernel(
    seqs, length, tok, halo, gain, gw, bw, taps, coff, wr, wi, roff, ioff, sp,
    normed, gate, branch, edge, mixed, rate, inlet, h, p, carry,
    hn, ext, dr, di, rp, ip,
):
    rows, width = seqs * length, gw.shape[1]
    sub = dr.shape[-1]

    @pl.when(pl.program_id(0) == 0)
    def _():
        def norm(i, _):
            x = tok[pl.ds(i * 32, 32), :].astype(F32)
            r = lax.rsqrt(jnp.mean(x * x, axis=-1, keepdims=True) + 1e-06)
            normed[pl.ds(i * 32, 32), :] = (x * r * gain[...]).astype(BF16)
            return 0

        lax.fori_loop(0, rows // 32, norm, 0)
        x = halo[...].astype(F32)
        r = lax.rsqrt(jnp.mean(x * x, axis=-1, keepdims=True) + 1e-06)
        hn[...] = (x * r * gain[...]).astype(BF16)

    gate[...] = nn(normed[...], gw[...])
    b16 = nn(normed[...], bw[...]).astype(BF16)
    e16 = nn(hn[...], bw[...]).astype(BF16)
    branch[...] = b16
    edge[...] = e16
    for s in range(seqs):
        ext[s, 0:8, :] = e16[8 * s : 8 * s + 8].astype(F32)
        ext[s, 8 : 8 + length, :] = b16[length * s : length * (s + 1)].astype(F32)

    tap = [taps[k : k + 1, :] for k in range(4)]
    off = coff[...]
    for s in range(seqs):

        def conv(i, _):
            x = ext[s, pl.ds(pl.multiple_of(i * 16, 16), 24), :]
            total = off + tap[0] * x[8:24]
            for k in range(1, 4):
                total = total + tap[k] * x[8 - k : 24 - k]
            mixed[pl.ds(pl.multiple_of(s * length + i * 16, 16), 16), :] = total.astype(BF16)
            return 0

        lax.fori_loop(0, length // 16, conv, 0)

    for g in range(width // sub):
        cols = slice(g * sub, (g + 1) * sub)
        spread(dr.at[g], [wr[g * 4 + a] for a in range(4)], 4, wr.shape[-1])
        spread(di.at[g], [wi[g * 4 + a] for a in range(4)], 4, wi.shape[-1])
        rp[:, cols] = nn(mixed[:, cols], dr[g])
        ip[:, cols] = nn(mixed[:, cols], di[g])

    ro, io, slope = roff[...], ioff[...], -8.0 * sp[...]

    def gates(i, _):
        at = pl.ds(pl.multiple_of(i * 16, 16), 16)
        rt = sigmoid(rp[at, :] + ro)
        it = sigmoid(ip[at, :] + io)
        log_decay = rt * slope
        decay = jnp.exp(log_decay)
        rate[at, :] = rt
        inlet[at, :] = it
        p[at, :] = decay
        h[at, :] = jnp.sqrt(drop(log_decay, decay)) * it * mixed[at, :].astype(F32)
        return 0

    lax.fori_loop(0, rows // 16, gates, 0)

    row = lax.broadcasted_iota(jnp.int32, (8, width), 0)

    def scan(i, last):
        out = []
        for s in range(seqs):
            at = pl.ds(pl.multiple_of(s * length + i * 8, 8), 8)
            a, b = p[at, :], h[at, :]
            for d in (1, 2, 4):
                keep = row >= d
                b = b + a * jnp.where(keep, pltpu.roll(b, d, 0), 0.0)
                a = a * jnp.where(keep, pltpu.roll(a, d, 0), 1.0)
            ap, bp = last[s]
            b = b + a * bp
            a = a * ap
            p[at, :] = a
            h[at, :] = b
            out.append((a[7:8], b[7:8]))
        return tuple(out)

    init = tuple((jnp.ones((1, width), F32), jnp.zeros((1, width), F32)) for _ in range(seqs))
    last = lax.fori_loop(0, length // 8, scan, init)
    for s in range(seqs):
        carry[0, s : s + 1, :] = last[s][0]
        carry[1, s : s + 1, :] = last[s][1]


def front(tok, halo, gain, gw, bw, taps, coff, wr, wi, roff, ioff, sp, seqs, length):
    rows, model = tok.shape
    lru = gw.shape[1]
    bw_, per = wr.shape[-1], 8
    width = per * bw_
    sub = 4 * bw_
    n = lru // width
    col = lambda r: pl.BlockSpec((r, width), lambda j: (0, j))
    blk = pl.BlockSpec((per, bw_, bw_), lambda j: (j, 0, 0))
    f = lambda dt: jax.ShapeDtypeStruct((rows, lru), dt)
    return pl.pallas_call(
        functools.partial(front_kernel, seqs, length),
        grid=(n,),
        in_specs=[
            whole((rows, model)), whole(halo.shape), whole((1, model)),
            pl.BlockSpec((model, width), lambda j: (0, j)), pl.BlockSpec((model, width), lambda j: (0, j)),
            col(4), col(1), blk, blk, col(1), col(1), col(1),
        ],
        out_specs=[
            whole((rows, model)), col(rows), col(rows), col(halo.shape[0]), col(rows), col(rows), col(rows), col(rows), col(rows),
            pl.BlockSpec((2, seqs, width), lambda j: (0, 0, j)),
        ],
        out_shape=[
            jax.ShapeDtypeStruct((rows, model), BF16), f(F32), f(BF16),
            jax.ShapeDtypeStruct((halo.shape[0], lru), BF16), f(BF16), f(F32), f(F32), f(F32), f(F32),
            jax.ShapeDtypeStruct((2, seqs, lru), F32),
        ],
        scratch_shapes=[
            pltpu.VMEM(halo.shape, BF16), pltpu.VMEM((seqs, 8 + length, width), F32),
            pltpu.VMEM((2, sub, sub), BF16), pltpu.VMEM((2, sub, sub), BF16),
            pltpu.VMEM((rows, width), F32), pltpu.VMEM((rows, width), F32),
        ],
        compiler_params=params(),
        name="front",
    )(tok, halo, gain, gw, bw, taps, coff, wr, wi, roff, ioff, sp)


def join_kernel(tok, gate, h, p, entry, ow, gain, joined, resid, normed):
    rows = tok.shape[0]
    ent = entry[0]

    def join(i, _):
        at = pl.ds(pl.multiple_of(i * 16, 16), 16)
        state = h[at, :] + p[at, :] * ent
        joined[at, :] = (gelu(gate[at, :]) * state).astype(BF16)
        return 0

    lax.fori_loop(0, rows // 16, join, 0)
    resid[...] = nn(joined[...], ow[...])

    def norm(i, _):
        at = pl.ds(pl.multiple_of(i * 32, 32), 32)
        y = tok[at, :].astype(F32) + resid[at, :]
        resid[at, :] = y
        r = lax.rsqrt(jnp.mean(y * y, axis=-1, keepdims=True) + 1e-06)
        normed[at, :] = (y * r * gain[...]).astype(BF16)
        return 0

    lax.fori_loop(0, rows // 32, norm, 0)


def join(tok, gate, h, p, entry, ow, gain, seqs, length):
    rows, model = tok.shape
    lru = gate.shape[1]
    tile = 128
    per = length // tile
    row = lambda w: pl.BlockSpec((tile, w), lambda i: (i, 0))
    return pl.pallas_call(
        join_kernel,
        grid=(rows // tile,),
        in_specs=[row(model), row(lru), row(lru), row(lru), pl.BlockSpec((1, 1, lru), lambda i: (i // per, 0, 0)), whole((lru, model)), whole((1, model))],
        out_specs=[row(lru), row(model), row(model)],
        out_shape=[jax.ShapeDtypeStruct((rows, lru), BF16), jax.ShapeDtypeStruct((rows, model), F32), jax.ShapeDtypeStruct((rows, model), BF16)],
        compiler_params=params(),
        name="join",
    )(tok, gate, h, p, entry.reshape(seqs, 1, lru), ow, gain)


def feed_kernel(first, who, *refs):
    if first:
        n2, cot, fg, fu, fd, hid, gg, gu, acc, ug, uv, gh = refs
    else:
        n2, cot, fg, fu, fd, start, hid, gg, gu, acc, ug, uv, gh = refs
    rows = n2.shape[0]
    ug[...] = nn(n2[...], fg[...])
    uv[...] = nn(n2[...], fu[...])
    gh[...] = nt(cot[...], fd[...])

    def body(i, _):
        at = pl.ds(pl.multiple_of(i * 16, 16), 16)
        act, slope = gelu_parts(ug[at, :])
        v, g = uv[at, :], gh[at, :]
        hid[at, :] = (act * v).astype(BF16)
        gg[at, :] = (g * v * slope).astype(BF16)
        gu[at, :] = (g * act).astype(BF16)
        return 0

    lax.fori_loop(0, rows // 16, body, 0)

    @pl.when(pl.program_id(0) == 0)
    def _():
        if first:
            acc[...] = jnp.zeros_like(acc)
        else:
            acc[...] = start[...]

    acc[...] += nt(gg[...], fg[...]) + nt(gu[...], fu[...])


def feed(half, n2, cot, fg, fu, fd, start):
    rows, model = n2.shape
    units = fg.shape[1]
    tile = 512
    n = units // 2 // tile
    first = start is None
    out = lambda: pl.BlockSpec((rows, tile), lambda i, w: (0, i))
    ins = [
        whole((rows, model)), whole((rows, model)),
        pl.BlockSpec((model, tile), lambda i, w: (0, w[0] * n + i)), pl.BlockSpec((model, tile), lambda i, w: (0, w[0] * n + i)),
        pl.BlockSpec((tile, model), lambda i, w: (w[0] * n + i, 0)),
    ]
    args = [n2, cot, fg, fu, fd]
    if not first:
        ins.append(whole((rows, model)))
        args.append(start)
    return pl.pallas_call(
        functools.partial(feed_kernel, first),
        grid_spec=pltpu.PrefetchScalarGridSpec(
            num_scalar_prefetch=1, grid=(n,), in_specs=ins, out_specs=[out(), out(), out(), whole((rows, model))],
            scratch_shapes=[pltpu.VMEM((rows, tile), F32)] * 3,
        ),
        out_shape=[jax.ShapeDtypeStruct((rows, units // 2), BF16)] * 3 + [jax.ShapeDtypeStruct((rows, model), F32)],
        compiler_params=params(),
        name="feed_a" if first else "feed_b",
    )(half, *args)


MESH = pl.DeviceIdType.MESH


def meet(peers):
    barrier = pltpu.get_barrier_semaphore()
    for peer in peers:
        pl.semaphore_signal(barrier, inc=1, device_id=peer, device_id_type=MESH)
    pl.semaphore_wait(barrier, len(peers))


def entry_state(part, n, reverse, collective_id):
    _, seqs, lru = part.shape

    def kernel(mine, out, got, send, recv):
        me, b = lax.axis_index("seq"), lax.axis_index("batch")
        peers = [(lax.rem(me + k, n), b) for k in range(1, n)]
        meet(peers)
        copies = []
        for k in range(1, n):
            copy = pltpu.make_async_remote_copy(
                src_ref=mine, dst_ref=got.at[me], send_sem=send.at[k], recv_sem=recv.at[k],
                device_id=peers[k - 1], device_id_type=MESH,
            )
            copy.start()
            copies.append(copy)
        got[me] = mine[...]
        for copy in copies:
            copy.wait()

        def one(k, state):
            j = n - 1 - k if reverse else k
            before = (j > me) if reverse else (j < me)
            return jnp.where(before, got[j, 0] * state + got[j, 1], state)

        out[...] = lax.fori_loop(0, n, one, jnp.zeros((seqs, lru), F32))

    return pl.pallas_call(
        kernel,
        in_specs=[pl.BlockSpec(memory_space=pltpu.VMEM)],
        out_specs=pl.BlockSpec(memory_space=pltpu.VMEM),
        out_shape=jax.ShapeDtypeStruct((seqs, lru), F32),
        scratch_shapes=[pltpu.VMEM((n, 2, seqs, lru), F32), pltpu.SemaphoreType.DMA((n,)), pltpu.SemaphoreType.DMA((n,))],
        compiler_params=pltpu.CompilerParams(collective_id=collective_id, has_side_effects=True, vmem_limit_bytes=VLIM),
        name="entry_back" if reverse else "entry",
    )(part)


def flip(index, bit):
    return index + bit - 2 * bit * (lax.rem(index // bit, 2))


ORDERS = {"D": ("xlyh", "ylxh"), "E": ("xlhy", "yxlh")}


class Exchange:
    def __init__(self, chunks, part, bufs, fin, send, recv):
        self.chunks, self.part, self.bufs, self.fin, self.sems = chunks, part, bufs, fin, (send, recv)
        seq, bat = lax.axis_index("seq"), lax.axis_index("batch")
        core, y = lax.rem(bat, 2), bat // 2
        x, low, high = lax.rem(seq, 2), lax.rem(seq // 2, 2), seq // 4
        bit = {"x": x, "y": y, "l": low, "h": high}
        move = {"x": (1 - 2 * x, 0), "y": (0, 2 - 4 * y), "l": (2 - 4 * low, 0), "h": (4 - 8 * high, 0)}
        pick = lambda a, b: a if a is b else (1 - core) * a + core * b
        self.core, self.y = core, y
        self.other, self.across = (seq, bat + 1 - 2 * core), (seq, bat + 2 - 4 * y)
        self.bits, self.peers = {}, {}
        for kind, (first, second) in ORDERS.items():
            self.bits[kind] = [pick(bit[a], bit[b]) for a, b in zip(first, second)]
            self.peers[kind] = [
                (seq + pick(move[a][0], move[b][0]), bat + pick(move[a][1], move[b][1])) for a, b in zip(first, second)
            ] + [self.across, self.other]
        self.greet = [(seq + move[a][0], bat) for a in "xlh"] + [self.across, self.other]
        self.freed, self.further = set(), {}

    def at(self, place):
        for k, q in PLAN.get(place, ()):
            self.step(k, q)

    def free(self, q):
        self.copy(0, q).wait_send()
        self.freed.add(q)

    def drain(self):
        self.at("drain")
        for q in range(len(self.chunks)):
            for k in range(4):
                if k > 0 or q not in self.freed:
                    self.copy(k, q).wait_send()

    def copy(self, k, q):
        grad, row, kind = self.chunks[q]
        size, bits = 8 >> k, self.bits[kind]
        if k == 0:
            src, dst = grad.at[pl.ds((1 - bits[0]) * 8, 8), row : row + self.part], self.bufs[0].at[q]
        elif k < 4:
            src, dst = self.bufs[k - 1].at[q, pl.ds((1 - bits[k]) * size, size)], self.bufs[k].at[q]
        elif k == 4:
            src = dst = self.fin.at[q, self.core, self.y]
        else:
            src = dst = self.fin.at[q, self.core]
        return pltpu.make_async_remote_copy(
            src_ref=src, dst_ref=dst, send_sem=self.sems[0].at[k, q], recv_sem=self.sems[1].at[k, q],
            device_id=self.peers[kind][k], device_id_type=MESH,
        )

    def add(self, k, q, base, size):
        grad, row, kind = self.chunks[q]
        dst = self.bufs[k]
        bits = self.bits[kind]
        for j in range(size):

            def body(i, _):
                a = pl.ds(pl.multiple_of(i * 128, 128), 128)
                if k == 0:
                    own = grad[bits[0] * 8 + base + j, pl.ds(pl.multiple_of(row + i * 128, 128), 128), :]
                else:
                    own = self.bufs[k - 1][q, bits[k] * (8 >> k) + base + j, a, :]
                dst[q, base + j, a, :] = dst[q, base + j, a, :] + own
                return 0

            lax.fori_loop(0, self.part // 128, body, 0)

    def step(self, k, q):
        if k > 5:
            self.further[k][q]()
        elif k < 0:
            self.copy(0, q).start()
        elif k < 3:
            half, bits = 4 >> k, self.bits[self.chunks[q][2]]
            self.copy(k, q).wait_recv()
            self.add(k, q, (1 - bits[k + 1]) * half, half)
            self.copy(k + 1, q).start()
            self.add(k, q, bits[k + 1] * half, half)
        elif k == 3:
            bits = self.bits[self.chunks[q][2]]
            self.copy(3, q).wait_recv()

            def body(i, _):
                a = pl.ds(pl.multiple_of(i * 128, 128), 128)
                self.fin[q, self.core, self.y, a, :] = self.bufs[3][q, 0, a, :] + self.bufs[2][q, bits[3], a, :]
                return 0

            lax.fori_loop(0, self.part // 128, body, 0)
            self.copy(4, q).start()
        elif k == 4:
            self.copy(4, q).wait()
            self.copy(5, q).start()
        else:
            self.copy(5, q).wait()

    @staticmethod
    def scratch(chunks, part):
        return [pltpu.VMEM((chunks, 8 >> k, part, 128), BF16) for k in range(4)] + [pltpu.SemaphoreType.DMA((6, chunks))] * 2


class BlockSums:
    def __init__(self, value, bufs, out, send, recv):
        self.value, self.bufs, self.out, self.sems = value, bufs, out, (send, recv)
        seq, bat = lax.axis_index("seq"), lax.axis_index("batch")
        core, y = lax.rem(bat, 2), bat // 2
        x, low, high = lax.rem(seq, 2), lax.rem(seq // 2, 2), seq // 4
        self.bits = [core, low, high, x, y]
        self.peers = [(seq, bat + 1 - 2 * core), (seq + 2 - 4 * low, bat), (seq + 4 - 8 * high, bat), (seq + 1 - 2 * x, bat), (seq, bat + 2 - 4 * y)]
        self.base = [0]
        for k in range(5):
            self.base.append(self.base[-1] + self.bits[k] * (16 >> k))

    def halve(self, k):
        size = 16 >> k
        return pltpu.make_async_remote_copy(
            src_ref=self.value.at[pl.ds(self.base[k] + (1 - self.bits[k]) * size, size)], dst_ref=self.bufs[k],
            send_sem=self.sems[0].at[k], recv_sem=self.sems[1].at[k], device_id=self.peers[k], device_id_type=MESH,
        )

    def hand(self, k):
        at = pl.ds(self.base[k + 1], 16 >> k)
        return pltpu.make_async_remote_copy(
            src_ref=self.out.at[at], dst_ref=self.out.at[at],
            send_sem=self.sems[0].at[5 + k], recv_sem=self.sems[1].at[5 + k], device_id=self.peers[k], device_id_type=MESH,
        )

    def events(self):
        def took(k):
            size = 16 >> k
            self.halve(k).wait()

            def body(j, _):
                at = self.base[k + 1] + j
                total = (self.value[at].astype(F32) + self.bufs[k][j].astype(F32)).astype(BF16)
                if k < 4:
                    self.value[at] = total
                else:
                    self.out[at] = total
                return 0

            lax.fori_loop(0, size, body, 0)
            if k < 4:
                self.halve(k + 1).start()
            else:
                self.hand(4).start()

        def got(k):
            self.hand(k).wait()
            if k > 0:
                self.hand(k - 1).start()

        first = [lambda: self.halve(0).start()]
        return first + [functools.partial(took, k) for k in range(5)] + [functools.partial(got, k) for k in range(4, -1, -1)]

    @staticmethod
    def scratch(width):
        return [pltpu.VMEM((16 >> k, width, 128), BF16) for k in range(5)] + [pltpu.SemaphoreType.DMA((10,))] * 2


def core_of():
    return lax.rem(lax.axis_index("batch"), 2)


def group(core):
    i = pl.program_id(0)
    return (1 - i) * (1 - core) + i * core


def put_pieces(chunks, acc, core, y, first, count):
    part, cols = acc.shape[0] // count, acc.shape[1]
    for j in range(count):
        for t in range(cols // 128):
            ref, row, kind = chunks[t * part // 384]
            at = place_of(core, first + j, y, kind)
            row = row + t * part % 384
            ref[at, row : row + part, :] = acc[j * part : (j + 1) * part, t * 128 : (t + 1) * 128].astype(BF16)


def place_of(core, s, y, kind):
    bit = {"x": s % 2, "l": (s // 2) % 2, "h": s // 4, "y": y}
    place = lambda order: sum(bit[a] * (8 >> k) for k, a in enumerate(order))
    first, second = ORDERS[kind]
    return place(first) if first == second else (1 - core) * place(first) + core * place(second)


def wgrad(core, chunks, lhs, lhs_far, rhs, rhs_far, own_columns):
    rows = lhs.shape[0]
    tile = rhs.shape[1] // (2 if own_columns else 4)
    base = 0 if own_columns else 2 * core

    def body(a, b, c, d):
        put_pieces(chunks, tn(a[...], c[...]) + tn(b[...], d[...]), core, pl.program_id(0), 0, 8)

    left = pl.BlockSpec(lhs.shape, lambda y: (0, 0), pipeline_mode=pl.Buffered(1))
    right = pl.BlockSpec((rows, tile), lambda y: (0, base + y))
    pltpu.emit_pipeline(body, grid=(2,), in_specs=[left, left, right, right])(lhs, lhs_far, rhs, rhs_far)


def wgrad_down(core, chunks, theirs, mine, far_theirs, far_mine, cot, cot_far, between):
    rows, units = mine.shape
    tile = cot.shape[1] // 4
    for a, b, first in ((theirs, far_mine, 4 * (1 - core)), (mine, far_theirs, 4 * core)):

        def body(l, m, c, d):
            put_pieces(chunks, tn(l[...], c[...]) + tn(m[...], d[...]), core, pl.program_id(0), first, 4)

        left = pl.BlockSpec((rows, units), lambda y: (0, 0), pipeline_mode=pl.Buffered(1))
        right = pl.BlockSpec((rows, tile), lambda y: (0, 2 * core + y))
        pltpu.emit_pipeline(body, grid=(2,), in_specs=[left, left, right, right])(a, b, cot, cot_far)
        between()
        between = lambda: None


def norm_back(core, gn, resid, cot, fgain, gres, low, gain_sum):
    rows, model = gn.shape
    tile = 128
    gain_sum[...] = jnp.zeros_like(gain_sum)

    def body(d_ref, y_ref, c_ref, out_ref):
        g = fgain[...]

        def norm(i, total):
            at = pl.ds(pl.multiple_of(i * 16, 16), 16)
            y, d = y_ref[at, :], d_ref[at, :]
            r = lax.rsqrt(jnp.mean(y * y, axis=-1, keepdims=True) + 1e-06)
            dg, yr = d * g, y * r
            dot = jnp.mean(dg * yr, axis=-1, keepdims=True)
            out = c_ref[at, :].astype(F32) + r * (dg - yr * dot)
            out_ref[at, :] = out
            low[pl.ds(pl.multiple_of(pl.program_id(0) * tile + i * 16, 16), 16), :] = out.astype(BF16)
            add = d * yr
            return total + add[0:8] + add[8:16]

        total = lax.fori_loop(0, tile // 16, norm, jnp.zeros((8, model), F32))
        gain_sum[...] += jnp.sum(total, axis=0, keepdims=True)

    row = pl.BlockSpec((tile, model), lambda i: (i, 0))
    pltpu.emit_pipeline(body, grid=(rows // tile,), in_specs=[row, row, row], out_specs=[row])(gn, resid, cot, gres)


def turn(core, seqs, length, low, ow, gate, h, p, entry, rate, sp, ggate, lc, q, carry, gj, begin):
    rows, lru = gate.shape
    width = lru // 2

    def body(ow_ref, gate_ref, h_ref, p_ref, e_ref, rate_ref, sp_ref, gg_ref, lc_ref, q_ref):
        pump = begin()
        for s in range(seqs):
            gj[s, 0:length, :] = nt(low[s * length : (s + 1) * length, :], ow_ref[...])
        pump()
        slope = -8.0 * sp_ref[...]
        for s in range(seqs):
            ent = e_ref[s]

            def act(i, _):
                at = pl.ds(pl.multiple_of(s * length + i * 16, 16), 16)
                here = pl.ds(pl.multiple_of(i * 16, 16), 16)
                value, der = gelu_parts(gate_ref[at, :])
                state = h_ref[at, :] + p_ref[at, :] * ent
                d = gj[s, here, :]
                gg_ref[0, at, :] = (d * state * der).astype(BF16)
                gj[s, here, :] = d * value
                return 0

            lax.fori_loop(0, length // 16, act, 0)
            pump()

        row = lax.broadcasted_iota(jnp.int32, (8, width), 0)
        tiles = length // 8

        def scan(k, last):
            i = tiles - 1 - k
            out = []
            for s in range(seqs):
                at = pl.ds(pl.multiple_of(s * length + i * 8, 8), 8)
                g = gj[s, pl.ds(pl.multiple_of(i * 8, 8), 8), :]
                a = jnp.exp(rate_ref[at, :] * slope)
                b = a * g
                for d in (1, 2, 4):
                    keep = row < 8 - d
                    b = b + a * jnp.where(keep, pltpu.roll(b, 8 - d, 0), 0.0)
                    a = a * jnp.where(keep, pltpu.roll(a, 8 - d, 0), 1.0)
                ap, bp = last[s]
                b = b + a * bp
                a = a * ap
                lc_ref[at, :] = g + jnp.where(row < 7, pltpu.roll(b, 7, 0), bp)
                q_ref[at, :] = jnp.where(row < 7, pltpu.roll(a, 7, 0), ap)
                out.append((a[0:1], b[0:1]))
            return tuple(out)

        init = tuple((jnp.ones((1, width), F32), jnp.zeros((1, width), F32)) for _ in range(seqs))
        last = lax.fori_loop(0, tiles, scan, init)
        for s in range(seqs):
            carry[group(core), 0, s : s + 1, :] = last[s][0]
            carry[group(core), 1, s : s + 1, :] = last[s][1]
        pump()

    grp = lambda i: (1 - i) * (1 - core) + i * core
    col = lambda r: pl.BlockSpec((r, width), lambda i: (0, grp(i)))
    pltpu.emit_pipeline(
        body, grid=(2,),
        in_specs=[
            pl.BlockSpec((width, ow.shape[1]), lambda i: (grp(i), 0)), col(rows), col(rows), col(rows),
            pl.BlockSpec((seqs, 1, width), lambda i: (0, 0, grp(i))), col(rows), col(1),
        ],
        out_specs=[pl.BlockSpec((1, rows, width), lambda i: (i, 0, 0)), col(rows), col(rows)],
    )(ow, gate, h, p, entry, rate, sp, ggate, lc, q)


def gates_back(
    own, core, seqs, length, lc, q, cin, h, p, entry, rate, inlet, mixed, branch, edge, wr, wi, taps, sp, sg,
    gb, head, tail, blocks, rate_sum, inlet_sum, sums_out, dr, di, gr, gi, gm, ext, begin,
):
    rows, lru = lc.shape
    width, bw_ = lru // 2, wr.shape[-1]
    per, sub = width // bw_, dr.shape[-1]

    def body(
        lc_ref, q_ref, h_ref, p_ref, e_ref, rate_ref, inlet_ref, mixed_ref, branch_ref, edge_ref, wr_ref, wi_ref, taps_ref, sp_ref, sg_ref,
        gb_ref,
    ):
        pump = begin()
        mine = group(core)
        slope = -8.0 * sp_ref[...]
        zero = jnp.zeros((8, width), F32)
        row = lax.broadcasted_iota(jnp.int32, (16, width), 0)

        sums = (zero, zero, zero)
        for s in range(seqs):
            c_in, ent = cin[mine, s : s + 1, :], e_ref[s]

            def gates(i, carry):
                (before, t0, t1, t2) = carry
                at = pl.ds(pl.multiple_of(s * length + i * 16, 16), 16)
                state = h_ref[at, :] + p_ref[at, :] * ent
                prev = jnp.where(row > 0, pltpu.roll(state, 1, 0), before)
                carried = lc_ref[at, :] + q_ref[at, :] * c_in
                rt, it, mx = rate_ref[at, :], inlet_ref[at, :], mixed_ref[at, :].astype(F32)
                log_decay = rt * slope
                decay = jnp.exp(log_decay)
                gap = drop(log_decay, decay)
                inv = lax.rsqrt(gap)
                nf = gap * inv
                im = it * mx
                g_log = carried * decay * (prev - im * decay * inv)
                cn = carried * nf
                g_rt = g_log * slope * (rt * (1.0 - rt))
                g_it = cn * im * (1.0 - it)
                gr[at, :] = g_rt.astype(BF16)
                gi[at, :] = g_it.astype(BF16)
                gm[s, pl.ds(pl.multiple_of(i * 16, 16), 16), :] = cn * it
                lr = g_log * rt
                return (state[15:16], t0 + lr[0:8] + lr[8:16], t1 + g_rt[0:8] + g_rt[8:16], t2 + g_it[0:8] + g_it[8:16])

            _, *sums = lax.fori_loop(0, length // 16, gates, (ent, *sums))
            pump()
        down = lambda v: jnp.sum(v, axis=0, keepdims=True)
        lanes = pl.ds(pl.multiple_of(mine * width, 128), width)
        sums_out[4:5, lanes] = down(sums[0]) * (-8.0 * sg_ref[...])
        sums_out[5:6, lanes] = down(sums[1])
        sums_out[6:7, lanes] = down(sums[2])

        for g in range(width // sub):
            cols = slice(g * sub, (g + 1) * sub)
            spread(dr, [wr_ref[g * 4 + a] for a in range(4)], 4, bw_)
            spread(di, [wi_ref[g * 4 + a] for a in range(4)], 4, bw_)
            back = nt(gr[:, cols], dr[...]) + nt(gi[:, cols], di[...])
            rs = tn(mixed_ref[:, cols], gr[:, cols])
            is_ = tn(mixed_ref[:, cols], gi[:, cols])
            for a in range(4):
                block = slice(a * bw_, (a + 1) * bw_)
                if own:
                    blocks[mine * per + g * 4 + a, :, 0:bw_] = rs[block, block].astype(BF16)
                    blocks[2 * per + mine * per + g * 4 + a, :, 0:bw_] = is_[block, block].astype(BF16)
                else:
                    rate_sum[mine * per + g * 4 + a] = rs[block, block]
                    inlet_sum[mine * per + g * 4 + a] = is_[block, block]
            for s in range(seqs):
                gm[s, 0:length, cols] += back[s * length : (s + 1) * length]
        pump()

        for s in range(seqs):
            gm[s, length : length + 8, :] = zero
            ext[s, 0:8, :] = edge_ref[8 * s : 8 * s + 8].astype(F32)
            ext[s, 8 : 8 + length, :] = branch_ref[s * length : (s + 1) * length].astype(F32)
            head[mine, 8 * s : 8 * s + 8, :] = gm[s, 0:8, :]

        tap = [taps_ref[k : k + 1, :] for k in range(4)]
        acc = (zero,) * 5
        for s in range(seqs):

            def conv(i, acc):
                lo = pl.multiple_of(i * 16, 16)
                y = gm[s, pl.ds(lo, 24), :]
                x = ext[s, pl.ds(lo, 24), :]
                total = tap[0] * y[0:16]
                for k in range(1, 4):
                    total = total + tap[k] * y[k : k + 16]
                gb_ref[0, pl.ds(pl.multiple_of(s * length + i * 16, 16), 16), :] = total.astype(BF16)
                now = y[0:16]
                new = []
                for k in range(4):
                    prod = now * x[8 - k : 24 - k]
                    new.append(acc[k] + prod[0:8] + prod[8:16])
                new.append(acc[4] + now[0:8] + now[8:16])
                return tuple(new)

            acc = lax.fori_loop(0, length // 16, conv, acc)
            y = gm[s, length - 16 : length + 8, :]
            total = tap[0] * y[0:16]
            for k in range(1, 4):
                total = total + tap[k] * y[k : k + 16]
            tail[mine, 16 * s : 16 * s + 16, :] = total
            pump()
        for k in range(4):
            sums_out[k : k + 1, lanes] = down(acc[k])
        sums_out[7:8, lanes] = down(acc[4])

    grp = lambda i: (1 - i) * (1 - core) + i * core
    col = lambda r: pl.BlockSpec((r, width), lambda i: (0, grp(i)))
    blk = pl.BlockSpec((per, bw_, bw_), lambda i: (grp(i), 0, 0))
    pltpu.emit_pipeline(
        body, grid=(2,),
        in_specs=[
            col(rows), col(rows), col(rows), col(rows), pl.BlockSpec((seqs, 1, width), lambda i: (0, 0, grp(i))),
            col(rows), col(rows), col(rows), col(rows), col(edge.shape[0]), blk, blk, col(4), col(1), col(1),
        ],
        out_specs=[pl.BlockSpec((1, rows, width), lambda i: (i, 0, 0))],
    )(lc, q, h, p, entry, rate, inlet, mixed, branch, edge, wr, wi, taps, sp, sg, gb)


class Entry:
    def __init__(self, part, got, n, send, recv):
        self.part, self.got, self.n = part, got, n
        self.me = lax.axis_index("seq")
        self.copies = [
            pltpu.make_async_remote_copy(
                src_ref=part, dst_ref=got.at[self.me], send_sem=send.at[k], recv_sem=recv.at[k],
                device_id=(lax.rem(self.me + k, n), lax.axis_index("batch")), device_id_type=MESH,
            )
            for k in range(1, n)
        ]

    def start(self):
        for copy in self.copies:
            copy.start()
        self.got[self.me] = self.part[...]

    def finish(self, out, reverse):
        for copy in self.copies:
            copy.wait()

        def one(k, state):
            j = self.n - 1 - k if reverse else k
            before = (j > self.me) if reverse else (j < self.me)
            return jnp.where(before, self.got[j, :, 0] * state + self.got[j, :, 1], state)

        out[...] = lax.fori_loop(0, self.n, one, jnp.zeros(out.shape, F32))


def spaced(exchange, name, steps):
    def begin():
        place = iter(range(64))

        def pump():
            j = next(place)
            for i in range(steps):
                if PLAN.get(f"{name}{i}{j}"):

                    @pl.when(pl.program_id(0) == i)
                    def _():
                        exchange.at(f"{name}{i}{j}")

        return pump

    return begin


def no_pump():
    return lambda: None


ANY = pl.BlockSpec(memory_space=pl.ANY)
INSIDE = pl.BlockSpec(memory_space=pltpu.VMEM)


KINDS = "DDEDDEDDE"
PLAN = {
    "a0": [(-1, 0), (-1, 1)],
    "a1": [(-1, 2), (-1, 3)],
    "t01": [(0, 0), (-1, 4), (0, 1), (-1, 5)],
    "t12": [(0, 2), (0, 3)],
    "b1": [(1, 0), (-1, 6), (1, 1)],
    "g00": [(1, 2), (1, 3), (0, 4), (0, 5), (2, 0), (2, 1)],
    "g03": [(2, 3)],
    "g11": [(3, 0), (0, 6), (3, 1), (2, 2)],
    "g13": [(4, 0), (3, 3)],
    "g14": [(5, 0), (4, 1)],
    "c1": [(-1, 7), (5, 1), (3, 2), (4, 3), (6, 0)],
    "c2": [(5, 3), (1, 4), (1, 5), (6, 1)],
    "c3": [(4, 2)],
    "c4": [(-1, 8), (5, 2), (2, 4), (1, 6)],
    "i00": [(2, 5), (6, 2)],
    "i10": [(0, 7), (3, 4), (2, 6)],
    "i30": [(4, 4), (3, 5), (6, 3)],
    "o00": [(5, 4), (3, 6), (0, 8), (6, 4), (4, 5), (7, 0)],
    "o10": [(5, 5)],
    "o20": [(4, 6), (6, 5)],
    "o30": [(5, 6), (1, 7), (6, 6), (7, 1)],
    "drain": [(1, 8), (6, 7), (7, 2), (2, 7), (2, 8), (6, 8), (7, 3), (3, 7), (3, 8), (4, 7), (7, 4), (4, 8), (5, 7), (6, 9), (5, 8), (6, 10)],
}


PART = 384


def backward(own, seqs, length, seq_n, batch_n, grads_in, values, collective_id):
    (
        gn, resid, cot, fgain, ow, gate, h, p, entry, rate, sp, inlet, mixed, branch, edge, wr, wi, taps, sg, gw, bw, tok, mgain, ht, hm, fd
    ) = values
    rows, model = gn.shape
    lru, units = gate.shape[1], fd.shape[0]
    width, bw_ = lru // 2, wr.shape[-1]
    per, sub = width // bw_, 4 * bw_
    steps = [("batch", 1 << k) for k in range(batch_n.bit_length() - 1)] + [("seq", 1 << k) for k in range(seq_n.bit_length() - 1)]
    n_steps = len(steps)
    if not own:
        grads_in = []

    def kernel(*refs):
        refs = list(refs)
        cut = lambda n: [refs.pop(0) for _ in range(n)]
        far_in = cut(len(grads_in))
        (
            gn, resid, cot, fgain, ow, gate, h, p, entry, rate, sp, inlet, mixed, branch, edge, wr, wi, taps, sg, gw, bw, tok, mgain, ht, hm, fd
        ) = cut(26)
        tokens_grad, block_out, totals, gres, low_out, low_far, ggate, ggate_far, lc, q, gb, gb_far = cut(12)
        fin, block_total = cut(2) if own else (None, None)
        rate_sum, inlet_sum = (None, None) if own else cut(2)
        low, carry, got, cin, dr, di, gr, gi, gm, ext, head, tail, ahead, fixed, gain_sum, acc, small = cut(17)
        send, recv, swap_send, swap_recv, one, local, s_send, s_recv = cut(8)

        core = core_of()
        seq, bat = lax.axis_index("seq"), lax.axis_index("batch")
        other = (seq, bat + 1 - 2 * core)
        peers = [(flip(seq, bit), bat) if axis == "seq" else (seq, flip(bat, bit)) for axis, bit in steps]
        exchange, blocks = None, None
        if own:
            g0, g1, g2, *bufs, x_send, x_recv = cut(9)
            blocks, *block_bufs, b_send, b_recv = cut(8)
            places = [(g0, 0), (g0, PART), (g1, 0), (g1, PART), (g2, 0), (g2, PART), (g0, 0), (g0, PART), (g1, 0)]
            chunks = [(ref, row, kind) for (ref, row), kind in zip(places, KINDS)]
            exchange = Exchange(chunks, PART, bufs, fin, x_send, x_recv)
            exchange.further[6] = BlockSums(blocks, block_bufs, block_total, b_send, b_recv).events()
            blocks[...] = jnp.zeros_like(blocks)
        small[0] = jnp.zeros((16, lru), F32)
        greet = [(lax.rem(seq + k, seq_n), bat) for k in range(1, seq_n)] + [peer for peer, step in zip(peers, steps) if step[0] == "batch"]
        meet(greet)

        def swap(j, src, dst):
            return pltpu.make_async_remote_copy(
                src_ref=src, dst_ref=dst, send_sem=swap_send.at[j], recv_sem=swap_recv.at[j], device_id=other, device_id_type=MESH
            )

        at = exchange.at if own else (lambda place: None)
        if own:
            n2, n2_far, gg, gg_far, gu, gu_far, ht_far, hm_far, cot_far, joined, joined_far, normed, normed_far = far_in
            wgrad(core, chunks[0:2], n2, n2_far, gg, gg_far, True)
            at("a0")
            wgrad(core, chunks[2:4], n2, n2_far, gu, gu_far, True)
            at("a1")
            wgrad_down(core, chunks[4:6], ht, hm, ht_far, hm_far, cot, cot_far, lambda: at("a2"))
            at("a3")
        norm_back(core, gn, resid, cot, fgain, gres, low, gain_sum)
        at("a4")
        keep = pltpu.make_async_copy(low, low_out, one)
        keep.start()
        low_swap = swap(0, low, low_far)
        low_swap.start()
        turn(
            core, seqs, length, low, ow, gate, h, p, entry, rate, sp, ggate, lc, q, carry, gm,
            spaced(exchange, "t", 2) if own else no_pump,
        )
        gate_swap = swap(1, ggate.at[0], ggate_far)
        gate_swap.start()
        arriving = Entry(carry, got, seq_n, send, recv)
        arriving.start()
        keep.wait()
        low_swap.wait()
        if own:
            at("b0")
            exchange.free(0)
            wgrad(core, chunks[6:7], joined, joined_far, low_out, low_far, False)
            at("b1")
        arriving.finish(cin, True)
        gate_swap.wait()
        at("b2")
        gates_back(
            own, core, seqs, length, lc, q, cin, h, p, entry, rate, inlet, mixed, branch, edge, wr, wi, taps, sp, sg,
            gb, head, tail, blocks, rate_sum, inlet_sum, small.at[0], dr, di, gr, gi, gm, ext,
            spaced(exchange, "g", 2) if own else no_pump,
        )

        to_left = pltpu.make_async_remote_copy(
            src_ref=head, dst_ref=ahead, send_sem=swap_send.at[2], recv_sem=swap_recv.at[2],
            device_id=(lax.rem(seq + seq_n - 1, seq_n), bat), device_id_type=MESH,
        )
        to_left.start()
        if own:
            at("c0")
            exchange.free(1)
            wgrad(core, chunks[7:8], normed, normed_far, ggate.at[1], ggate_far, True)
            at("c1")
        to_left.wait()
        weight = (seq < seq_n - 1).astype(F32)
        copies = []
        for i in range(2):
            mine = (1 - i) * (1 - core) + i * core
            for s in range(seqs):
                y = ahead[mine, 8 * s : 8 * s + 8, :] * weight
                t = tail[mine, 16 * s : 16 * s + 16, :]
                grown = jnp.concatenate([jnp.zeros((16, width), F32), y], axis=0)
                for k in range(1, 4):
                    t = t + taps[k : k + 1, pl.ds(pl.multiple_of(mine * width, 128), width)] * grown[k : k + 16]
                fixed[i, 16 * s : 16 * s + 16, :] = t.astype(BF16)
                copy = pltpu.make_async_copy(
                    fixed.at[i, 16 * s : 16 * s + 16], gb.at[i, (s + 1) * length - 16 : (s + 1) * length], local.at[i, s]
                )
                copy.start()
                copies.append(copy)
        for copy in copies:
            copy.wait()
        branch_swap = swap(3, gb.at[0], gb_far)
        branch_swap.start()
        at("c2")
        branch_swap.wait()
        at("c3")
        if own:
            exchange.free(2)
            wgrad(core, chunks[8:9], normed, normed_far, gb.at[1], gb_far, True)
            at("c4")

        begin = spaced(exchange, "i", 4) if own else no_pump
        tile = 128
        acc[...] = jnp.zeros_like(acc)

        def input_grad(gg_ref, gb_ref, gwt, gwm, bwt, bwm, x_ref, gr_ref, out):
            pump = begin()
            d = nt(gg_ref[0], gwt[...]) + nt(gg_ref[1], gwm[...]) + nt(gb_ref[0], bwt[...]) + nt(gb_ref[1], bwm[...])
            x = x_ref[...].astype(F32)
            r = lax.rsqrt(jnp.mean(x * x, axis=-1, keepdims=True) + 1e-06)
            xr, dg = x * r, d * mgain[...]
            out[...] = gr_ref[...] + r * (dg - xr * jnp.mean(dg * xr, axis=-1, keepdims=True))
            acc[...] += jnp.sum(d * xr, axis=0, keepdims=True)
            pump()

        row = pl.BlockSpec((tile, model), lambda i: (i, 0))
        pair = pl.BlockSpec((2, tile, width), lambda i: (0, i, 0))
        side = lambda c: pl.BlockSpec((model, width), lambda i: (0, c), pipeline_mode=pl.Buffered(1))
        pltpu.emit_pipeline(
            input_grad, grid=(rows // tile,), in_specs=[pair, pair, side(1 - core), side(core), side(1 - core), side(core), row, row], out_specs=[row]
        )(ggate, gb, gw, gw, bw, bw, tok, gres, tokens_grad)

        small[0, 8:9, 0:model] = acc[...]
        small[0, 9:10, 0:model] = gain_sum[...]

        def small_step(k):
            return pltpu.make_async_remote_copy(
                src_ref=small.at[0], dst_ref=small.at[k + 1], send_sem=s_send.at[k], recv_sem=s_recv.at[k],
                device_id=peers[k], device_id_type=MESH,
            )

        def small_event(k):
            small_step(k).wait()
            small[0] = small[0] + small[k + 1]
            if k + 1 < n_steps:
                small_step(k + 1).start()

        small_events = [functools.partial(small_event, k) for k in range(n_steps)]
        small_step(0).start()
        if own:
            exchange.further[7] = small_events
        begin_out = spaced(exchange, "o", 4) if own else no_pump
        tile_out = 256

        def last(r, ha, hb, fa, fb, out):
            pump = begin_out()
            out[...] = (r[...] + nn(ha[...], fa[...]) + nn(hb[...], fb[...])).astype(BF16)
            pump()

        col = pl.BlockSpec((rows, tile_out), lambda i: (0, i))
        hid = pl.BlockSpec((rows, units // 2), lambda i: (0, 0), pipeline_mode=pl.Buffered(1))
        down = lambda c: pl.BlockSpec((units // 2, tile_out), lambda i: (c, i))
        pltpu.emit_pipeline(last, grid=(model // tile_out,), in_specs=[col, hid, hid, down(1 - core), down(core)], out_specs=[col])(
            resid, ht, hm, fd, fd, block_out
        )
        if own:
            exchange.drain()
        else:
            for event in small_events:
                event()
        totals[...] = small[0]

    f = lambda *shape: jax.ShapeDtypeStruct(shape, F32)
    b = lambda *shape: jax.ShapeDtypeStruct(shape, BF16)
    vm, dma = pltpu.VMEM, lambda *shape: pltpu.SemaphoreType.DMA(shape)
    out_shape = [
        f(rows, model), b(rows, model), f(16, lru),
        f(rows, model), b(rows, model), b(rows, model), b(2, rows, width), b(rows, width), f(rows, lru), f(rows, lru), b(2, rows, width), b(rows, width),
    ]
    out_specs = [ANY, ANY, INSIDE] + [ANY] * 9
    scratch = [
        vm((rows, model), BF16), vm((2, 2, seqs, width), F32), vm((seq_n, 2, 2, seqs, width), F32), vm((2, seqs, width), F32),
        vm((sub, sub), BF16), vm((sub, sub), BF16), vm((rows, width), BF16), vm((rows, width), BF16),
        vm((seqs, length + 8, width), F32), vm((seqs, length + 8, width), F32), vm((2, 8 * seqs, width), F32), vm((2, 16 * seqs, width), F32),
        vm((2, 8 * seqs, width), F32), vm((2, 16 * seqs, width), BF16), vm((1, model), F32), vm((1, model), F32), vm((n_steps + 1, 16, lru), F32),
        dma(seq_n), dma(seq_n), dma(4), dma(4), pltpu.SemaphoreType.DMA, dma(2, seqs), dma(n_steps), dma(n_steps),
    ]
    if own:
        out_shape += [b(9, 2, 2, PART, 128), b(4 * per, bw_, 128)]
        out_specs += [INSIDE, INSIDE]
        scratch += [vm((16, 2 * PART, 128), BF16)] * 3 + Exchange.scratch(9, PART)
        scratch += [vm((4 * per, bw_, 128), BF16)] + BlockSums.scratch(bw_)
    else:
        out_shape += [f(*wr.shape), f(*wi.shape)]
        out_specs += [INSIDE, INSIDE]
    ins = [ANY] * (len(grads_in) + len(values))
    for j in (3, 17, 22):
        ins[len(grads_in) + j] = INSIDE
    return pl.pallas_call(
        kernel,
        in_specs=ins,
        out_specs=out_specs,
        out_shape=out_shape,
        scratch_shapes=scratch,
        compiler_params=pltpu.CompilerParams(collective_id=collective_id, has_side_effects=True, vmem_limit_bytes=60 * 2**20),
        name="backward",
    )(*grads_in, *values)


def lay(sums, model, lru, units, n):
    shapes = [(model // n, units), (model // n, units), (units // n, model), (lru // n, model), (model // n, lru), (model // n, lru)]

    def kernel(v, *outs):
        first = 0
        for out in outs:
            part, wide = out.shape
            for t in range(wide // 128):
                at = t * part
                out[:, t * 128 : (t + 1) * 128] = v[first + at // PART, 0, 0, at % PART : at % PART + part, :].astype(F32)
            first += part * wide // 128 // PART

    return pl.pallas_call(
        kernel,
        grid=(4,),
        in_specs=[pl.BlockSpec((9, 1, 1, PART, 128), lambda i: (0, i // 2, i % 2, 0, 0))],
        out_specs=[pl.BlockSpec((part, wide // 4), lambda i: (0, i)) for part, wide in shapes],
        out_shape=[jax.ShapeDtypeStruct(shape, F32) for shape in shapes],
        compiler_params=params(),
        name="lay",
    )(sums)


def shifted(value, axis, steps):
    count = lax.axis_size(axis)
    return lax.ppermute(value, axis, [(i, i + steps) for i in range(count) if 0 <= i + steps < count])


def swap(value):
    count = lax.axis_size("batch")
    return lax.ppermute(value, "batch", [(i, i ^ 1) for i in range(count)])


def local(
    tokens, cotangent, gate_weight, branch_weight, out_weight, conv_taps, conv_offset, rate_weight, inlet_weight,
    rate_offset, inlet_offset, decay_param, mixer_gain, feed_gain, feed_gate, feed_up, feed_down,
):
    seqs, length, model = tokens.shape
    lru, units = gate_weight.shape[1], feed_gate.shape[1]
    rows = seqs * length
    seq_n, batch_n = lax.axis_size("seq"), lax.axis_size("batch")
    core = lax.rem(lax.axis_index("batch"), 2)
    half = jnp.full((1,), core, jnp.int32)

    halo = shifted(tokens[:, length - 8 :, :], "seq", 1).reshape(8 * seqs, model)
    tok, cot = tokens.reshape(rows, model), cotangent.reshape(rows, model)
    cot_far = swap(cot)
    soft, sgm = jax.nn.softplus(decay_param)[None], jax.nn.sigmoid(decay_param)[None]
    gain1, gain2 = mixer_gain[None], feed_gain[None]

    normed, gate, branch, edge, mixed, rate, inlet, h, p, carry = front(
        tok, halo, gain1, gate_weight, branch_weight, conv_taps, conv_offset[None], rate_weight, inlet_weight,
        rate_offset[None], inlet_offset[None], soft, seqs, length,
    )
    normed_far = swap(normed)
    entry = entry_state(carry, seq_n, False, 0)
    joined, resid, normed_two = join(tok, gate, h, p, entry, out_weight, gain2, seqs, length)
    joined_far, normed_two_far = swap(joined), swap(normed_two)
    hid_t, gg_t, gu_t, acc = feed(1 - half, normed_two, cot, feed_gate, feed_up, feed_down, None)
    hid_t_far, gg_far, gu_far = swap(hid_t), swap(gg_t), swap(gu_t)
    hid_m, gg_m, gu_m, grad_two = feed(half, normed_two, cot, feed_gate, feed_up, feed_down, acc)
    hid_m_far = swap(hid_m)

    own = (seq_n, batch_n) == (8, 4)
    grads_in = [normed_two, normed_two_far, gg_m, gg_far, gu_m, gu_far, hid_t_far, hid_m_far, cot_far, joined, joined_far, normed, normed_far]
    tokens_grad, out, totals, _, grad_low, _, ggate, _, _, _, gb, _, *sums = backward(
        own, seqs, length, seq_n, batch_n, grads_in,
        [
            grad_two, resid, cot, gain2, out_weight, gate, h, p, entry.reshape(seqs, 1, lru), rate, soft, inlet, mixed, branch, edge,
            rate_weight, inlet_weight, conv_taps, sgm, gate_weight, branch_weight, tok, gain1, hid_t, hid_m, feed_down,
        ],
        1,
    )
    if own:
        gate_feed_all, up_feed_all, down_all, out_all, gate_all, branch_all = lay(sums[0], model, lru, units, seq_n)
        count, wide = rate_weight.shape[0], rate_weight.shape[2]
        rate_all, inlet_all = sums[1][:count, :, :wide].astype(F32), sums[1][count:, :, :wide].astype(F32)
    else:
        rate_all, inlet_all = lax.psum((sums[0], sums[1]), ("seq", "batch"))

        def full(theirs, mine):
            a, b = jnp.where(core == 0, mine, theirs), jnp.where(core == 0, theirs, mine)
            return jnp.concatenate([a, b], axis=1)

        def total(left, right):
            return lax.psum(lax.psum_scatter(tn(left, right), "seq", scatter_dimension=0, tiled=True), "batch")

        down_all = total(full(hid_t, hid_m), cot)
        gate_feed_all = total(normed_two, full(gg_t, gg_m))
        up_feed_all = total(normed_two, full(gu_t, gu_m))
        out_all = total(joined, grad_low)
        gate_all = total(normed, full(ggate[0], ggate[1]))
        branch_all = total(normed, full(gb[0], gb[1]))

    return (
        out.reshape(seqs, length, model), tokens_grad.reshape(seqs, length, model), gate_all, branch_all, out_all,
        totals[0:4], totals[7], rate_all, inlet_all, totals[5], totals[6], totals[4], totals[8, :model], totals[9, :model],
        gate_feed_all, up_feed_all, down_all,
    )


def solution(mesh):
    big = P("batch", "seq", None)
    in_specs = (big, big) + (P(),) * 15
    out_specs = (big, big) + (P("seq", None),) * 3 + (P(),) * 9 + (P("seq", None),) * 3
    return jax.shard_map(local, mesh=mesh, in_specs=in_specs, out_specs=out_specs, check_vma=False)
```

time: 489 us -> 323 us (0.66)
  Pallas kernels: 419 us -> 287 us
  local copies, waits for them, and re-layouts: 32.1 us -> 16 us
  between operations: 14.3 us -> 0.77 us
  starting transfers between devices: 11.4 us -> 6.23 us
    pallas_call x14 -> x2, Pallas kernels: 327 us -> 204 us  [the longest x1 198 us: backward(): pl.pallas_call(kernel, in_specs=ins, out_specs=out_specs, out_shape=out_s...]
    pallas_call x2 -> x1, Pallas kernels: 19.3 us -> 9.92 us  [entry_state(): pl.pallas_call(kernel, in_specs=[pl.BlockSpec(memory_space=pltpu.VMEM)],...]
    convert_element_type x8 -> x0, local copies, waits for them, and re-layouts: 6.64 us -> none  [laid(): sums.reshape(2, 2, t, part, 128).transpose(3, 0, 1, 2, 4)]
    unnamed x34 -> x22, local copies, waits for them, and re-layouts: 9.85 us -> 4.35 us
  transfers between devices with their start and end apart: 14 -> 9, of which waited for: 3 -> 3; matrix products, arithmetic and copies ran while one was open for 6% -> 2% of each run, Pallas kernels for 64% -> 26%
where the time goes in v2:
time: 323 us; the launch traced here: 319 us
  Pallas kernels  287 us (89%)
  local copies, waits for them, and re-layouts  16 us (5%)
  waiting for transfers between devices  6.61 us (2%)
  starting transfers between devices  6.23 us (2%)
    pallas_call x1, Pallas kernels, backward(): pl.pallas_call(kernel, in_specs=ins, out_specs=out_specs, out_shape=out_s...  198 us
    pallas_call x2, Pallas kernels, feed(): pl.pallas_call(functools.partial(feed_kernel, first), grid_spec=pltpu.Pre...  34.2 us
    pallas_call x1, Pallas kernels, front(): pl.pallas_call(functools.partial(front_kernel, seqs, length), grid=(n,),...  27.9 us
    pallas_call x1, Pallas kernels, join(): pl.pallas_call(join_kernel, grid=(rows // tile,), in_specs=[row(model), r...  10.8 us
    pallas_call x1, Pallas kernels, entry_state(): pl.pallas_call(kernel, in_specs=[pl.BlockSpec(memory_space=pltpu.VMEM)],...  9.92 us
    ppermute x8, waiting for transfers between devices, swap(): return lax.ppermute(value, 'batch', [(i, i ^ 1) for i in range(count)])  6.61 us
  transfers between devices with their start and end apart: 9, of which 3 were waited for; matrix products, arithmetic and copies ran while one was open for 2% of the time, Pallas kernels for 26%

profile of v2, /device:TPU:13, one launch (start us, length us, event | category | flops | bytes accessed | tf_op | source)
XLA Modules:
  0.0 319.4 jit_solution(15591716949543711552)
XLA Ops:
  0.7 0.8 slice.30
  1.4 3.1 collective-permute-start
  4.5 1.0 collective-permute-start.6
  5.6 0.7 add_divide_fusion
  6.3 1.3 broadcast_in_dim.25.coff
  7.6 1.3 broadcast_in_dim.26.roff
  8.9 1.3 broadcast_in_dim.27.ioff
  11.4 27.9 %front.1 = (bf16[512,1024]{1,0:T(8,128)(2,1)}, f32[512,1536]{1,0:T(8,128)}, bf16[512,1536]{1,0:T(8,128)(2,1)}, bf16[16,1536]{1,0:T(8,128)(2,1)}, bf16[512,1536]{...) custom-call(bf16[512,1024]{1,0:T(8,128)(2,1)} %bitcast.10, ...), custom_call_target="tpu_custom_call" | custom-call | tf_op jit(solution)/shard_map/front/pallas_call | solution.py:174
  39.2 9.9 %entry.1 = f32[2,1536]{1,0:T(2,128)} custom-call(f32[2,2,1536]{2,1,0:T(2,128)} %get-tuple-element.52.mine), custom_call_target="tpu_custom_call" | custom-call | tf_op jit(solution)/shard_map/entry/pallas_call | solution.py:337
  49.2 1.3 reshape.55.entry.refs_21_
  51.0 10.8 %join.1 = (bf16[512,1536]{1,0:T(8,128)(2,1)}, f32[512,1024]{1,0:T(8,128)}, bf16[512,1024]{1,0:T(8,128)(2,1)}) custom-call(bf16[512,1024]{1,0:T(8,128)(2,1)} %bitcast.11, f32[512,1536]{1,0:T(8,128)} %get-tuple-element.49.gate.refs_18_, f32[512,1536]{1,0:T(8,128)} %get-tuple-element.50.h.refs_19_, f32[512,1536]{1,0:T(8,128)} %get-tuple-element.51.p.refs_20_, ...), custom_call_target="tpu_custom_call" | custom-call | tf_op jit(solution)/shard_map/join/pallas_call | solution.py:231
  62.3 16.7 %feed_a.1 = (bf16[512,1536]{1,0:T(8,128)(2,1)}, bf16[512,1536]{1,0:T(8,128)(2,1)}, bf16[512,1536]{1,0:T(8,128)(2,1)}, f32[512,1024]{1,0:T(8,128)}) custom-call(s32[1]{0:T(128)S(6)} %sub.3.who, bf16[512,1024]{1,0:T(8,128)(2,1)} %get-tuple-element.53.refs_0_, bf16[512,1024]{1,0:T(8,128)(2,1)} %bitcast.14, bf16[1024,3072]{1,0:T(8,128)(2,1)} %refs_2_.3, ...), custom_call_target="tpu_custom_call" | custom-call | tf_op jit(solution)/shard_map/feed_a/pallas_call | solution.py:289
  79.1 17.5 %feed_b.1 = (bf16[512,1536]{1,0:T(8,128)(2,1)}, bf16[512,1536]{1,0:T(8,128)(2,1)}, bf16[512,1536]{1,0:T(8,128)(2,1)}, f32[512,1024]{1,0:T(8,128)}) custom-call(s32[1]{0:T(128)} %bitcast.4.who, bf16[512,1024]{1,0:T(8,128)(2,1)} %get-tuple-element.53.refs_0_, bf16[512,1024]{1,0:T(8,128)(2,1)} %bitcast.15, bf16[1024,3072]{1,0:T(8,128)(2,1)} %refs_2_.3, ...), custom_call_target="tpu_custom_call" | custom-call | tf_op jit(solution)/shard_map/feed_b/pallas_call | solution.py:289
  98.3 1.9 collective-permute-done.3.refs_5_
  100.2 4.5 %collective-permute-done.4.refs_6_ = bf16[512,1536]{1,0:T(8,128)(2,1)S(1)} collective-permute-done((bf16[512,1536]{1,0:T(8,128)(2,1)S(1)}, bf16[512,1536]{1,0:T(8,128)(2,1)S(1)}, u32[]{:S(2)}, u32[]{:S(2)}) %collective-permute-start.4) | collective-permute-done | bytes 1572896 | tf_op jit(solution)/shard_map/ppermute | solution.py:1125
  104.9 1.0 copy-done.5
  106.3 198.4 %backward.1 = (f32[512,1024]{1,0:T(8,128)}, bf16[512,1024]{1,0:T(8,128)(2,1)}, f32[16,1536]{1,0:T(8,128)}, f32[512,1024]{1,0:T(8,128)}, bf16[512,1024]{1,0:T(8,1...) custom-call(bf16[512,1024]{1,0:T(8,128)(2,1)} %get-tuple-element.53., ...), custom_call_target="tpu_custom_call" | custom-call | tf_op jit(solution)/shard_map/backward/pallas_call | solution.py:1084
  304.7 1.4 fusion
  306.1 1.4 slice.31
  307.5 1.6 slice_reduce_fusion
  309.1 2.4 slice_convert_fusion
  311.6 5.5 %lay.1 = (f32[128,3072]{1,0:T(8,128)}, f32[128,3072]{1,0:T(8,128)}, f32[384,1024]{1,0:T(8,128)}, f32[192,1024]{1,0:T(8,128)}, f32[128,1536]{1,0:T(8,128)}, /*index=5*/f32[128,1536]{1,0:T(8,128)}) custom-call(bf16[9,2,2,384,128]{4,3,2,1,0:T(8,128)(2,1)} %get-tuple-element.72.v), custom_call_target="tpu_custom_call" | custom-call | tf_op jit(solution)/shard_map/lay/pallas_call | solution.py:1107
  317.1 1.0 copy.36
  318.1 1.3 copy.37
  (35 shorter events, 4.6 us)
Async XLA Ops:
  1.4 9.3 %collective-permute-start = (bf16[2,8,1024]{2,1,0:T(8,128)(2,1)S(1)}, bf16[2,8,1024]{2,1,0:T(8,128)(2,1)S(1)}, u32[]{:S(2)}, u32[]{:S(2)}) collective-permute-start(bf16[2,8,1024]{2,1,0:T(8,128)(2,1)S(1)} %slice.30), channel_id=1, source_target_pairs={{0,4},{4,8},{8,12},{12,16},{16,20},{20,24},{24,28},{1,5},{5,9},{9,... | collective-permute-start | bytes 98312 | tf_op jit(solution)/shard_map/ppermute | solution.py:1120
  4.5 92.1 %collective-permute-start.6 = (bf16[512,1024]{1,0:T(8,128)(2,1)}, bf16[512,1024]{1,0:T(8,128)(2,1)}, u32[]{:S(2)}, u32[]{:S(2)}) collective-permute-start(bf16[512,1024]{1,0:T(8,128)(2,1)} %bitcast.13), channel_id=1, source_target_pairs={{0,1},{1,0},{2,3},{3,2},{4,5},{5,4},{6,7},{7,6},{8,9},{9,8},{10,11... | collective-permute-start | bytes 3145736 | tf_op jit(solution)/shard_map/ppermute | solution.py:1125
  10.8 0.6 copy-start.8
  50.5 46.7 %collective-permute-start.8 = (bf16[512,1024]{1,0:T(8,128)(2,1)}, bf16[512,1024]{1,0:T(8,128)(2,1)}, u32[]{:S(2)}, u32[]{:S(2)}) collective-permute-start(bf16[512,1024]{1,0:T(8,128)(2,1)} %get-tuple-element.62.refs_11_), channel_id=1, source_target_pairs={{0,1},{1,0},{2,3},{3,2},{4,5},{5,4},{6,7},{7,6},{8,9},{9,8},{10,11... | collective-permute-start | bytes 3145736 | tf_op jit(solution)/shard_map/ppermute | solution.py:1125
  61.8 35.5 %collective-permute-start.1 = (bf16[512,1024]{1,0:T(8,128)(2,1)}, bf16[512,1024]{1,0:T(8,128)(2,1)}, u32[]{:S(2)}, u32[]{:S(2)}) collective-permute-start(bf16[512,1024]{1,0:T(8,128)(2,1)} %get-tuple-element.53.refs_0_), channel_id=1, source_target_pairs={{0,1},{1,0},{2,3},{3,2},{4,5},{5,4},{6,7},{7,6},{8,9},{9,8},{10,11... | collective-permute-start | bytes 3145736 | tf_op jit(solution)/shard_map/ppermute | solution.py:1125
  61.8 36.4 %collective-permute-start.7 = (bf16[512,1536]{1,0:T(8,128)(2,1)}, bf16[512,1536]{1,0:T(8,128)(2,1)S(1)}, u32[]{:S(2)}, u32[]{:S(2)}) collective-permute-start(bf16[512,1536]{1,0:T(8,128)(2,1)} %get-tuple-element.61.refs_9_), channel_id=1, source_target_pairs={{0,1},{1,0},{2,3},{3,2},{4,5},{5,4},{6,7},{7,6},{8,9},{9,8},{10,11... | collective-permute-start | bytes 4718600 | tf_op jit(solution)/shard_map/ppermute | solution.py:1125
  79.0 19.3 %collective-permute-start.2 = (bf16[512,1536]{1,0:T(8,128)(2,1)}, bf16[512,1536]{1,0:T(8,128)(2,1)S(1)}, u32[]{:S(2)}, u32[]{:S(2)}) collective-permute-start(bf16[512,1536]{1,0:T(8,128)(2,1)} %get-tuple-element.56), channel_id=1, source_target_pairs={{0,1},{1,0},{2,3},{3,2},{4,5},{5,4},{6,7},{7,6},{8,9},{9,8},{10,11... | collective-permute-start | bytes 4718600 | tf_op jit(solution)/shard_map/ppermute | solution.py:1125
  79.1 17.5 %copy-start.9 = (bf16[512,1536]{1,0:T(8,128)(2,1)S(1)}, bf16[512,1536]{1,0:T(8,128)(2,1)}, u32[]{:S(2)}) copy-start(bf16[512,1536]{1,0:T(8,128)(2,1)} %get-tuple-element.58) | copy-start | bytes 4718596
  79.1 18.0 %copy-start.2 = (bf16[512,1536]{1,0:T(8,128)(2,1)S(1)}, bf16[512,1536]{1,0:T(8,128)(2,1)}, u32[]{:S(2)}) copy-start(bf16[512,1536]{1,0:T(8,128)(2,1)} %get-tuple-element.59.refs_36_) | copy-start | bytes 4718596
  96.6 3.6 %collective-permute-start.3 = (bf16[512,1536]{1,0:T(8,128)(2,1)S(1)}, bf16[512,1536]{1,0:T(8,128)(2,1)S(1)}, u32[]{:S(2)}, u32[]{:S(2)}) collective-permute-start(bf16[512,1536]{1,0:T(8,128)(2,1)S(1)} %copy-done.9), channel_id=1, source_target_pairs={{0,1},{1,0},{2,3},{3,2},{4,5},{5,4},{6,7},{7,6},{8,9},{9,8},{10,11... | collective-permute-start | bytes 4718600 | tf_op jit(solution)/shard_map/ppermute | solution.py:1125
  97.2 7.5 %collective-permute-start.4 = (bf16[512,1536]{1,0:T(8,128)(2,1)S(1)}, bf16[512,1536]{1,0:T(8,128)(2,1)S(1)}, u32[]{:S(2)}, u32[]{:S(2)}) collective-permute-start(bf16[512,1536]{1,0:T(8,128)(2,1)S(1)} %copy-done.2), channel_id=1, source_target_pairs={{0,1},{1,0},{2,3},{3,2},{4,5},{5,4},{6,7},{7,6},{8,9},{9,8},{10,11... | collective-permute-start | bytes 4718600 | tf_op jit(solution)/shard_map/ppermute | solution.py:1125
  97.2 7.6 %collective-permute-start.5 = (bf16[512,1536]{1,0:T(8,128)(2,1)}, bf16[512,1536]{1,0:T(8,128)(2,1)S(1)}, u32[]{:S(2)}, u32[]{:S(2)}) collective-permute-start(bf16[512,1536]{1,0:T(8,128)(2,1)} %get-tuple-element.60.refs_37_), channel_id=1, source_target_pairs={{0,1},{1,0},{2,3},{3,2},{4,5},{5,4},{6,7},{7,6},{8,9},{9,8},{10,11... | collective-permute-start | bytes 4718600 | tf_op jit(solution)/shard_map/ppermute | solution.py:1125
  98.3 8.0 %copy-start.1 = (bf16[512,1536]{1,0:T(8,128)(2,1)}, bf16[512,1536]{1,0:T(8,128)(2,1)S(1)}, u32[]{:S(2)}) copy-start(bf16[512,1536]{1,0:T(8,128)(2,1)S(1)} %collective-permute-done.7.refs_10_) | copy-start | bytes 4718596
  98.3 6.4 %copy-start.3 = (bf16[512,1536]{1,0:T(8,128)(2,1)}, bf16[512,1536]{1,0:T(8,128)(2,1)S(1)}, u32[]{:S(2)}) copy-start(bf16[512,1536]{1,0:T(8,128)(2,1)S(1)} %collective-permute-done.2.refs_3_) | copy-start | bytes 4718596
  100.2 4.7 %copy-start.4 = (bf16[512,1536]{1,0:T(8,128)(2,1)}, bf16[512,1536]{1,0:T(8,128)(2,1)S(1)}, u32[]{:S(2)}) copy-start(bf16[512,1536]{1,0:T(8,128)(2,1)S(1)} %collective-permute-done.3.refs_5_) | copy-start | bytes 4718596
  104.7 1.2 copy-start.5
  104.9 1.4 copy-start.6
  311.6 5.5 %copy-start.7 = (bf16[512,1024]{1,0:T(8,128)(2,1)S(1)}, bf16[512,1024]{1,0:T(8,128)(2,1)}, u32[]{:S(2)}) copy-start(bf16[512,1024]{1,0:T(8,128)(2,1)} %get-tuple-element.70) | copy-start | bytes 3145732
  311.6 6.5 %copy-start = (f32[512,1024]{1,0:T(8,128)S(1)}, f32[512,1024]{1,0:T(8,128)}, u32[]{:S(2)}) copy-start(f32[512,1024]{1,0:T(8,128)} %get-tuple-element.71) | copy-start | bytes 6291460

commit v3 on v2

v3 whole, which is shorter than its diff:
```python
import functools
import jax
import jax.numpy as jnp
from jax import lax
from jax.experimental import pallas as pl
from jax.experimental.pallas import tpu as pltpu
from jax.sharding import PartitionSpec as P

F32, BF16 = jnp.float32, jnp.bfloat16
VLIM = 56 * 2**20
GELU_A, GELU_B = 0.7978845608028654, 0.044715


def nn(a, b):
    return lax.dot_general(a, b, (((1,), (0,)), ((), ())), preferred_element_type=F32)


def nt(a, b):
    return lax.dot_general(a, b, (((1,), (1,)), ((), ())), preferred_element_type=F32)


def tn(a, b):
    return lax.dot_general(a, b, (((0,), (0,)), ((), ())), preferred_element_type=F32)


def sigmoid(v):
    return 1.0 / (1.0 + jnp.exp(-v))


def drop(u, decay):
    v = 2.0 * u
    series = 1.0 + v * (1.0 / 7.0)
    for k in (6.0, 5.0, 4.0, 3.0, 2.0):
        series = 1.0 + (v * (1.0 / k)) * series
    return jnp.where(v > -0.35, -v * series, 1.0 - decay * decay)


def gelu_parts(v):
    square = v * v
    inner = jnp.tanh(GELU_A * v * (1.0 + GELU_B * square))
    half = 0.5 + 0.5 * inner
    act = v * half
    slope = half + 0.5 * v * (1.0 - inner * inner) * (GELU_A + 3.0 * GELU_A * GELU_B * square)
    return act, slope


def gelu(v):
    inner = jnp.tanh(GELU_A * v * (1.0 + GELU_B * (v * v)))
    return v * (0.5 + 0.5 * inner)


def spread(dense, blocks, count, width):
    for a in range(count):
        parts = []
        if a > 0:
            parts.append(jnp.zeros((width, a * width), dense.dtype))
        parts.append(blocks[a])
        if a < count - 1:
            parts.append(jnp.zeros((width, (count - 1 - a) * width), dense.dtype))
        dense[a * width : (a + 1) * width, :] = jnp.concatenate(parts, axis=1)


def params(sem=("arbitrary",), **kw):
    return pltpu.CompilerParams(dimension_semantics=sem, vmem_limit_bytes=VLIM, **kw)


def whole(shape):
    return pl.BlockSpec(shape, lambda *_: (0,) * len(shape))


MESH = pl.DeviceIdType.MESH


def meet(peers):
    barrier = pltpu.get_barrier_semaphore()
    for peer in peers:
        pl.semaphore_signal(barrier, inc=1, device_id=peer, device_id_type=MESH)
    pl.semaphore_wait(barrier, len(peers))


def flip(index, bit):
    return index + bit - 2 * bit * (lax.rem(index // bit, 2))


class Entry:
    def __init__(self, part, got, n, send, recv):
        self.part, self.got, self.n = part, got, n
        self.me = lax.axis_index("seq")
        self.copies = [
            pltpu.make_async_remote_copy(
                src_ref=part, dst_ref=got.at[self.me], send_sem=send.at[k], recv_sem=recv.at[k],
                device_id=(lax.rem(self.me + k, n), lax.axis_index("batch")), device_id_type=MESH,
            )
            for k in range(1, n)
        ]

    def start(self):
        for copy in self.copies:
            copy.start()
        self.got[self.me] = self.part[...]

    def finish(self, out, reverse):
        for copy in self.copies:
            copy.wait()

        def one(k, state):
            j = self.n - 1 - k if reverse else k
            before = (j > self.me) if reverse else (j < self.me)
            return jnp.where(before, self.got[j, :, 0] * state + self.got[j, :, 1], state)

        out[...] = lax.fori_loop(0, self.n, one, jnp.zeros(out.shape, F32))


def front_kernel(
    seqs, length, seq_n, tok, gain, gw, bw, taps, vec, wr, wi,
    normed, gate, branch, edge, mixed, rate, inlet, h, p, entry,
    halo, hn, ext, dr, di, rp, ip, carry, got, state, h_send, h_recv, send, recv,
):
    rows, width = seqs * length, gw.shape[1]
    sub = dr.shape[-1]

    seq, bat = lax.axis_index("seq"), lax.axis_index("batch")

    @pl.when(pl.program_id(0) == 0)
    def _():
        meet([(lax.rem(seq + k, seq_n), bat) for k in range(1, seq_n)])
        copies = [
            pltpu.make_async_remote_copy(
                src_ref=tok.at[(s + 1) * length - 16 : (s + 1) * length], dst_ref=halo.at[s], send_sem=h_send.at[s], recv_sem=h_recv.at[s],
                device_id=(lax.rem(seq + 1, seq_n), bat), device_id_type=MESH,
            )
            for s in range(seqs)
        ]
        for copy in copies:
            copy.start()

        def norm(i, _):
            x = tok[pl.ds(i * 32, 32), :].astype(F32)
            r = lax.rsqrt(jnp.mean(x * x, axis=-1, keepdims=True) + 1e-06)
            normed[pl.ds(i * 32, 32), :] = (x * r * gain[...]).astype(BF16)
            return 0

        lax.fori_loop(0, rows // 32, norm, 0)
        for s in range(seqs):
            copies[s].wait()
            x = halo[s].astype(F32)
            r = lax.rsqrt(jnp.mean(x * x, axis=-1, keepdims=True) + 1e-06)
            hn[16 * s : 16 * s + 16, :] = (x * r * gain[...]).astype(BF16)

    gate[...] = nn(normed[...], gw[...])
    b16 = nn(normed[...], bw[...]).astype(BF16)
    e16 = (nn(hn[...], bw[...]) * (seq > 0).astype(F32)).astype(BF16)
    branch[...] = b16
    edge[...] = e16
    e32 = e16.astype(F32)
    for s in range(seqs):
        ext[s, 0:8, :] = e32[16 * s + 8 : 16 * s + 16]
        ext[s, 8 : 8 + length, :] = b16[length * s : length * (s + 1)].astype(F32)

    tap = [taps[k : k + 1, :] for k in range(4)]
    off = vec[0:1, :]
    for s in range(seqs):

        def conv(i, _):
            x = ext[s, pl.ds(pl.multiple_of(i * 16, 16), 24), :]
            total = off + tap[0] * x[8:24]
            for k in range(1, 4):
                total = total + tap[k] * x[8 - k : 24 - k]
            mixed[pl.ds(pl.multiple_of(s * length + i * 16, 16), 16), :] = total.astype(BF16)
            return 0

        lax.fori_loop(0, length // 16, conv, 0)

    for g in range(width // sub):
        cols = slice(g * sub, (g + 1) * sub)
        spread(dr.at[g], [wr[g * 4 + a] for a in range(4)], 4, wr.shape[-1])
        spread(di.at[g], [wi[g * 4 + a] for a in range(4)], 4, wi.shape[-1])
        rp[:, cols] = nn(mixed[:, cols], dr[g])
        ip[:, cols] = nn(mixed[:, cols], di[g])

    ro, io, slope = vec[1:2, :], vec[2:3, :], -8.0 * vec[3:4, :]

    def gates(i, _):
        at = pl.ds(pl.multiple_of(i * 16, 16), 16)
        rt = sigmoid(rp[at, :] + ro)
        it = sigmoid(ip[at, :] + io)
        log_decay = rt * slope
        decay = jnp.exp(log_decay)
        rate[at, :] = rt
        inlet[at, :] = it
        p[at, :] = decay
        h[at, :] = jnp.sqrt(drop(log_decay, decay)) * it * mixed[at, :].astype(F32)
        return 0

    lax.fori_loop(0, rows // 16, gates, 0)

    row = lax.broadcasted_iota(jnp.int32, (8, width), 0)

    def scan(i, last):
        out = []
        for s in range(seqs):
            at = pl.ds(pl.multiple_of(s * length + i * 8, 8), 8)
            a, b = p[at, :], h[at, :]
            for d in (1, 2, 4):
                keep = row >= d
                b = b + a * jnp.where(keep, pltpu.roll(b, d, 0), 0.0)
                a = a * jnp.where(keep, pltpu.roll(a, d, 0), 1.0)
            ap, bp = last[s]
            b = b + a * bp
            a = a * ap
            p[at, :] = a
            h[at, :] = b
            out.append((a[7:8], b[7:8]))
        return tuple(out)

    init = tuple((jnp.ones((1, width), F32), jnp.zeros((1, width), F32)) for _ in range(seqs))
    last = lax.fori_loop(0, length // 8, scan, init)
    for s in range(seqs):
        carry[pl.program_id(0), 0, s : s + 1, :] = last[s][0]
        carry[pl.program_id(0), 1, s : s + 1, :] = last[s][1]

    @pl.when(pl.program_id(0) == 1)
    def _():
        arriving = Entry(carry, got, seq_n, send, recv)
        arriving.start()
        arriving.finish(state, False)
        for g in range(2):
            for s in range(seqs):
                entry[s, :, g * width : (g + 1) * width] = state[g, s : s + 1, :]


def front(tok, gain, gw, bw, taps, vec, wr, wi, seqs, length, seq_n, collective_id):
    rows, model = tok.shape
    lru, bw_ = gw.shape[1], wr.shape[-1]
    width, sub, per = lru // 2, 4 * bw_, lru // 2 // bw_
    col = lambda r: pl.BlockSpec((r, width), lambda j: (0, j))
    blk = pl.BlockSpec((per, bw_, bw_), lambda j: (j, 0, 0))
    f = lambda dt: jax.ShapeDtypeStruct((rows, lru), dt)
    vm, dma = pltpu.VMEM, lambda n: pltpu.SemaphoreType.DMA((n,))
    return pl.pallas_call(
        functools.partial(front_kernel, seqs, length, seq_n),
        grid=(2,),
        in_specs=[
            whole((rows, model)), whole((1, model)),
            pl.BlockSpec((model, width), lambda j: (0, j)), pl.BlockSpec((model, width), lambda j: (0, j)), col(4), col(8), blk, blk,
        ],
        out_specs=[
            whole((rows, model)), col(rows), col(rows), col(16 * seqs), col(rows), col(rows), col(rows), col(rows), col(rows),
            whole((seqs, 1, lru)),
        ],
        out_shape=[
            jax.ShapeDtypeStruct((rows, model), BF16), f(F32), f(BF16),
            jax.ShapeDtypeStruct((16 * seqs, lru), BF16), f(BF16), f(F32), f(F32), f(F32), f(F32),
            jax.ShapeDtypeStruct((seqs, 1, lru), F32),
        ],
        scratch_shapes=[
            vm((seqs, 16, model), BF16), vm((16 * seqs, model), BF16), vm((seqs, 8 + length, width), F32),
            vm((2, sub, sub), BF16), vm((2, sub, sub), BF16), vm((rows, width), F32), vm((rows, width), F32),
            vm((2, 2, seqs, width), F32), vm((seq_n, 2, 2, seqs, width), F32), vm((2, seqs, width), F32),
            dma(seqs), dma(seqs), dma(seq_n), dma(seq_n),
        ],
        compiler_params=params(collective_id=collective_id, has_side_effects=True),
        name="front",
    )(tok, gain, gw, bw, taps, vec, wr, wi)


def join_kernel(tok, gate, h, p, entry, ow, gain, joined, resid, normed, state_ref):
    rows = tok.shape[0]
    ent = entry[0]

    def join(i, _):
        at = pl.ds(pl.multiple_of(i * 16, 16), 16)
        state = h[at, :] + p[at, :] * ent
        state_ref[at, :] = state
        joined[at, :] = (gelu(gate[at, :]) * state).astype(BF16)
        return 0

    lax.fori_loop(0, rows // 16, join, 0)
    resid[...] = nn(joined[...], ow[...])

    def norm(i, _):
        at = pl.ds(pl.multiple_of(i * 32, 32), 32)
        y = tok[at, :].astype(F32) + resid[at, :]
        resid[at, :] = y
        r = lax.rsqrt(jnp.mean(y * y, axis=-1, keepdims=True) + 1e-06)
        normed[at, :] = (y * r * gain[...]).astype(BF16)
        return 0

    lax.fori_loop(0, rows // 32, norm, 0)


def join(tok, gate, h, p, entry, ow, gain, seqs, length):
    rows, model = tok.shape
    lru = gate.shape[1]
    tile = 128
    per = length // tile
    row = lambda w: pl.BlockSpec((tile, w), lambda i: (i, 0))
    return pl.pallas_call(
        join_kernel,
        grid=(rows // tile,),
        in_specs=[row(model), row(lru), row(lru), row(lru), pl.BlockSpec((1, 1, lru), lambda i: (i // per, 0, 0)), whole((lru, model)), whole((1, model))],
        out_specs=[row(lru), row(model), row(model), row(lru)],
        out_shape=[jax.ShapeDtypeStruct((rows, lru), BF16), jax.ShapeDtypeStruct((rows, model), F32), jax.ShapeDtypeStruct((rows, model), BF16), jax.ShapeDtypeStruct((rows, lru), F32)],
        compiler_params=params(),
        name="join",
    )(tok, gate, h, p, entry, ow, gain)


ORDERS = {"A": ("xhyl", "yxhl"), "E": ("xlhy", "yxlh"), "F": ("xylh", "yxlh")}


class Exchange:
    def __init__(self, chunks, bufs, fin, send, recv):
        self.chunks, self.bufs, self.fin, self.sems = chunks, bufs, fin, (send, recv)
        self.first = [sum(c[2] for c in chunks[:q]) for q in range(len(chunks))]
        seq, bat = lax.axis_index("seq"), lax.axis_index("batch")
        core, y = lax.rem(bat, 2), bat // 2
        x, low, high = lax.rem(seq, 2), lax.rem(seq // 2, 2), seq // 4
        bit = {"x": x, "y": y, "l": low, "h": high}
        move = {"x": (1 - 2 * x, 0), "y": (0, 2 - 4 * y), "l": (2 - 4 * low, 0), "h": (4 - 8 * high, 0)}
        pick = lambda a, b: a if a is b else (1 - core) * a + core * b
        self.core, self.y = core, y
        self.other, self.across = (seq, bat + 1 - 2 * core), (seq, bat + 2 - 4 * y)
        self.bits, self.peers = {}, {}
        for kind, (first, second) in ORDERS.items():
            self.bits[kind] = [pick(bit[a], bit[b]) for a, b in zip(first, second)]
            self.peers[kind] = [
                (seq + pick(move[a][0], move[b][0]), bat + pick(move[a][1], move[b][1])) for a, b in zip(first, second)
            ] + [self.across, self.other]
        self.greet = [(seq + move[a][0], bat) for a in "xlh"] + [self.across, self.other]
        self.freed, self.further = set(), {}

    def at(self, place):
        for k, q in PLAN.get(place, ()):
            self.step(k, q)

    def free(self, q):
        self.copy(0, q).wait_send()
        self.freed.add(q)

    def drain(self):
        self.at("drain")
        for q in range(len(self.chunks)):
            for k in range(4):
                if k > 0 or q not in self.freed:
                    self.copy(k, q).wait_send()

    def copy(self, k, q):
        grad, row, part, kind = self.chunks[q]
        size, bits = 8 >> k, self.bits[kind]
        at = slice(self.first[q], self.first[q] + part)
        if k == 0:
            src, dst = grad.at[pl.ds((1 - bits[0]) * 8, 8), row : row + part], self.bufs[0].at[:, at]
        elif k < 4:
            src, dst = self.bufs[k - 1].at[pl.ds((1 - bits[k]) * size, size), at], self.bufs[k].at[:, at]
        elif k == 4:
            src = dst = self.fin.at[self.core, self.y, at]
        else:
            src = dst = self.fin.at[self.core, :, at]
        return pltpu.make_async_remote_copy(
            src_ref=src, dst_ref=dst, send_sem=self.sems[0].at[k, q], recv_sem=self.sems[1].at[k, q],
            device_id=self.peers[kind][k], device_id_type=MESH,
        )

    def add(self, k, q, base, size):
        grad, row, part, kind = self.chunks[q]
        dst, bits = self.bufs[k], self.bits[kind]
        for j in range(size):

            def body(i, _):
                a = pl.ds(pl.multiple_of(self.first[q] + i * 128, 128), 128)
                if k == 0:
                    own = grad[bits[0] * 8 + base + j, pl.ds(pl.multiple_of(row + i * 128, 128), 128), :]
                else:
                    own = self.bufs[k - 1][bits[k] * (8 >> k) + base + j, a, :]
                dst[base + j, a, :] = dst[base + j, a, :] + own
                return 0

            lax.fori_loop(0, part // 128, body, 0)

    def step(self, k, q):
        if k > 5:
            self.further[k][q]()
        elif k < 0:
            self.copy(0, q).start()
        elif k < 3:
            half, bits = 4 >> k, self.bits[self.chunks[q][3]]
            self.copy(k, q).wait_recv()
            self.add(k, q, (1 - bits[k + 1]) * half, half)
            self.copy(k + 1, q).start()
            self.add(k, q, bits[k + 1] * half, half)
        elif k == 3:
            bits = self.bits[self.chunks[q][3]]
            self.copy(3, q).wait_recv()

            def body(i, _):
                a = pl.ds(pl.multiple_of(self.first[q] + i * 128, 128), 128)
                self.fin[self.core, self.y, a, :] = self.bufs[3][0, a, :] + self.bufs[2][bits[3], a, :]
                return 0

            lax.fori_loop(0, self.chunks[q][2] // 128, body, 0)
            self.copy(4, q).start()
        elif k == 4:
            self.copy(4, q).wait()
            self.copy(5, q).start()
        else:
            self.copy(5, q).wait()

    @staticmethod
    def scratch(chunks, rows):
        return [pltpu.VMEM((8 >> k, rows, 128), BF16) for k in range(4)] + [pltpu.SemaphoreType.DMA((6, chunks))] * 2


class BlockSums:
    def __init__(self, value, bufs, out, send, recv):
        self.value, self.bufs, self.out, self.sems = value, bufs, out, (send, recv)
        seq, bat = lax.axis_index("seq"), lax.axis_index("batch")
        core, y = lax.rem(bat, 2), bat // 2
        x, low, high = lax.rem(seq, 2), lax.rem(seq // 2, 2), seq // 4
        self.bits = [core, low, high, x, y]
        self.peers = [(seq, bat + 1 - 2 * core), (seq + 2 - 4 * low, bat), (seq + 4 - 8 * high, bat), (seq + 1 - 2 * x, bat), (seq, bat + 2 - 4 * y)]
        self.base = [0]
        for k in range(5):
            self.base.append(self.base[-1] + self.bits[k] * (16 >> k))

    def halve(self, k):
        size = 16 >> k
        return pltpu.make_async_remote_copy(
            src_ref=self.value.at[pl.ds(self.base[k] + (1 - self.bits[k]) * size, size)], dst_ref=self.bufs[k],
            send_sem=self.sems[0].at[k], recv_sem=self.sems[1].at[k], device_id=self.peers[k], device_id_type=MESH,
        )

    def hand(self, k):
        at = pl.ds(self.base[k + 1], 16 >> k)
        return pltpu.make_async_remote_copy(
            src_ref=self.out.at[at], dst_ref=self.out.at[at],
            send_sem=self.sems[0].at[5 + k], recv_sem=self.sems[1].at[5 + k], device_id=self.peers[k], device_id_type=MESH,
        )

    def events(self):
        def took(k):
            size = 16 >> k
            self.halve(k).wait()

            def body(j, _):
                at = self.base[k + 1] + j
                total = (self.value[at].astype(F32) + self.bufs[k][j].astype(F32)).astype(BF16)
                if k < 4:
                    self.value[at] = total
                else:
                    self.out[at] = total
                return 0

            lax.fori_loop(0, size, body, 0)
            if k < 4:
                self.halve(k + 1).start()
            else:
                self.hand(4).start()

        def got(k):
            self.hand(k).wait()
            if k > 0:
                self.hand(k - 1).start()

        first = [lambda: self.halve(0).start()]
        return first + [functools.partial(took, k) for k in range(5)] + [functools.partial(got, k) for k in range(4, -1, -1)]

    @staticmethod
    def scratch(width):
        return [pltpu.VMEM((16 >> k, width, 128), BF16) for k in range(5)] + [pltpu.SemaphoreType.DMA((10,))] * 2


def core_of():
    return lax.rem(lax.axis_index("batch"), 2)


def group(core):
    i = pl.program_id(0)
    return (1 - i) * (1 - core) + i * core


def put_pieces(chunks, row, acc, core, y, s):
    part, cols = acc.shape
    for t in range(cols // 128):
        at = row[t] if isinstance(row, (list, tuple)) else row + t * part
        base = 0
        for ref, first, rows, kind in chunks:
            low, high = max(at, base), min(at + part, base + rows)
            if low < high:
                ref[place_of(core, s, y, kind), first + low - base : first + high - base, :] = acc[
                    low - at : high - at, t * 128 : (t + 1) * 128
                ].astype(BF16)
            base += rows


def place_of(core, s, y, kind):
    bit = {"x": s % 2, "l": (s // 2) % 2, "h": s // 4, "y": y}
    place = lambda order: sum(bit[a] * (8 >> k) for k, a in enumerate(order))
    first, second = ORDERS[kind]
    return place(first) if first == second else (1 - core) * place(first) + core * place(second)


def wgrad(core, chunks, lhs, lhs_far, rhs, rhs_far, own_columns):
    rows, deep = lhs.shape
    tile = rhs.shape[1] // (2 if own_columns else 4)
    base, part = 0 if own_columns else 2 * core, deep // 8

    def body(a, b, c, d):
        acc = tn(a[...], c[...]) + tn(b[...], d[...])
        for s in range(8):
            put_pieces(chunks, 0, acc[s * part : (s + 1) * part], core, pl.program_id(0), s)

    left = pl.BlockSpec(lhs.shape, lambda y: (0, 0), pipeline_mode=pl.Buffered(1))
    right = pl.BlockSpec((rows, tile), lambda y: (0, base + y))
    pltpu.emit_pipeline(body, grid=(2,), in_specs=[left, left, right, right])(lhs, lhs_far, rhs, rhs_far)


def wgrad_up(core, gate_chunk, up_chunk, lhs, lhs_far, rhs, rhs_far, begin):
    rows, deep = lhs.shape
    tile, part = rhs.shape[2], deep // 8

    def body(a, b, c, d):
        pump = begin()
        acc = tn(a[...], c[0]) + tn(b[...], d[0])
        for j, chunk in enumerate((gate_chunk, up_chunk)):

            @pl.when(pl.program_id(0) == j)
            def _():
                for s in range(8):
                    for y in range(2):
                        put_pieces([chunk], 0, acc[s * part : (s + 1) * part, y * tile // 2 : (y + 1) * tile // 2], core, y, s)

        pump()

    left = pl.BlockSpec(lhs.shape, lambda i: (0, 0), pipeline_mode=pl.Buffered(1))
    right = pl.BlockSpec((1, rows, tile), lambda i: (i, 0, 0))
    pltpu.emit_pipeline(body, grid=(2,), in_specs=[left, left, right, right])(lhs, lhs_far, rhs, rhs_far)


def wgrad_down(core, chunks, hid, hid_far, cot, cot_far, begin):
    _, parts, rows, units = hid.shape
    half_cols = cot.shape[1] // 2
    block = 2 * parts * units // 8

    def body(l, m, c, d):
        pump = begin()
        i = pl.program_id(0)
        acc = tn(l[0, 0], c[...]) + tn(m[0, 0], d[...])
        for side in range(2):
            for p in range(parts):

                @pl.when(i == side * parts + p)
                def _():
                    half = core if side else 1 - core
                    for j in range(units // 128):
                        unit = p * units + j * 128
                        s = 4 * half + unit // block
                        row = unit % block
                        for y in range(2):
                            cut = acc[j * 128 : (j + 1) * 128, y * half_cols // 2 : (y + 1) * half_cols // 2]
                            put_pieces(chunks, [row, block + row], cut, core, y, s)

        pump()

    mine = pl.BlockSpec((1, 1, rows, units), lambda i: (i // parts, i % parts, 0, 0))
    theirs = pl.BlockSpec((1, 1, rows, units), lambda i: (1 - i // parts, i % parts, 0, 0))
    right = pl.BlockSpec((rows, half_cols), lambda i: (0, core), pipeline_mode=pl.Buffered(1))
    pltpu.emit_pipeline(body, grid=(2 * parts,), in_specs=[mine, theirs, right, right])(hid, hid_far, cot, cot_far)


def feed(core, part, n2, cot, fg, fu, fd, hid, ups, acc, begin):
    rows, model = n2.shape
    parts, tile = hid.shape[1], hid.shape[3]
    block = rows // 2

    def body(n2_ref, cot_ref, fg_ref, fu_ref, fd_ref, hid_ref, gg_ref, gu_ref):
        pump = begin()
        for r in range(2):
            at = slice(r * block, (r + 1) * block)
            gate, up = nn(n2_ref[at, :], fg_ref[...]), nn(n2_ref[at, :], fu_ref[...])
            g = nt(cot_ref[at, :], fd_ref[...])
            act, slope = gelu_parts(gate)
            hid_ref[0, 0, at, :] = (act * up).astype(BF16)
            gg_ref[0, 0, at, :] = (g * up * slope).astype(BF16)
            gu_ref[0, 0, at, :] = (g * act).astype(BF16)
        total = nt(gg_ref[0, 0], fg_ref[...]) + nt(gu_ref[0, 0], fu_ref[...])
        if part == 0:

            @pl.when(pl.program_id(0) == 0)
            def _():
                acc[...] = total

            @pl.when(pl.program_id(0) > 0)
            def _():
                acc[...] += total

        else:
            acc[...] += total
        pump()

    unit = lambda i: ((1 - i) * (1 - core) + i * core) * parts + part
    flat = pl.BlockSpec((rows, model), lambda i: (0, 0), pipeline_mode=pl.Buffered(1))
    col = pl.BlockSpec((model, tile), lambda i: (0, unit(i)))
    out = pl.BlockSpec((1, 1, rows, tile), lambda i: (i, part, 0, 0))
    pltpu.emit_pipeline(
        body, grid=(2,), in_specs=[flat, flat, col, col, pl.BlockSpec((tile, model), lambda i: (unit(i), 0))], out_specs=[out, out, out]
    )(n2, cot, fg, fu, fd, hid, ups.at[0], ups.at[1])


def norm_back(core, gn, resid, cot, fgain, gres, low, gain_sum):
    rows, model = gn.shape
    tile = 128
    gain_sum[...] = jnp.zeros_like(gain_sum)

    def body(y_ref, c_ref, out_ref):
        g = fgain[...]

        def norm(i, total):
            at = pl.ds(pl.multiple_of(i * 16, 16), 16)
            place = pl.ds(pl.multiple_of(pl.program_id(0) * tile + i * 16, 16), 16)
            y, d = y_ref[at, :], gn[place, :]
            r = lax.rsqrt(jnp.mean(y * y, axis=-1, keepdims=True) + 1e-06)
            dg, yr = d * g, y * r
            dot = jnp.mean(dg * yr, axis=-1, keepdims=True)
            out = c_ref[at, :].astype(F32) + r * (dg - yr * dot)
            out_ref[at, :] = out
            low[place, :] = out.astype(BF16)
            add = d * yr
            return total + add[0:8] + add[8:16]

        total = lax.fori_loop(0, tile // 16, norm, jnp.zeros((8, model), F32))
        gain_sum[...] += jnp.sum(total, axis=0, keepdims=True)

    row = pl.BlockSpec((tile, model), lambda i: (i, 0))
    pltpu.emit_pipeline(body, grid=(rows // tile,), in_specs=[row, row], out_specs=[row])(resid, cot, gres)


def turn(core, seqs, length, low, ow, gate, state, rate, vec, ggate, lc, q, carry, gj, begin):
    rows, lru = gate.shape
    width = lru // 2

    def body(ow_ref, gate_ref, state_ref, rate_ref, vec_ref, gg_ref, lc_ref, q_ref):
        pump = begin()
        for s in range(seqs):
            gj[s, 0:length, :] = nt(low[s * length : (s + 1) * length, :], ow_ref[...])
        pump()
        slope = -8.0 * vec_ref[3:4, :]
        for s in range(seqs):

            def act(i, _):
                at = pl.ds(pl.multiple_of(s * length + i * 16, 16), 16)
                here = pl.ds(pl.multiple_of(i * 16, 16), 16)
                value, der = gelu_parts(gate_ref[at, :])
                d = gj[s, here, :]
                gg_ref[0, at, :] = (d * state_ref[at, :] * der).astype(BF16)
                gj[s, here, :] = d * value
                return 0

            lax.fori_loop(0, length // 16, act, 0)
            pump()

        row = lax.broadcasted_iota(jnp.int32, (8, width), 0)
        tiles = length // 8

        def scan(k, last):
            i = tiles - 1 - k
            out = []
            for s in range(seqs):
                at = pl.ds(pl.multiple_of(s * length + i * 8, 8), 8)
                g = gj[s, pl.ds(pl.multiple_of(i * 8, 8), 8), :]
                a = jnp.exp(rate_ref[at, :] * slope)
                b = a * g
                for d in (1, 2, 4):
                    keep = row < 8 - d
                    b = b + a * jnp.where(keep, pltpu.roll(b, 8 - d, 0), 0.0)
                    a = a * jnp.where(keep, pltpu.roll(a, 8 - d, 0), 1.0)
                ap, bp = last[s]
                b = b + a * bp
                a = a * ap
                lc_ref[at, :] = g + jnp.where(row < 7, pltpu.roll(b, 7, 0), bp)
                q_ref[at, :] = jnp.where(row < 7, pltpu.roll(a, 7, 0), ap)
                out.append((a[0:1], b[0:1]))
            return tuple(out)

        init = tuple((jnp.ones((1, width), F32), jnp.zeros((1, width), F32)) for _ in range(seqs))
        last = lax.fori_loop(0, tiles, scan, init)
        for s in range(seqs):
            carry[group(core), 0, s : s + 1, :] = last[s][0]
            carry[group(core), 1, s : s + 1, :] = last[s][1]
        pump()

    grp = lambda i: (1 - i) * (1 - core) + i * core
    col = lambda r: pl.BlockSpec((r, width), lambda i: (0, grp(i)))
    pltpu.emit_pipeline(
        body, grid=(2,),
        in_specs=[
            pl.BlockSpec((width, ow.shape[1]), lambda i: (grp(i), 0)), col(rows), col(rows), col(rows), col(8),
        ],
        out_specs=[pl.BlockSpec((1, rows, width), lambda i: (i, 0, 0)), col(rows), col(rows)],
    )(ow, gate, state, rate, vec, ggate, lc, q)


def gates_back(
    own, core, seqs, length, lc, q, cin, states, entry, rate, inlet, mixed, branch, edge, wr, wi, taps, vec,
    gb, head, tail, blocks, rate_sum, inlet_sum, sums_out, dr, di, gr, gi, gm, ext, begin,
):
    rows, lru = lc.shape
    width, bw_ = lru // 2, wr.shape[-1]
    per, sub = width // bw_, dr.shape[-1]

    def body(
        lc_ref, q_ref, state_ref, e_ref, rate_ref, inlet_ref, mixed_ref, branch_ref, edge_ref, wr_ref, wi_ref, taps_ref, vec_ref,
        gb_ref,
    ):
        pump = begin()
        mine = group(core)
        slope = -8.0 * vec_ref[3:4, :]
        zero = jnp.zeros((8, width), F32)
        row = lax.broadcasted_iota(jnp.int32, (16, width), 0)

        sums = (zero, zero, zero)
        for s in range(seqs):
            c_in, ent = cin[mine, s : s + 1, :], e_ref[s]

            def gates(i, carry):
                (before, t0, t1, t2) = carry
                at = pl.ds(pl.multiple_of(s * length + i * 16, 16), 16)
                state = state_ref[at, :]
                prev = jnp.where(row > 0, pltpu.roll(state, 1, 0), before)
                carried = lc_ref[at, :] + q_ref[at, :] * c_in
                rt, it, mx = rate_ref[at, :], inlet_ref[at, :], mixed_ref[at, :].astype(F32)
                log_decay = rt * slope
                decay = jnp.exp(log_decay)
                gap = drop(log_decay, decay)
                inv = lax.rsqrt(gap)
                nf = gap * inv
                im = it * mx
                g_log = carried * decay * (prev - im * decay * inv)
                cn = carried * nf
                g_rt = g_log * slope * (rt * (1.0 - rt))
                g_it = cn * im * (1.0 - it)
                gr[at, :] = g_rt.astype(BF16)
                gi[at, :] = g_it.astype(BF16)
                gm[s, pl.ds(pl.multiple_of(i * 16, 16), 16), :] = cn * it
                lr = g_log * rt
                return (state[15:16], t0 + lr[0:8] + lr[8:16], t1 + g_rt[0:8] + g_rt[8:16], t2 + g_it[0:8] + g_it[8:16])

            _, *sums = lax.fori_loop(0, length // 16, gates, (ent, *sums))
            pump()
        down = lambda v: jnp.sum(v, axis=0, keepdims=True)
        lanes = pl.ds(pl.multiple_of(mine * width, 128), width)
        sums_out[4:5, lanes] = down(sums[0]) * (-8.0 * vec_ref[4:5, :])
        sums_out[5:6, lanes] = down(sums[1])
        sums_out[6:7, lanes] = down(sums[2])

        for g in range(width // sub):
            cols = slice(g * sub, (g + 1) * sub)
            spread(dr, [wr_ref[g * 4 + a] for a in range(4)], 4, bw_)
            spread(di, [wi_ref[g * 4 + a] for a in range(4)], 4, bw_)
            back = nt(gr[:, cols], dr[...]) + nt(gi[:, cols], di[...])
            rs = tn(mixed_ref[:, cols], gr[:, cols])
            is_ = tn(mixed_ref[:, cols], gi[:, cols])
            for a in range(4):
                block = slice(a * bw_, (a + 1) * bw_)
                if own:
                    blocks[mine * per + g * 4 + a, :, 0:bw_] = rs[block, block].astype(BF16)
                    blocks[2 * per + mine * per + g * 4 + a, :, 0:bw_] = is_[block, block].astype(BF16)
                else:
                    rate_sum[mine * per + g * 4 + a] = rs[block, block]
                    inlet_sum[mine * per + g * 4 + a] = is_[block, block]
            for s in range(seqs):
                gm[s, 0:length, cols] += back[s * length : (s + 1) * length]
        pump()

        for s in range(seqs):
            gm[s, length : length + 8, :] = zero
            ext[s, 0:8, :] = edge_ref[16 * s : 16 * s + 16].astype(F32)[8:16]
            ext[s, 8 : 8 + length, :] = branch_ref[s * length : (s + 1) * length].astype(F32)
            head[mine, 8 * s : 8 * s + 8, :] = gm[s, 0:8, :]

        tap = [taps_ref[k : k + 1, :] for k in range(4)]
        acc = (zero,) * 5
        for s in range(seqs):

            def conv(i, acc):
                lo = pl.multiple_of(i * 16, 16)
                y = gm[s, pl.ds(lo, 24), :]
                x = ext[s, pl.ds(lo, 24), :]
                total = tap[0] * y[0:16]
                for k in range(1, 4):
                    total = total + tap[k] * y[k : k + 16]
                gb_ref[0, pl.ds(pl.multiple_of(s * length + i * 16, 16), 16), :] = total.astype(BF16)
                now = y[0:16]
                new = []
                for k in range(4):
                    prod = now * x[8 - k : 24 - k]
                    new.append(acc[k] + prod[0:8] + prod[8:16])
                new.append(acc[4] + now[0:8] + now[8:16])
                return tuple(new)

            acc = lax.fori_loop(0, length // 16, conv, acc)
            y = gm[s, length - 16 : length + 8, :]
            total = tap[0] * y[0:16]
            for k in range(1, 4):
                total = total + tap[k] * y[k : k + 16]
            tail[mine, 16 * s : 16 * s + 16, :] = total
            pump()
        for k in range(4):
            sums_out[k : k + 1, lanes] = down(acc[k])
        sums_out[7:8, lanes] = down(acc[4])

    grp = lambda i: (1 - i) * (1 - core) + i * core
    col = lambda r: pl.BlockSpec((r, width), lambda i: (0, grp(i)))
    blk = pl.BlockSpec((per, bw_, bw_), lambda i: (grp(i), 0, 0))
    pltpu.emit_pipeline(
        body, grid=(2,),
        in_specs=[
            col(rows), col(rows), col(rows), pl.BlockSpec((seqs, 1, width), lambda i: (0, 0, grp(i))),
            col(rows), col(rows), col(rows), col(rows), col(edge.shape[0]), blk, blk, col(4), col(8),
        ],
        out_specs=[pl.BlockSpec((1, rows, width), lambda i: (i, 0, 0))],
    )(lc, q, states, entry, rate, inlet, mixed, branch, edge, wr, wi, taps, vec, gb)


def spaced(exchange, name, steps):
    def begin():
        place = iter(range(64))

        def pump():
            j = next(place)
            for i in range(steps):
                if PLAN.get(f"{name}{i}{j}"):

                    @pl.when(pl.program_id(0) == i)
                    def _():
                        exchange.at(f"{name}{i}{j}")

        return pump

    return begin


def no_pump():
    return lambda: None


ANY = pl.BlockSpec(memory_space=pl.ANY)
INSIDE = pl.BlockSpec(memory_space=pltpu.VMEM)


KINDS = "AFEAFEAFEAFE"
PLAN = {
    "u000": [(-1, 0)],
    "u010": [(-1, 1)],
    "f200": [(0, 0), (0, 1)],
    "u100": [(-1, 2)],
    "u110": [(1, 0), (-1, 3), (1, 1)],
    "u200": [(-1, 4)],
    "d00": [(2, 0), (2, 1)],
    "d40": [(3, 0), (3, 1), (0, 2), (-1, 5)],
    "t00": [(4, 0), (4, 1), (0, 3), (-1, 6)],
    "t01": [(1, 2)],
    "t02": [(5, 0), (5, 1), (0, 4), (-1, 7)],
    "t12": [(2, 2)],
    "b1": [(3, 2), (1, 3), (0, 5), (-1, 8)],
    "b2": [(1, 4)],
    "g01": [(4, 2), (0, 6), (-1, 9)],
    "g02": [(2, 3), (2, 4)],
    "g03": [(5, 2), (0, 7)],
    "g10": [(1, 5)],
    "g11": [(3, 3), (3, 4)],
    "c1": [(-1, 10), (4, 3), (4, 4), (2, 5), (1, 6), (1, 7), (0, 8), (6, 0)],
    "c3": [(5, 3), (5, 4), (6, 1)],
    "c4": [(-1, 11), (3, 5)],
    "i00": [(2, 6), (2, 7), (0, 9)],
    "i10": [(4, 5)],
    "i30": [(5, 5)],
    "o00": [(3, 6), (3, 7), (1, 8), (6, 2)],
    "o10": [(7, 0)],
    "drain": [(4, 6), (4, 7), (0, 10), (7, 1), (5, 6), (5, 7), (6, 3), (2, 8), (0, 11), (1, 9), (7, 2), (3, 8), (6, 4), (6, 5), (4, 8), (1, 10), (7, 3), (6, 6), (2, 9), (5, 8), (6, 7), (1, 11), (7, 4), (3, 9), (6, 8), (2, 10), (4, 9), (5, 9), (2, 11), (3, 10), (6, 9), (3, 11), (4, 10), (6, 10), (5, 10), (4, 11), (5, 11)],
}

PARTS = [256] * 9 + [384] * 3
SWAPS = 10


def backward(own, seqs, length, seq_n, batch_n, grads_in, values, collective_id):
    (
        n2, resid, cot, fgain, ow, gate, state, entry, rate, vec, inlet, mixed, branch, edge, wr, wi, taps, gw, bw, tok, mgain,
        fg, fu, fd, joined, normed,
    ) = values
    rows, model = n2.shape
    lru, units = gate.shape[1], fd.shape[0]
    width, bw_ = lru // 2, wr.shape[-1]
    per, sub = width // bw_, 4 * bw_
    steps = [("batch", 1 << k) for k in range(batch_n.bit_length() - 1)] + [("seq", 1 << k) for k in range(seq_n.bit_length() - 1)]
    n_steps = len(steps)
    parts, unit = 3, units // 6
    if not own:
        grads_in = []

    def kernel(*refs):
        refs = list(refs)
        cut = lambda n: [refs.pop(0) for _ in range(n)]
        far_in = cut(len(grads_in))
        (
            n2, resid, cot, fgain, ow, gate, state, entry, rate, vec, inlet, mixed, branch, edge, wr, wi, taps, gw, bw, tok, mgain,
            fg, fu, fd, joined, normed,
        ) = cut(26)
        tokens_grad, block_out, totals, gres, low_out, low_far, ggate, ggate_far, lc, q, gb, gb_far, hid, hid_far, ups, ups_far, n2_far, joined_far = cut(18)
        fin, block_total = cut(2) if own else (None, None)
        rate_sum, inlet_sum = (None, None) if own else cut(2)
        low, carry, got, cin, dr, di, gr, gi, gm, ext, head, tail, ahead, fixed, gain_sum, acc, small, gn = cut(18)
        send, recv, swap_send, swap_recv, one, local, s_send, s_recv = cut(8)

        core = core_of()
        seq, bat = lax.axis_index("seq"), lax.axis_index("batch")
        other = (seq, bat + 1 - 2 * core)
        peers = [(flip(seq, bit), bat) if axis == "seq" else (seq, flip(bat, bit)) for axis, bit in steps]
        exchange, blocks = None, None
        if own:
            g0, g1, g2, *bufs, x_send, x_recv = cut(9)
            blocks, *block_bufs, b_send, b_recv = cut(8)
            places = [(ref, row) for row in (0, 256, 512) for ref in (g0, g1)] + [(g2, 0), (g2, 256), (g2, 512), (g0, 0), (g0, 384), (g1, 0)]
            chunks = [(ref, row, part, kind) for (ref, row), part, kind in zip(places, PARTS, KINDS)]
            exchange = Exchange(chunks, bufs, fin, x_send, x_recv)
            exchange.further[6] = BlockSums(blocks, block_bufs, block_total, b_send, b_recv).events()
            blocks[...] = jnp.zeros_like(blocks)
        small[0] = jnp.zeros((16, lru), F32)
        greet = [(lax.rem(seq + k, seq_n), bat) for k in range(1, seq_n)] + [peer for peer, step in zip(peers, steps) if step[0] == "batch"]
        meet(greet)

        def swap(j, src, dst):
            return pltpu.make_async_remote_copy(
                src_ref=src, dst_ref=dst, send_sem=swap_send.at[j], recv_sem=swap_recv.at[j], device_id=other, device_id_type=MESH
            )

        at = exchange.at if own else (lambda place: None)
        plan = lambda name, steps: spaced(exchange, name, steps) if own else no_pump
        run_feed = lambda p: feed(core, p, n2, cot, fg, fu, fd, hid, ups, gn, plan(f"f{p}", 2))
        if own:
            cot_far, normed_far = far_in
            n2_swap, joined_swap = swap(4, n2, n2_far), swap(5, joined, joined_far)
            ups_swaps = [swap(6 + p, ups.at[:, 0, p], ups_far.at[:, p]) for p in range(parts)]
            hid_swap = swap(9, hid, hid_far)
            run_up = lambda p: wgrad_up(core, chunks[2 * p], chunks[2 * p + 1], n2, n2_far, ups.at[:, 1, p], ups_far.at[:, p], plan(f"u{p}", 2))
            n2_swap.start()
            run_feed(0)
            ups_swaps[0].start()
            joined_swap.start()
            n2_swap.wait()
            ups_swaps[0].wait()
            run_up(0)
            run_feed(1)
            ups_swaps[1].start()
            run_feed(2)
            ups_swaps[2].start()
            hid_swap.start()
            ups_swaps[1].wait()
            run_up(1)
            ups_swaps[2].wait()
            run_up(2)
            joined_swap.wait()
            hid_swap.wait()
            wgrad_down(core, chunks[6:9], hid, hid_far, cot, cot_far, plan("d", 2 * parts))
        else:
            for p in range(parts):
                run_feed(p)
        norm_back(core, gn, resid, cot, fgain, gres, low, gain_sum)
        at("a4")
        keep = pltpu.make_async_copy(low, low_out, one)
        keep.start()
        low_swap = swap(0, low, low_far)
        low_swap.start()
        turn(
            core, seqs, length, low, ow, gate, state, rate, vec, ggate, lc, q, carry, gm,
            plan("t", 2),
        )
        gate_swap = swap(1, ggate.at[0], ggate_far)
        gate_swap.start()
        arriving = Entry(carry, got, seq_n, send, recv)
        arriving.start()
        keep.wait()
        low_swap.wait()
        if own:
            at("b0")
            exchange.free(0)
            exchange.free(2)
            wgrad(core, chunks[9:10], joined, joined_far, low_out, low_far, False)
            at("b1")
        arriving.finish(cin, True)
        gate_swap.wait()
        at("b2")
        gates_back(
            own, core, seqs, length, lc, q, cin, state, entry, rate, inlet, mixed, branch, edge, wr, wi, taps, vec,
            gb, head, tail, blocks, rate_sum, inlet_sum, small.at[0], dr, di, gr, gi, gm, ext,
            plan("g", 2),
        )

        to_left = pltpu.make_async_remote_copy(
            src_ref=head, dst_ref=ahead, send_sem=swap_send.at[2], recv_sem=swap_recv.at[2],
            device_id=(lax.rem(seq + seq_n - 1, seq_n), bat), device_id_type=MESH,
        )
        to_left.start()
        if own:
            at("c0")
            exchange.free(4)
            wgrad(core, chunks[10:11], normed, normed_far, ggate.at[1], ggate_far, True)
            at("c1")
        to_left.wait()
        weight = (seq < seq_n - 1).astype(F32)
        copies = []
        for i in range(2):
            mine = (1 - i) * (1 - core) + i * core
            for s in range(seqs):
                y = ahead[mine, 8 * s : 8 * s + 8, :] * weight
                t = tail[mine, 16 * s : 16 * s + 16, :]
                grown = jnp.concatenate([jnp.zeros((16, width), F32), y], axis=0)
                for k in range(1, 4):
                    t = t + taps[k : k + 1, pl.ds(pl.multiple_of(mine * width, 128), width)] * grown[k : k + 16]
                fixed[i, 16 * s : 16 * s + 16, :] = t.astype(BF16)
                copy = pltpu.make_async_copy(
                    fixed.at[i, 16 * s : 16 * s + 16], gb.at[i, (s + 1) * length - 16 : (s + 1) * length], local.at[i, s]
                )
                copy.start()
                copies.append(copy)
        for copy in copies:
            copy.wait()
        branch_swap = swap(3, gb.at[0], gb_far)
        branch_swap.start()
        at("c2")
        branch_swap.wait()
        at("c3")
        if own:
            exchange.free(1)
            exchange.free(3)
            wgrad(core, chunks[11:12], normed, normed_far, gb.at[1], gb_far, True)
            at("c4")

        begin = plan("i", 4)
        tile = 128
        acc[...] = jnp.zeros_like(acc)

        def input_grad(gg_ref, gb_ref, gwt, gwm, bwt, bwm, x_ref, gr_ref, out):
            pump = begin()
            d = nt(gg_ref[0], gwt[...]) + nt(gg_ref[1], gwm[...]) + nt(gb_ref[0], bwt[...]) + nt(gb_ref[1], bwm[...])
            x = x_ref[...].astype(F32)
            r = lax.rsqrt(jnp.mean(x * x, axis=-1, keepdims=True) + 1e-06)
            xr, dg = x * r, d * mgain[...]
            out[...] = gr_ref[...] + r * (dg - xr * jnp.mean(dg * xr, axis=-1, keepdims=True))
            acc[...] += jnp.sum(d * xr, axis=0, keepdims=True)
            pump()

        row = pl.BlockSpec((tile, model), lambda i: (i, 0))
        pair = pl.BlockSpec((2, tile, width), lambda i: (0, i, 0))
        side = lambda c: pl.BlockSpec((model, width), lambda i: (0, c), pipeline_mode=pl.Buffered(1))
        pltpu.emit_pipeline(
            input_grad, grid=(rows // tile,), in_specs=[pair, pair, side(1 - core), side(core), side(1 - core), side(core), row, row], out_specs=[row]
        )(ggate, gb, gw, gw, bw, bw, tok, gres, tokens_grad)

        small[0, 8:9, 0:model] = acc[...]
        small[0, 9:10, 0:model] = gain_sum[...]

        def small_step(k):
            return pltpu.make_async_remote_copy(
                src_ref=small.at[0], dst_ref=small.at[k + 1], send_sem=s_send.at[k], recv_sem=s_recv.at[k],
                device_id=peers[k], device_id_type=MESH,
            )

        def small_event(k):
            small_step(k).wait()
            small[0] = small[0] + small[k + 1]
            if k + 1 < n_steps:
                small_step(k + 1).start()

        small_events = [functools.partial(small_event, k) for k in range(n_steps)]
        small_step(0).start()
        if own:
            exchange.further[7] = small_events
        begin_out = plan("o", 4)
        tile_out = 256

        def last(r, *rest):
            pump = begin_out()
            hid_refs, down_refs, out = rest[: 2 * parts], rest[2 * parts : 4 * parts], rest[-1]
            total = r[...]
            for l, w in zip(hid_refs, down_refs):
                total = total + nn(l[0, 0], w[...])
            out[...] = total.astype(BF16)
            pump()

        col = pl.BlockSpec((rows, tile_out), lambda i: (0, i))
        order = [(side, p) for side in range(2) for p in range(parts)]
        hid_spec = lambda side, p: pl.BlockSpec((1, 1, rows, unit), lambda i: (side, p, 0, 0), pipeline_mode=pl.Buffered(1))
        down_spec = lambda half, p: pl.BlockSpec((unit, tile_out), lambda i: (half * parts + p, i))
        pltpu.emit_pipeline(
            last, grid=(model // tile_out,),
            in_specs=[col] + [hid_spec(*o) for o in order] + [down_spec(core if side else 1 - core, p) for side, p in order], out_specs=[col],
        )(resid, *([hid] * 2 * parts), *([fd] * 2 * parts), block_out)
        if own:
            exchange.drain()
        else:
            for event in small_events:
                event()
        totals[...] = small[0]

    f = lambda *shape: jax.ShapeDtypeStruct(shape, F32)
    b = lambda *shape: jax.ShapeDtypeStruct(shape, BF16)
    vm, dma = pltpu.VMEM, lambda *shape: pltpu.SemaphoreType.DMA(shape)
    out_shape = [
        f(rows, model), b(rows, model), f(16, lru),
        f(rows, model), b(rows, model), b(rows, model), b(2, rows, width), b(rows, width), f(rows, lru), f(rows, lru), b(2, rows, width), b(rows, width),
        b(2, parts, rows, unit), b(2, parts, rows, unit), b(2, 2, parts, rows, unit), b(2, parts, rows, unit), b(rows, model), b(rows, lru),
    ]
    out_specs = [ANY, ANY, INSIDE] + [ANY] * 15
    scratch = [
        vm((rows, model), BF16), vm((2, 2, seqs, width), F32), vm((seq_n, 2, 2, seqs, width), F32), vm((2, seqs, width), F32),
        vm((sub, sub), BF16), vm((sub, sub), BF16), vm((rows, width), BF16), vm((rows, width), BF16),
        vm((seqs, length + 8, width), F32), vm((seqs, length + 8, width), F32), vm((2, 8 * seqs, width), F32), vm((2, 16 * seqs, width), F32),
        vm((2, 8 * seqs, width), F32), vm((2, 16 * seqs, width), BF16), vm((1, model), F32), vm((1, model), F32), vm((n_steps + 1, 16, lru), F32), vm((rows, model), F32),
        dma(seq_n), dma(seq_n), dma(SWAPS), dma(SWAPS), pltpu.SemaphoreType.DMA, dma(2, seqs), dma(n_steps), dma(n_steps),
    ]
    if own:
        out_shape += [b(2, 2, sum(PARTS), 128), b(4 * per, bw_, 128)]
        out_specs += [INSIDE, INSIDE]
        scratch += [vm((16, 768, 128), BF16)] * 3 + Exchange.scratch(len(PARTS), sum(PARTS))
        scratch += [vm((4 * per, bw_, 128), BF16)] + BlockSums.scratch(bw_)
    else:
        out_shape += [f(*wr.shape), f(*wi.shape)]
        out_specs += [INSIDE, INSIDE]
    ins = [ANY] * (len(grads_in) + len(values))
    for j in (3, 16, 20):
        ins[len(grads_in) + j] = INSIDE
    return pl.pallas_call(
        kernel,
        in_specs=ins,
        out_specs=out_specs,
        out_shape=out_shape,
        scratch_shapes=scratch,
        compiler_params=pltpu.CompilerParams(collective_id=collective_id, has_side_effects=True, vmem_limit_bytes=60 * 2**20),
        name="backward",
    )(*grads_in, *values)


def lay(sums, totals, blocks, model, lru, units, n):
    shapes = [(model // n, units), (model // n, units), (units // n, model), (lru // n, model), (model // n, lru), (model // n, lru)]
    rows = sums.shape[2]
    count, wide_b = blocks.shape[0] // 2, blocks.shape[1]

    def kernel(v, b, rate, inlet, *outs):
        for y in range(2):
            for m, out in enumerate(outs):
                part, wide = out.shape
                for t in range(wide // 256):
                    if m < 2:
                        at, col = t // 2 * 512 + m * 256 + t % 2 * 128, t // 2 * 512 + y * 256 + t % 2 * 128
                    else:
                        at, col = 1536 + [0, 768, 1152, 1536][m - 2] + t * part, y * wide // 2 + t * 128
                    out[:, col : col + 128] = v[0, y, at : at + part, :].astype(F32)
        for j in range(count // 2):
            rate[j] = b[0, j, :, 0:wide_b].astype(F32)
            inlet[j] = b[1, j, :, 0:wide_b].astype(F32)

    block = pl.BlockSpec((count // 2, wide_b, wide_b), lambda i: (i, 0, 0))
    rate, inlet, *grads = pl.pallas_call(
        kernel,
        grid=(2,),
        in_specs=[pl.BlockSpec((1, 2, rows, 128), lambda i: (i, 0, 0, 0)), pl.BlockSpec((2, count // 2, wide_b, 128), lambda i: (0, i, 0, 0))],
        out_specs=[block, block] + [pl.BlockSpec((part, wide // 2), lambda i: (0, i)) for part, wide in shapes],
        out_shape=[jax.ShapeDtypeStruct((count, wide_b, wide_b), F32)] * 2 + [jax.ShapeDtypeStruct(shape, F32) for shape in shapes],
        compiler_params=params(),
        name="lay",
    )(sums, blocks.reshape(2, count, wide_b, 128))
    return rate, inlet, grads


def swap(value):
    count = lax.axis_size("batch")
    return lax.ppermute(value, "batch", [(i, i ^ 1) for i in range(count)])


def local(
    tokens, cotangent, gate_weight, branch_weight, out_weight, conv_taps, conv_offset, rate_weight, inlet_weight,
    rate_offset, inlet_offset, decay_param, mixer_gain, feed_gain, feed_gate, feed_up, feed_down,
):
    seqs, length, model = tokens.shape
    lru, units = gate_weight.shape[1], feed_gate.shape[1]
    rows = seqs * length
    seq_n, batch_n = lax.axis_size("seq"), lax.axis_size("batch")
    core = lax.rem(lax.axis_index("batch"), 2)

    tok, cot = tokens.reshape(rows, model), cotangent.reshape(rows, model)
    cot_far = swap(cot)
    none = jnp.zeros_like(conv_offset)
    vec = jnp.stack(
        [conv_offset, rate_offset, inlet_offset, jax.nn.softplus(decay_param), jax.nn.sigmoid(decay_param), none, none, none]
    )
    gain1, gain2 = mixer_gain[None], feed_gain[None]

    normed, gate, branch, edge, mixed, rate, inlet, h, p, entry = front(
        tok, gain1, gate_weight, branch_weight, conv_taps, vec, rate_weight, inlet_weight, seqs, length, seq_n, 0
    )
    normed_far = swap(normed)
    joined, resid, normed_two, state = join(tok, gate, h, p, entry, out_weight, gain2, seqs, length)

    own = (seq_n, batch_n) == (8, 4)
    tokens_grad, out, totals, _, grad_low, _, ggate, _, _, _, gb, _, hid, _, ups, _, _, _, *sums = backward(
        own, seqs, length, seq_n, batch_n, [cot_far, normed_far],
        [
            normed_two, resid, cot, gain2, out_weight, gate, state, entry, rate, vec, inlet, mixed, branch, edge,
            rate_weight, inlet_weight, conv_taps, gate_weight, branch_weight, tok, gain1, feed_gate, feed_up, feed_down, joined, normed,
        ],
        1,
    )
    if own:
        rate_all, inlet_all, grads = lay(sums[0], totals, sums[1], model, lru, units, seq_n)
        gate_feed_all, up_feed_all, down_all, out_all, gate_all, branch_all = grads
    else:
        rate_all, inlet_all = lax.psum((sums[0], sums[1]), ("seq", "batch"))

        def full(pair):
            pair = pair if pair.ndim == 4 else pair[:, None]
            pair = jnp.where(core == 0, pair[::-1], pair)
            return pair.transpose(2, 0, 1, 3).reshape(rows, -1)

        def total(left, right):
            return lax.psum(lax.psum_scatter(tn(left, right), "seq", scatter_dimension=0, tiled=True), "batch")

        down_all = total(full(hid), cot)
        gate_feed_all, up_feed_all = total(normed_two, full(ups[0])), total(normed_two, full(ups[1]))
        out_all = total(joined, grad_low)
        gate_all, branch_all = total(normed, full(ggate)), total(normed, full(gb))

    return (
        out.reshape(seqs, length, model), tokens_grad.reshape(seqs, length, model), gate_all, branch_all, out_all,
        totals[0:4], totals[7], rate_all, inlet_all, totals[5], totals[6], totals[4], totals[8, :model], totals[9, :model],
        gate_feed_all, up_feed_all, down_all,
    )


def solution(mesh):
    big = P("batch", "seq", None)
    in_specs = (big, big) + (P(),) * 15
    out_specs = (big, big) + (P("seq", None),) * 3 + (P(),) * 9 + (P("seq", None),) * 3
    return jax.shard_map(local, mesh=mesh, in_specs=in_specs, out_specs=out_specs, check_vma=False)
```

time: 323 us -> 286 us (0.89)
  Pallas kernels: 287 us -> 270 us
  waiting for transfers between devices: 6.61 us -> 0.01 us
  local copies, waits for them, and re-layouts: 16 us -> 10.9 us
  starting transfers between devices: 6.23 us -> 1.38 us
    pallas_call x5 -> x2, Pallas kernels: 77.5 us -> 43.6 us  [the longest x1 38.2 us: front(): pl.pallas_call(functools.partial(front_kernel, seqs, length, seq_n), grid...]
    pallas_call x1, Pallas kernels: 198 us -> 215 us  [backward(): pl.pallas_call(kernel, in_specs=ins, out_specs=out_specs, out_shape=out_s...]
    ppermute x8 -> x2, waiting for transfers between devices: 6.61 us -> 0.01 us  [swap(): return lax.ppermute(value, 'batch', [(i, i ^ 1) for i in range(count)])]
    broadcast_in_dim x5 -> x0, local copies, waits for them, and re-layouts: 5.08 us -> none  [the longest x1 1.3 us: local(): conv_offset[None]]
  transfers between devices with their start and end apart: 9 -> 2, of which waited for: 3 -> 0; matrix products, arithmetic and copies ran while one was open for 2% -> 1% of each run, Pallas kernels for 26% -> 18%
where the time goes in v3:
time: 286 us; the launch traced here: 284 us
  Pallas kernels  270 us (94%)
  local copies, waits for them, and re-layouts  10.9 us (4%)
    pallas_call x1, Pallas kernels, backward(): pl.pallas_call(kernel, in_specs=ins, out_specs=out_specs, out_shape=out_s...  215 us
    pallas_call x1, Pallas kernels, front(): pl.pallas_call(functools.partial(front_kernel, seqs, length, seq_n), grid...  38.2 us
    pallas_call x1, Pallas kernels, join(): pl.pallas_call(join_kernel, grid=(rows // tile,), in_specs=[row(model), r...  11.5 us
  transfers between devices with their start and end apart: 2, of which 0 were waited for; matrix products, arithmetic and copies ran while one was open for 1% of the time, Pallas kernels for 18%

profile of v3, /device:TPU:13, one launch (start us, length us, event | category | flops | bytes accessed | tf_op | source)
XLA Modules:
  0.0 283.9 jit_solution(8541536601426749818)
XLA Ops:
  0.7 0.7 collective-permute-start
  1.4 0.7 stack.21
  2.1 0.7 stack.22
  2.8 0.7 stack.23
  3.5 0.7 add_divide_fusion
  4.3 0.7 stack.27.vec.refs_11_
  5.0 38.2 %front.1 = (bf16[512,1024]{1,0:T(8,128)(2,1)}, f32[512,1536]{1,0:T(8,128)}, bf16[512,1536]{1,0:T(8,128)(2,1)}, bf16[32,1536]{1,0:T(8,128)(2,1)}, bf16[512,1536]{...) custom-call(bf16[512,1024]{1,0:T(8,128)(2,1)} %bitcast.9, ...), custom_call_target="tpu_custom_call" | custom-call | tf_op jit(solution)/shard_map/front/pallas_call | solution.py:240
  43.2 0.6 collective-permute-start.1
  43.8 11.5 %join.1 = (bf16[512,1536]{1,0:T(8,128)(2,1)}, f32[512,1024]{1,0:T(8,128)}, bf16[512,1024]{1,0:T(8,128)(2,1)}, f32[512,1536]{1,0:T(8,128)}) custom-call(bf16[512,1024]{1,0:T(8,128)(2,1)} %bitcast.10, f32[512,1536]{1,0:T(8,128)} %get-tuple-element.45.gate.refs_7_, f32[512,1536]{1,0:T(8,128)} %get-tuple-element.46.h, f32[512,1536]{1,0:T(8,128)} %get-tuple-element.47.p, ...), custom_call_target="tpu_custom_call" | custom-call | tf_op jit(solution)/shard_map/join/pallas_call | solution.py:298
  55.4 0.0 collective-permute-done.refs_0_
  55.4 0.0 copy-start.1
  55.4 0.0 collective-permute-done.1.refs_1_
  55.4 0.0 copy-start.2
  55.4 0.9 copy-done.1
  56.4 0.3 copy-done.2
  56.7 215.0 %backward.1 = (f32[512,1024]{1,0:T(8,128)}, bf16[512,1024]{1,0:T(8,128)(2,1)}, f32[16,1536]{1,0:T(8,128)}, f32[512,1024]{1,0:T(8,128)}, bf16[512,1024]{1,0:T(8,1...) custom-call(bf16[512,1024]{1,0:T(8,128)(2,1)} %copy-done.1, ...), custom_call_target="tpu_custom_call" | custom-call | tf_op jit(solution)/shard_map/backward/pallas_call | solution.py:1134
  271.8 0.0 copy-start.3
  271.8 1.5 fusion
  273.2 1.4 slice.21
  274.6 1.6 slice_reduce_fusion
  276.3 5.3 %lay.1 = (f32[16,96,96]{2,1,0:T(8,128)}, f32[16,96,96]{2,1,0:T(8,128)}, f32[128,3072]{1,0:T(8,128)}, f32[128,3072]{1,0:T(8,128)}, f32[384,1024]{1,0:T(8,128)}, /...) custom-call(bf16[2,2,3456,128]{3,2,1,0:T(8,128)(2,1)} %get-tuple-element.60.v, ...), custom_call_target="tpu_custom_call" | custom-call | tf_op jit(solution)/shard_map/lay/pallas_call | solution.py:1165
  281.6 0.0 copy-done.3
  281.6 1.0 copy.36
  282.6 1.3 copy.37
  (6 shorter events, 0.0 us)
Async XLA Ops:
  0.7 54.7 %collective-permute-start = (bf16[512,1024]{1,0:T(8,128)(2,1)}, bf16[512,1024]{1,0:T(8,128)(2,1)S(1)}, u32[]{:S(2)}, u32[]{:S(2)}) collective-permute-start(bf16[512,1024]{1,0:T(8,128)(2,1)} %bitcast.13), channel_id=1, source_target_pairs={{0,1},{1,0},{2,3},{3,2},{4,5},{5,4},{6,7},{7,6},{8,9},{9,8},{10,11... | collective-permute-start | bytes 3145736 | tf_op jit(solution)/shard_map/ppermute | solution.py:1179
  43.2 12.2 %collective-permute-start.1 = (bf16[512,1024]{1,0:T(8,128)(2,1)}, bf16[512,1024]{1,0:T(8,128)(2,1)S(1)}, u32[]{:S(2)}, u32[]{:S(2)}) collective-permute-start(bf16[512,1024]{1,0:T(8,128)(2,1)} %get-tuple-element.44.refs_27_), channel_id=1, source_target_pairs={{0,1},{1,0},{2,3},{3,2},{4,5},{5,4},{6,7},{7,6},{8,9},{9,8},{10,11... | collective-permute-start | bytes 3145736 | tf_op jit(solution)/shard_map/ppermute | solution.py:1179
  55.4 1.0 copy-start.1
  55.4 1.3 copy-start.2
  271.8 9.8 %copy-start.3 = (bf16[512,1024]{1,0:T(8,128)(2,1)S(1)}, bf16[512,1024]{1,0:T(8,128)(2,1)}, u32[]{:S(2)}) copy-start(bf16[512,1024]{1,0:T(8,128)(2,1)} %get-tuple-element.58) | copy-start | bytes 3145732
  276.3 6.3 %copy-start = (f32[512,1024]{1,0:T(8,128)S(1)}, f32[512,1024]{1,0:T(8,128)}, u32[]{:S(2)}) copy-start(f32[512,1024]{1,0:T(8,128)} %get-tuple-element.59) | copy-start | bytes 6291460

commit v4 on v3

--- a/solution.py
+++ b/solution.py
@@ -1147,7 +1147,12 @@
     rows = sums.shape[2]
     count, wide_b = blocks.shape[0] // 2, blocks.shape[1]
 
-    def kernel(v, b, rate, inlet, *outs):
+    def kernel(v, b, s, rate, inlet, taps, decay, rate_off, inlet_off, conv_off, gain1, gain2, *outs):
+        taps[...] = s[0:4, :]
+        for j, vector in enumerate((decay, rate_off, inlet_off, conv_off)):
+            vector[...] = s[4 + j, :]
+        gain1[...] = s[8, 0:model]
+        gain2[...] = s[9, 0:model]
         for y in range(2):
             for m, out in enumerate(outs):
                 part, wide = out.shape
@@ -1162,16 +1167,17 @@
             inlet[j] = b[1, j, :, 0:wide_b].astype(F32)
 
     block = pl.BlockSpec((count // 2, wide_b, wide_b), lambda i: (i, 0, 0))
-    rate, inlet, *grads = pl.pallas_call(
+    flat = lambda size: (pl.BlockSpec((size,), lambda i: (0,)), jax.ShapeDtypeStruct((size,), F32))
+    vectors = [(whole((4, lru)), jax.ShapeDtypeStruct((4, lru), F32))] + [flat(lru)] * 4 + [flat(model)] * 2
+    return pl.pallas_call(
         kernel,
         grid=(2,),
-        in_specs=[pl.BlockSpec((1, 2, rows, 128), lambda i: (i, 0, 0, 0)), pl.BlockSpec((2, count // 2, wide_b, 128), lambda i: (0, i, 0, 0))],
-        out_specs=[block, block] + [pl.BlockSpec((part, wide // 2), lambda i: (0, i)) for part, wide in shapes],
-        out_shape=[jax.ShapeDtypeStruct((count, wide_b, wide_b), F32)] * 2 + [jax.ShapeDtypeStruct(shape, F32) for shape in shapes],
+        in_specs=[pl.BlockSpec((1, 2, rows, 128), lambda i: (i, 0, 0, 0)), pl.BlockSpec((2, count // 2, wide_b, 128), lambda i: (0, i, 0, 0)), whole(totals.shape)],
+        out_specs=[block, block] + [v[0] for v in vectors] + [pl.BlockSpec((part, wide // 2), lambda i: (0, i)) for part, wide in shapes],
+        out_shape=[jax.ShapeDtypeStruct((count, wide_b, wide_b), F32)] * 2 + [v[1] for v in vectors] + [jax.ShapeDtypeStruct(shape, F32) for shape in shapes],
         compiler_params=params(),
         name="lay",
-    )(sums, blocks.reshape(2, count, wide_b, 128))
-    return rate, inlet, grads
+    )(sums, blocks.reshape(2, count, wide_b, 128), totals)
 
 
 def swap(value):
@@ -1213,9 +1219,10 @@
         1,
     )
     if own:
-        rate_all, inlet_all, grads = lay(sums[0], totals, sums[1], model, lru, units, seq_n)
-        gate_feed_all, up_feed_all, down_all, out_all, gate_all, branch_all = grads
+        rate_all, inlet_all, *vectors = lay(sums[0], totals, sums[1], model, lru, units, seq_n)
+        vectors, (gate_feed_all, up_feed_all, down_all, out_all, gate_all, branch_all) = vectors[:7], vectors[7:]
     else:
+        vectors = [totals[0:4], *totals[4:8], totals[8, :model], totals[9, :model]]
         rate_all, inlet_all = lax.psum((sums[0], sums[1]), ("seq", "batch"))
 
         def full(pair):
@@ -1233,7 +1240,7 @@
 
     return (
         out.reshape(seqs, length, model), tokens_grad.reshape(seqs, length, model), gate_all, branch_all, out_all,
-        totals[0:4], totals[7], rate_all, inlet_all, totals[5], totals[6], totals[4], totals[8, :model], totals[9, :model],
+        vectors[0], vectors[4], rate_all, inlet_all, vectors[2], vectors[3], vectors[1], vectors[5], vectors[6],
         gate_feed_all, up_feed_all, down_all,
     )
 

time: 286 us -> 282 us (0.986)
  local copies, waits for them, and re-layouts: 10.9 us -> 6.4 us
    slice x3 -> x0, local copies, waits for them, and re-layouts: 4.5 us -> none  [the longest x1 1.62 us: local(): totals[4]]
where the time goes in v4:
time: 282 us; the launch traced here: 280 us
  Pallas kernels  270 us (96%)
  local copies, waits for them, and re-layouts  6.4 us (2%)
    pallas_call x1, Pallas kernels, backward(): pl.pallas_call(kernel, in_specs=ins, out_specs=out_specs, out_shape=out_s...  215 us
    pallas_call x1, Pallas kernels, front(): pl.pallas_call(functools.partial(front_kernel, seqs, length, seq_n), grid...  38.3 us
    pallas_call x1, Pallas kernels, join(): pl.pallas_call(join_kernel, grid=(rows // tile,), in_specs=[row(model), r...  11.6 us
  transfers between devices with their start and end apart: 2, of which 0 were waited for; matrix products, arithmetic and copies ran while one was open for 1% of the time, Pallas kernels for 18%

profile of v4, /device:TPU:13, one launch (start us, length us, event | category | flops | bytes accessed | tf_op | source)
XLA Modules:
  0.0 279.7 jit_solution(4633028062228385835)
XLA Ops:
  0.7 0.7 collective-permute-start
  1.4 0.7 stack.21
  2.1 0.7 stack.22
  2.8 0.7 stack.23
  3.5 0.7 add_divide_fusion
  4.3 0.7 stack.27.vec.refs_11_
  5.0 38.3 %front.1 = (bf16[512,1024]{1,0:T(8,128)(2,1)}, f32[512,1536]{1,0:T(8,128)}, bf16[512,1536]{1,0:T(8,128)(2,1)}, bf16[32,1536]{1,0:T(8,128)(2,1)}, bf16[512,1536]{...) custom-call(bf16[512,1024]{1,0:T(8,128)(2,1)} %bitcast.7, ...), custom_call_target="tpu_custom_call" | custom-call | tf_op jit(solution)/shard_map/front/pallas_call | solution.py:240
  43.3 0.6 collective-permute-start.1
  43.9 11.6 %join.1 = (bf16[512,1536]{1,0:T(8,128)(2,1)}, f32[512,1024]{1,0:T(8,128)}, bf16[512,1024]{1,0:T(8,128)(2,1)}, f32[512,1536]{1,0:T(8,128)}) custom-call(bf16[512,1024]{1,0:T(8,128)(2,1)} %bitcast.8, f32[512,1536]{1,0:T(8,128)} %get-tuple-element.52.gate.refs_7_, f32[512,1536]{1,0:T(8,128)} %get-tuple-element.53.h, f32[512,1536]{1,0:T(8,128)} %get-tuple-element.54.p, ...), custom_call_target="tpu_custom_call" | custom-call | tf_op jit(solution)/shard_map/join/pallas_call | solution.py:298
  55.5 0.0 collective-permute-done.refs_0_
  55.5 0.0 copy-start.1
  55.5 0.0 collective-permute-done.1.refs_1_
  55.5 0.0 copy-start.2
  55.5 0.9 copy-done.1
  56.4 0.3 copy-done.2
  56.8 215.2 %backward.1 = (f32[512,1024]{1,0:T(8,128)}, bf16[512,1024]{1,0:T(8,128)(2,1)}, f32[16,1536]{1,0:T(8,128)}, f32[512,1024]{1,0:T(8,128)}, bf16[512,1024]{1,0:T(8,1...) custom-call(bf16[512,1024]{1,0:T(8,128)(2,1)} %copy-done.1, ...), custom_call_target="tpu_custom_call" | custom-call | tf_op jit(solution)/shard_map/backward/pallas_call | solution.py:1134
  271.9 0.0 copy-start.3
  272.0 0.0 copy-start
  272.0 5.4 %lay.1 = (f32[16,96,96]{2,1,0:T(8,128)}, f32[16,96,96]{2,1,0:T(8,128)}, f32[4,1536]{1,0:T(4,128)}, f32[1536]{0:T(1024)}, f32[1536]{0:T(1024)}, /*index=5*/f32[15...) custom-call(bf16[2,2,3456,128]{3,2,1,0:T(8,128)(2,1)} %get-tuple-ele, ...), custom_call_target="tpu_custom_call" | custom-call | tf_op jit(solution)/shard_map/lay/pallas_call | solution.py:1172
  277.4 0.0 copy-done.3
  277.4 1.0 copy.36
  278.4 0.0 copy-done
  278.4 1.3 copy.37
  (4 shorter events, 0.0 us)
Async XLA Ops:
  0.7 54.8 %collective-permute-start = (bf16[512,1024]{1,0:T(8,128)(2,1)}, bf16[512,1024]{1,0:T(8,128)(2,1)S(1)}, u32[]{:S(2)}, u32[]{:S(2)}) collective-permute-start(bf16[512,1024]{1,0:T(8,128)(2,1)} %bitcast.11), channel_id=1, source_target_pairs={{0,1},{1,0},{2,3},{3,2},{4,5},{5,4},{6,7},{7,6},{8,9},{9,8},{10,11... | collective-permute-start | bytes 3145736 | tf_op jit(solution)/shard_map/ppermute | solution.py:1185
  43.3 12.2 %collective-permute-start.1 = (bf16[512,1024]{1,0:T(8,128)(2,1)}, bf16[512,1024]{1,0:T(8,128)(2,1)S(1)}, u32[]{:S(2)}, u32[]{:S(2)}) collective-permute-start(bf16[512,1024]{1,0:T(8,128)(2,1)} %get-tuple-element.51.refs_27_), channel_id=1, source_target_pairs={{0,1},{1,0},{2,3},{3,2},{4,5},{5,4},{6,7},{7,6},{8,9},{9,8},{10,11... | collective-permute-start | bytes 3145736 | tf_op jit(solution)/shard_map/ppermute | solution.py:1185
  55.5 1.0 copy-start.1
  55.5 1.3 copy-start.2
  271.9 5.5 %copy-start.3 = (bf16[512,1024]{1,0:T(8,128)(2,1)S(1)}, bf16[512,1024]{1,0:T(8,128)(2,1)}, u32[]{:S(2)}) copy-start(bf16[512,1024]{1,0:T(8,128)(2,1)} %get-tuple-element.65) | copy-start | bytes 3145732
  272.0 6.4 %copy-start = (f32[512,1024]{1,0:T(8,128)S(1)}, f32[512,1024]{1,0:T(8,128)}, u32[]{:S(2)}) copy-start(f32[512,1024]{1,0:T(8,128)} %get-tuple-element.66) | copy-start | bytes 6291460

commit v5 on v4

--- a/solution.py
+++ b/solution.py
@@ -71,11 +71,14 @@
 MESH = pl.DeviceIdType.MESH
 
 
-def meet(peers):
+def greet(peers):
     barrier = pltpu.get_barrier_semaphore()
     for peer in peers:
         pl.semaphore_signal(barrier, inc=1, device_id=peer, device_id_type=MESH)
-    pl.semaphore_wait(barrier, len(peers))
+
+
+def met(count):
+    pl.semaphore_wait(pltpu.get_barrier_semaphore(), count)
 
 
 def flip(index, bit):
@@ -121,18 +124,17 @@
 
     seq, bat = lax.axis_index("seq"), lax.axis_index("batch")
 
+    copies = [
+        pltpu.make_async_remote_copy(
+            src_ref=tok.at[(s + 1) * length - 16 : (s + 1) * length], dst_ref=halo.at[s], send_sem=h_send.at[s], recv_sem=h_recv.at[s],
+            device_id=(lax.rem(seq + 1, seq_n), bat), device_id_type=MESH,
+        )
+        for s in range(seqs)
+    ]
+
     @pl.when(pl.program_id(0) == 0)
     def _():
-        meet([(lax.rem(seq + k, seq_n), bat) for k in range(1, seq_n)])
-        copies = [
-            pltpu.make_async_remote_copy(
-                src_ref=tok.at[(s + 1) * length - 16 : (s + 1) * length], dst_ref=halo.at[s], send_sem=h_send.at[s], recv_sem=h_recv.at[s],
-                device_id=(lax.rem(seq + 1, seq_n), bat), device_id_type=MESH,
-            )
-            for s in range(seqs)
-        ]
-        for copy in copies:
-            copy.start()
+        greet([(lax.rem(seq + k, seq_n), bat) for k in range(1, seq_n)])
 
         def norm(i, _):
             x = tok[pl.ds(i * 32, 32), :].astype(F32)
@@ -141,14 +143,21 @@
             return 0
 
         lax.fori_loop(0, rows // 32, norm, 0)
+        met(seq_n - 1)
+        for copy in copies:
+            copy.start()
+
+    gate[...] = nn(normed[...], gw[...])
+    b16 = nn(normed[...], bw[...]).astype(BF16)
+
+    @pl.when(pl.program_id(0) == 0)
+    def _():
         for s in range(seqs):
             copies[s].wait()
             x = halo[s].astype(F32)
             r = lax.rsqrt(jnp.mean(x * x, axis=-1, keepdims=True) + 1e-06)
             hn[16 * s : 16 * s + 16, :] = (x * r * gain[...]).astype(BF16)
 
-    gate[...] = nn(normed[...], gw[...])
-    b16 = nn(normed[...], bw[...]).astype(BF16)
     e16 = (nn(hn[...], bw[...]) * (seq > 0).astype(F32)).astype(BF16)
     branch[...] = b16
     edge[...] = e16
@@ -927,8 +936,8 @@
             exchange.further[6] = BlockSums(blocks, block_bufs, block_total, b_send, b_recv).events()
             blocks[...] = jnp.zeros_like(blocks)
         small[0] = jnp.zeros((16, lru), F32)
-        greet = [(lax.rem(seq + k, seq_n), bat) for k in range(1, seq_n)] + [peer for peer, step in zip(peers, steps) if step[0] == "batch"]
-        meet(greet)
+        all_peers = [(lax.rem(seq + k, seq_n), bat) for k in range(1, seq_n)] + [peer for peer, step in zip(peers, steps) if step[0] == "batch"]
+        greet(all_peers)
 
         def swap(j, src, dst):
             return pltpu.make_async_remote_copy(
@@ -937,23 +946,32 @@
 
         at = exchange.at if own else (lambda place: None)
         plan = lambda name, steps: spaced(exchange, name, steps) if own else no_pump
-        run_feed = lambda p: feed(core, p, n2, cot, fg, fu, fd, hid, ups, gn, plan(f"f{p}", 2))
+        run_feed = lambda p, begin: feed(core, p, n2, cot, fg, fu, fd, hid, ups, gn, begin)
         if own:
             cot_far, normed_far = far_in
             n2_swap, joined_swap = swap(4, n2, n2_far), swap(5, joined, joined_far)
             ups_swaps = [swap(6 + p, ups.at[:, 0, p], ups_far.at[:, p]) for p in range(parts)]
             hid_swap = swap(9, hid, hid_far)
             run_up = lambda p: wgrad_up(core, chunks[2 * p], chunks[2 * p + 1], n2, n2_far, ups.at[:, 1, p], ups_far.at[:, p], plan(f"u{p}", 2))
-            n2_swap.start()
-            run_feed(0)
+
+            def opening():
+                def pump():
+                    @pl.when(pl.program_id(0) == 0)
+                    def _():
+                        met(len(all_peers))
+                        n2_swap.start()
+
+                return pump
+
+            run_feed(0, opening)
             ups_swaps[0].start()
             joined_swap.start()
             n2_swap.wait()
             ups_swaps[0].wait()
             run_up(0)
-            run_feed(1)
+            run_feed(1, plan("f1", 2))
             ups_swaps[1].start()
-            run_feed(2)
+            run_feed(2, plan("f2", 2))
             ups_swaps[2].start()
             hid_swap.start()
             ups_swaps[1].wait()
@@ -964,8 +982,9 @@
             hid_swap.wait()
             wgrad_down(core, chunks[6:9], hid, hid_far, cot, cot_far, plan("d", 2 * parts))
         else:
+            met(len(all_peers))
             for p in range(parts):
-                run_feed(p)
+                run_feed(p, no_pump)
         norm_back(core, gn, resid, cot, fgain, gres, low, gain_sum)
         at("a4")
         keep = pltpu.make_async_copy(low, low_out, one)

time: 282 us -> 279 us (0.989)
  Pallas kernels: 270 us -> 267 us
  transfers between devices with their start and end apart: 2 -> 2, of which waited for: 0 -> 0; matrix products, arithmetic and copies ran while one was open for 1% -> 1% of each run, Pallas kernels for 18% -> 17%
where the time goes in v5:
time: 279 us; the launch traced here: 278 us
  Pallas kernels  267 us (96%)
  local copies, waits for them, and re-layouts  6.4 us (2%)
  starting transfers between devices  2.83 us (1%)
    pallas_call x1, Pallas kernels, backward(): pl.pallas_call(kernel, in_specs=ins, out_specs=out_specs, out_shape=out_s...  215 us
    pallas_call x1, Pallas kernels, front(): pl.pallas_call(functools.partial(front_kernel, seqs, length, seq_n), grid...  35.6 us
    pallas_call x1, Pallas kernels, join(): pl.pallas_call(join_kernel, grid=(rows // tile,), in_specs=[row(model), r...  11.6 us
  transfers between devices with their start and end apart: 2, of which 0 were waited for; matrix products, arithmetic and copies ran while one was open for 1% of the time, Pallas kernels for 17%

profile of v5, /device:TPU:13, one launch (start us, length us, event | category | flops | bytes accessed | tf_op | source)
XLA Modules:
  0.0 278.0 jit_solution(15309587483676850715)
XLA Ops:
  0.7 0.7 collective-permute-start
  1.4 0.7 stack.21
  2.1 0.7 stack.22
  2.8 0.7 stack.23
  3.5 0.7 add_divide_fusion
  4.3 0.7 stack.27.vec.refs_11_
  5.0 35.6 %front.1 = (bf16[512,1024]{1,0:T(8,128)(2,1)}, f32[512,1536]{1,0:T(8,128)}, bf16[512,1536]{1,0:T(8,128)(2,1)}, bf16[32,1536]{1,0:T(8,128)(2,1)}, bf16[512,1536]{...) custom-call(bf16[512,1024]{1,0:T(8,128)(2,1)} %bitcast.7, ...), custom_call_target="tpu_custom_call" | custom-call | tf_op jit(solution)/shard_map/front/pallas_call | solution.py:249
  40.6 2.1 collective-permute-start.1
  42.7 11.6 %join.1 = (bf16[512,1536]{1,0:T(8,128)(2,1)}, f32[512,1024]{1,0:T(8,128)}, bf16[512,1024]{1,0:T(8,128)(2,1)}, f32[512,1536]{1,0:T(8,128)}) custom-call(bf16[512,1024]{1,0:T(8,128)(2,1)} %bitcast.8, f32[512,1536]{1,0:T(8,128)} %get-tuple-element.52.gate.refs_7_, f32[512,1536]{1,0:T(8,128)} %get-tuple-element.53.h, f32[512,1536]{1,0:T(8,128)} %get-tuple-element.54.p, ...), custom_call_target="tpu_custom_call" | custom-call | tf_op jit(solution)/shard_map/join/pallas_call | solution.py:307
  54.2 0.0 collective-permute-done.refs_0_
  54.2 0.0 copy-start.1
  54.2 0.0 collective-permute-done.1.refs_1_
  54.3 0.0 copy-start.2
  54.3 0.9 copy-done.1
  55.2 0.3 copy-done.2
  55.6 214.7 %backward.1 = (f32[512,1024]{1,0:T(8,128)}, bf16[512,1024]{1,0:T(8,128)(2,1)}, f32[16,1536]{1,0:T(8,128)}, f32[512,1024]{1,0:T(8,128)}, bf16[512,1024]{1,0:T(8,1...) custom-call(bf16[512,1024]{1,0:T(8,128)(2,1)} %copy-done.1, ...), custom_call_target="tpu_custom_call" | custom-call | tf_op jit(solution)/shard_map/backward/pallas_call | solution.py:1153
  270.2 0.0 copy-start.3
  270.2 0.0 copy-start
  270.3 5.4 %lay.1 = (f32[16,96,96]{2,1,0:T(8,128)}, f32[16,96,96]{2,1,0:T(8,128)}, f32[4,1536]{1,0:T(4,128)}, f32[1536]{0:T(1024)}, f32[1536]{0:T(1024)}, /*index=5*/f32[15...) custom-call(bf16[2,2,3456,128]{3,2,1,0:T(8,128)(2,1)} %get-tuple-ele, ...), custom_call_target="tpu_custom_call" | custom-call | tf_op jit(solution)/shard_map/lay/pallas_call | solution.py:1191
  275.7 0.0 copy-done.3
  275.7 1.0 copy.36
  276.7 0.0 copy-done
  276.7 1.3 copy.37
  (4 shorter events, 0.0 us)
Async XLA Ops:
  0.7 53.6 %collective-permute-start = (bf16[512,1024]{1,0:T(8,128)(2,1)}, bf16[512,1024]{1,0:T(8,128)(2,1)S(1)}, u32[]{:S(2)}, u32[]{:S(2)}) collective-permute-start(bf16[512,1024]{1,0:T(8,128)(2,1)} %bitcast.11), channel_id=1, source_target_pairs={{0,1},{1,0},{2,3},{3,2},{4,5},{5,4},{6,7},{7,6},{8,9},{9,8},{10,11... | collective-permute-start | bytes 3145736 | tf_op jit(solution)/shard_map/ppermute | solution.py:1204
  40.6 13.7 %collective-permute-start.1 = (bf16[512,1024]{1,0:T(8,128)(2,1)}, bf16[512,1024]{1,0:T(8,128)(2,1)S(1)}, u32[]{:S(2)}, u32[]{:S(2)}) collective-permute-start(bf16[512,1024]{1,0:T(8,128)(2,1)} %get-tuple-element.51.refs_27_), channel_id=1, source_target_pairs={{0,1},{1,0},{2,3},{3,2},{4,5},{5,4},{6,7},{7,6},{8,9},{9,8},{10,11... | collective-permute-start | bytes 3145736 | tf_op jit(solution)/shard_map/ppermute | solution.py:1204
  54.2 1.0 copy-start.1
  54.3 1.3 copy-start.2
  270.2 5.5 %copy-start.3 = (bf16[512,1024]{1,0:T(8,128)(2,1)S(1)}, bf16[512,1024]{1,0:T(8,128)(2,1)}, u32[]{:S(2)}) copy-start(bf16[512,1024]{1,0:T(8,128)(2,1)} %get-tuple-element.65) | copy-start | bytes 3145732
  270.2 6.4 %copy-start = (f32[512,1024]{1,0:T(8,128)S(1)}, f32[512,1024]{1,0:T(8,128)}, u32[]{:S(2)}) copy-start(f32[512,1024]{1,0:T(8,128)} %get-tuple-element.66) | copy-start | bytes 6291460

commit v6 on v5

--- a/solution.py
+++ b/solution.py
@@ -171,14 +171,14 @@
     for s in range(seqs):
 
         def conv(i, _):
-            x = ext[s, pl.ds(pl.multiple_of(i * 16, 16), 24), :]
-            total = off + tap[0] * x[8:24]
+            x = ext[s, pl.ds(pl.multiple_of(i * 32, 32), 40), :]
+            total = off + tap[0] * x[8:40]
             for k in range(1, 4):
-                total = total + tap[k] * x[8 - k : 24 - k]
-            mixed[pl.ds(pl.multiple_of(s * length + i * 16, 16), 16), :] = total.astype(BF16)
+                total = total + tap[k] * x[8 - k : 40 - k]
+            mixed[pl.ds(pl.multiple_of(s * length + i * 32, 32), 32), :] = total.astype(BF16)
             return 0
 
-        lax.fori_loop(0, length // 16, conv, 0)
+        lax.fori_loop(0, length // 32, conv, 0)
 
     for g in range(width // sub):
         cols = slice(g * sub, (g + 1) * sub)
@@ -190,7 +190,7 @@
     ro, io, slope = vec[1:2, :], vec[2:3, :], -8.0 * vec[3:4, :]
 
     def gates(i, _):
-        at = pl.ds(pl.multiple_of(i * 16, 16), 16)
+        at = pl.ds(pl.multiple_of(i * 32, 32), 32)
         rt = sigmoid(rp[at, :] + ro)
         it = sigmoid(ip[at, :] + io)
         log_decay = rt * slope
@@ -201,7 +201,7 @@
         h[at, :] = jnp.sqrt(drop(log_decay, decay)) * it * mixed[at, :].astype(F32)
         return 0
 
-    lax.fori_loop(0, rows // 16, gates, 0)
+    lax.fori_loop(0, rows // 32, gates, 0)
 
     row = lax.broadcasted_iota(jnp.int32, (8, width), 0)
 

time: 279 us -> 279 us (level)
  no operation moved by 1% of the time
where the time goes in v6:
time: 279 us; the launch traced here: 277 us
  Pallas kernels  267 us (96%)
  local copies, waits for them, and re-layouts  6.4 us (2%)
  starting transfers between devices  2.85 us (1%)
    pallas_call x1, Pallas kernels, backward(): pl.pallas_call(kernel, in_specs=ins, out_specs=out_specs, out_shape=out_s...  215 us
    pallas_call x1, Pallas kernels, front(): pl.pallas_call(functools.partial(front_kernel, seqs, length, seq_n), grid...  35 us
    pallas_call x1, Pallas kernels, join(): pl.pallas_call(join_kernel, grid=(rows // tile,), in_specs=[row(model), r...  11.5 us
  transfers between devices with their start and end apart: 2, of which 0 were waited for; matrix products, arithmetic and copies ran while one was open for 1% of the time, Pallas kernels for 17%

profile of v6, /device:TPU:13, one launch (start us, length us, event | category | flops | bytes accessed | tf_op | source)
XLA Modules:
  0.0 277.4 jit_solution(5948927195502130519)
XLA Ops:
  0.7 0.7 collective-permute-start
  1.4 0.7 stack.21
  2.1 0.7 stack.22
  2.8 0.7 stack.23
  3.5 0.7 add_divide_fusion
  4.3 0.7 stack.27.vec.refs_11_
  5.0 35.0 %front.1 = (bf16[512,1024]{1,0:T(8,128)(2,1)}, f32[512,1536]{1,0:T(8,128)}, bf16[512,1536]{1,0:T(8,128)(2,1)}, bf16[32,1536]{1,0:T(8,128)(2,1)}, bf16[512,1536]{...) custom-call(bf16[512,1024]{1,0:T(8,128)(2,1)} %bitcast.7, ...), custom_call_target="tpu_custom_call" | custom-call | tf_op jit(solution)/shard_map/front/pallas_call | solution.py:249
  40.0 2.1 collective-permute-start.1
  42.1 11.5 %join.1 = (bf16[512,1536]{1,0:T(8,128)(2,1)}, f32[512,1024]{1,0:T(8,128)}, bf16[512,1024]{1,0:T(8,128)(2,1)}, f32[512,1536]{1,0:T(8,128)}) custom-call(bf16[512,1024]{1,0:T(8,128)(2,1)} %bitcast.8, f32[512,1536]{1,0:T(8,128)} %get-tuple-element.52.gate.refs_7_, f32[512,1536]{1,0:T(8,128)} %get-tuple-element.53.h, f32[512,1536]{1,0:T(8,128)} %get-tuple-element.54.p, ...), custom_call_target="tpu_custom_call" | custom-call | tf_op jit(solution)/shard_map/join/pallas_call | solution.py:307
  53.6 0.0 collective-permute-done.refs_0_
  53.6 0.0 copy-start.1
  53.6 0.0 collective-permute-done.1.refs_1_
  53.6 0.0 copy-start.2
  53.7 0.9 copy-done.1
  54.6 0.3 copy-done.2
  54.9 214.7 %backward.1 = (f32[512,1024]{1,0:T(8,128)}, bf16[512,1024]{1,0:T(8,128)(2,1)}, f32[16,1536]{1,0:T(8,128)}, f32[512,1024]{1,0:T(8,128)}, bf16[512,1024]{1,0:T(8,1...) custom-call(bf16[512,1024]{1,0:T(8,128)(2,1)} %copy-done.1, ...), custom_call_target="tpu_custom_call" | custom-call | tf_op jit(solution)/shard_map/backward/pallas_call | solution.py:1153
  269.6 0.0 copy-start.3
  269.6 0.0 copy-start
  269.6 5.4 %lay.1 = (f32[16,96,96]{2,1,0:T(8,128)}, f32[16,96,96]{2,1,0:T(8,128)}, f32[4,1536]{1,0:T(4,128)}, f32[1536]{0:T(1024)}, f32[1536]{0:T(1024)}, /*index=5*/f32[15...) custom-call(bf16[2,2,3456,128]{3,2,1,0:T(8,128)(2,1)} %get-tuple-ele, ...), custom_call_target="tpu_custom_call" | custom-call | tf_op jit(solution)/shard_map/lay/pallas_call | solution.py:1191
  275.1 0.0 copy-done.3
  275.1 1.0 copy.36
  276.0 0.0 copy-done
  276.1 1.3 copy.37
  (4 shorter events, 0.0 us)
Async XLA Ops:
  0.7 53.0 %collective-permute-start = (bf16[512,1024]{1,0:T(8,128)(2,1)}, bf16[512,1024]{1,0:T(8,128)(2,1)S(1)}, u32[]{:S(2)}, u32[]{:S(2)}) collective-permute-start(bf16[512,1024]{1,0:T(8,128)(2,1)} %bitcast.11), channel_id=1, source_target_pairs={{0,1},{1,0},{2,3},{3,2},{4,5},{5,4},{6,7},{7,6},{8,9},{9,8},{10,11... | collective-permute-start | bytes 3145736 | tf_op jit(solution)/shard_map/ppermute | solution.py:1204
  40.0 13.7 %collective-permute-start.1 = (bf16[512,1024]{1,0:T(8,128)(2,1)}, bf16[512,1024]{1,0:T(8,128)(2,1)S(1)}, u32[]{:S(2)}, u32[]{:S(2)}) collective-permute-start(bf16[512,1024]{1,0:T(8,128)(2,1)} %get-tuple-element.51.refs_27_), channel_id=1, source_target_pairs={{0,1},{1,0},{2,3},{3,2},{4,5},{5,4},{6,7},{7,6},{8,9},{9,8},{10,11... | collective-permute-start | bytes 3145736 | tf_op jit(solution)/shard_map/ppermute | solution.py:1204
  53.6 1.0 copy-start.1
  53.6 1.3 copy-start.2
  269.6 5.5 %copy-start.3 = (bf16[512,1024]{1,0:T(8,128)(2,1)S(1)}, bf16[512,1024]{1,0:T(8,128)(2,1)}, u32[]{:S(2)}) copy-start(bf16[512,1024]{1,0:T(8,128)(2,1)} %get-tuple-element.65) | copy-start | bytes 3145732
  269.6 6.4 %copy-start = (f32[512,1024]{1,0:T(8,128)S(1)}, f32[512,1024]{1,0:T(8,128)}, u32[]{:S(2)}) copy-start(f32[512,1024]{1,0:T(8,128)} %get-tuple-element.66) | copy-start | bytes 6291460
